TPU v7x, 128 devices: a whole 4x4x4 slice. The times are simulated.
128 devices in a mesh: dp: 16 (over x, z), ctx: 8 (over y, core).
Axes of the slice: x: 4, y: 4, z: 4, core: 2. Of those that a mesh axis runs over, the one named last changes fastest.
Arguments:
- query_rows: bfloat16 [16, 1024, 8192], P('dp', 'ctx'), may hold values from -5 to 5
- key_rows: bfloat16 [16, 1024, 1024], P('dp', 'ctx'), may hold values from -5 to 5
- value_rows: bfloat16 [16, 1024, 1024], P('dp', 'ctx'), may hold values from -6 to 6
- layer_input: bfloat16 [16, 1024, 4096], P('dp', 'ctx'), may hold values from -6 to 6
- out_grad: bfloat16 [16, 1024, 8192], P('dp', 'ctx'), may hold values from -6 to 6
- parents: int32 [16, 8], P('dp'), may hold values from 0 to 7, as said below
- labels: int32 [16, 8], P('dp'), may hold values from 0 to 2
Outputs:
- attention_out: bfloat16 [16, 1024, 8192], P('dp', 'ctx')
- query_grad: bfloat16 [16, 1024, 8192], P('dp', 'ctx')
- key_grad: bfloat16 [16, 1024, 1024], P('dp', 'ctx')
- value_grad: bfloat16 [16, 1024, 1024], P('dp', 'ctx')
- value_weight_grad: float32 [4096, 1024], P(('dp', 'ctx'))
Inputs may be any that keep to these rules, and one draw needn't show every extreme that they name: parents[r, b] <= b for every block b; an entry equal to its own block starts a tree; blocks 0 and 7 always start trees.
All inputs are finite; a program needn't handle non-finite values.
Results may differ from a plain program's by a relative error of at most 0.024.
Values may be sent and summed in bfloat16 or wider, within the bound.
No kernel may reach another device: no remote copies, remote signals or barrier semaphores. Data moves between devices by JAX's collectives and lax.ppermute only.
A program may use at most 128 MiB of HBM per device.

v0:
```python
import functools

import jax
import jax.numpy as jnp
from jax import lax
from jax.experimental import pallas as pl
from jax.experimental.pallas import tpu as pltpu
from jax.sharding import PartitionSpec as P

HD = 128
BLK = 128
GRP = 8
NY = 4
NZ = 4
NX = 4
HALF = 4
CH = 1
PER = HALF // CH
QW = GRP * HD
SLOTS = 2 * NY
PAIRS = 4
NG = 2
TF = 1024
TB = 1024
LOW = jnp.bfloat16
F32 = jnp.float32
SCALE = HD**-0.5
EXP_SCALE = SCALE * 1.4426950408889634
MASKED = -1e30


def dot_nt(a, b):
    return lax.dot_general(a, b, (((1,), (1,)), ((), ())), preferred_element_type=F32)


def dot_nn(a, b):
    return lax.dot_general(a, b, (((1,), (0,)), ((), ())), preferred_element_type=F32)


def dot_tn(a, b):
    return lax.dot_general(a, b, (((0,), (0,)), ((), ())), preferred_element_type=F32)


def attention_kernel(
    place, parents, labels,
    q_own, q_par, g_own, g_par, kv,
    o_own, o_par, dq_own, dq_par, dk_out, dv_out,
    chain, k_pair, v_pair, kt_pair, vt_pair, q_st, g_st, gt_st, p_st, w_st, ds_st,
    m_st, mt_st, l_st, in_st, ot_st, dqt_st, dk_acc, dv_acc,
):
    y = place[0]
    c = place[1]
    heads = range(NG)
    dk_acc[...] = jnp.zeros_like(dk_acc)
    dv_acc[...] = jnp.zeros_like(dv_acc)
    key_pos = lax.broadcasted_iota(jnp.int32, (BLK, BLK), 0)
    query_pos = lax.broadcasted_iota(jnp.int32, (BLK, BLK), 1)
    causal = jnp.where(key_pos <= query_pos, 0.0, MASKED).astype(F32)
    causal = jnp.concatenate([causal] * (TF // BLK), axis=1)
    tiles_f = [slice(i * TF, (i + 1) * TF) for i in range(GRP * BLK // TF)]
    tiles_b = [slice(i * TB, (i + 1) * TB) for i in range(GRP * BLK // TB)]

    def fold(a, op):
        while a.shape[0] > 8:
            half = a.shape[0] // 2
            a = op(a[:half], a[half:])
        return a

    def one_block(block, q_ref, g_ref, o_ref, dq_ref):
        def walk(step, carry):
            current, count = carry
            above = parents[0, current]
            more = above != current
            nxt = jnp.where(more, above, current)
            chain[step + 1] = nxt
            return nxt, count + more.astype(jnp.int32)

        chain[0] = block
        _, count = lax.fori_loop(0, SLOTS - 1, walk, (block, jnp.int32(1)))
        pairs = (count + 1) // 2
        sign = jnp.full((BLK, HD), jnp.where(labels[0, block] == 2, -1.0, 1.0), F32).astype(LOW)

        for n in heads:
            for h in range(GRP):
                rows = slice(h * BLK, (h + 1) * BLK)
                cols = slice(n * QW + h * HD, n * QW + (h + 1) * HD)
                q_st[n, rows, :] = q_ref[:, cols]
                g = g_ref[:, cols] * sign
                g_st[n, rows, :] = g
                gt_st[n, :, rows] = g.T

        def forward(t, first):
            second = jnp.where(2 * t + 1 < count, 0.0, MASKED).astype(F32)
            for n in heads:
                for e in range(2):
                    s = chain[2 * t + e]
                    rows = slice(e * BLK, (e + 1) * BLK)
                    k = kv[s, 0, :, n * HD : (n + 1) * HD]
                    v = kv[s, 1, :, n * HD : (n + 1) * HD]
                    k_pair[n, t, rows, :] = k
                    v_pair[n, t, rows, :] = v
                    kt_pair[n, t, :, rows] = k.T
                    vt_pair[n, t, :, rows] = v.T
            for cols in tiles_f:
                for n in heads:
                    s = dot_nt(k_pair[n, t], q_st[n, cols, :])
                    s_a = s[:BLK]
                    if first:
                        s_a = s_a + causal
                    s_b = s[BLK:] + second
                    top = jnp.max(fold(jnp.maximum(s_a, s_b), jnp.maximum), axis=0, keepdims=True)
                    if not first:
                        old = m_st[n, 0:1, cols]
                        top = jnp.maximum(top, old)
                        alpha = jnp.exp2((old - top) * EXP_SCALE)
                    p_a = jnp.exp2((s_a - top) * EXP_SCALE)
                    p_b = jnp.exp2((s_b - top) * EXP_SCALE)
                    p_low = jnp.concatenate([p_a.astype(LOW), p_b.astype(LOW)], axis=0)
                    p_st[n, t, :, cols] = p_low
                    total = fold(p_a + p_b, jnp.add)
                    out = dot_nn(vt_pair[n, t], p_low)
                    if first:
                        l_st[n, :, cols] = total
                        ot_st[n, :, cols] = out
                    else:
                        l_st[n, :, cols] = l_st[n, :, cols] * alpha + total
                        ot_st[n, :, cols] = ot_st[n, :, cols] * alpha + out
                    m_st[n, 0:1, cols] = top
                    mt_st[n, t, 0:1, cols] = top

        def more_forward(t, carry):
            forward(t, False)
            return carry

        forward(0, True)
        lax.fori_loop(1, pairs, more_forward, 0)
        for h in range(GRP):
            for n in heads:
                cols = slice(h * BLK, (h + 1) * BLK)
                r = 1.0 / jnp.sum(l_st[n, :, cols], axis=0, keepdims=True)
                out = (ot_st[n, :, cols] * r).astype(LOW)
                o_ref[:, n * QW + h * HD : n * QW + (h + 1) * HD] = out.T
                l_st[n, 0:1, cols] = r
                in_st[n, 0:1, cols] = jnp.sum(
                    gt_st[n, :, cols].astype(F32) * out.astype(F32), axis=0, keepdims=True
                )

        def backward(t, first):
            for cols in tiles_b:
                for n in heads:
                    f = jnp.exp2((mt_st[n, t, 0:1, cols] - m_st[n, 0:1, cols]) * EXP_SCALE) * l_st[n, 0:1, cols]
                    w = p_st[n, t, :, cols].astype(F32) * f
                    w_st[n, :, cols] = w.astype(LOW)
                    dp = dot_nn(v_pair[n, t], gt_st[n, :, cols])
                    ds = (w * (dp - in_st[n, 0:1, cols])).astype(LOW)
                    ds_st[n, :, cols] = ds
                    dq = dot_nn(kt_pair[n, t], ds)
                    if first:
                        dqt_st[n, :, cols] = dq
                    else:
                        dqt_st[n, :, cols] += dq
            for n in heads:
                dv = dot_nn(w_st[n], g_st[n])
                dk = dot_nn(ds_st[n], q_st[n])
                for e in range(2):
                    s = chain[2 * t + e]
                    dv_acc[n, s] += dv[e * BLK : (e + 1) * BLK, :]
                    dk_acc[n, s] += dk[e * BLK : (e + 1) * BLK, :]

        def more_backward(t, carry):
            backward(t, False)
            return carry

        backward(0, True)
        lax.fori_loop(1, pairs, more_backward, 0)
        for h in range(GRP):
            for n in heads:
                cols = slice(h * BLK, (h + 1) * BLK)
                dq_ref[:, n * QW + h * HD : n * QW + (h + 1) * HD] = (dqt_st[n, :, cols] * SCALE).astype(LOW).T

    one_block(2 * y + c, q_own, g_own, o_own, dq_own)
    one_block(2 * y + 1 - c, q_par, g_par, o_par, dq_par)
    for s in range(SLOTS):
        for n in heads:
            dk_out[s, :, n * HD : (n + 1) * HD] = (dk_acc[n, s] * SCALE).astype(LOW)
            dv_out[s, :, n * HD : (n + 1) * HD] = dv_acc[n, s].astype(LOW)


def attention_onward_kernel(*refs):
    attention_kernel(*refs[:8], *refs[10:])


def attention(chunk, place, parents, labels, q, q_par, g, g_par, kv, before):
    wide = NG * QW
    own = pl.BlockSpec((BLK, wide), lambda i, place, par, lab: (0, (place[1] * HALF + chunk * PER) // NG + i))
    par = pl.BlockSpec((BLK, wide), lambda i, place, par, lab: (0, chunk * PER // NG + i))
    par_out = pl.BlockSpec((BLK, wide), lambda i, place, par, lab: (0, i))
    kv_in = pl.BlockSpec((SLOTS, 2, BLK, NG * HD), lambda i, place, par, lab: (0, 0, 0, i))
    grad = pl.BlockSpec((SLOTS, BLK, NG * HD), lambda i, place, par, lab: (0, 0, i))
    own_shape = jax.ShapeDtypeStruct((BLK, 2 * HALF * QW), LOW)
    par_shape = jax.ShapeDtypeStruct((BLK, PER * QW), LOW)
    grad_shape = jax.ShapeDtypeStruct((SLOTS, BLK, PER * HD), LOW)
    rows = GRP * BLK
    return pl.pallas_call(
        attention_onward_kernel if before else attention_kernel,
        grid_spec=pltpu.PrefetchScalarGridSpec(
            num_scalar_prefetch=3,
            grid=(PER // NG,),
            in_specs=[own, par, own, par, kv_in] + [pl.BlockSpec(memory_space=pl.ANY)] * len(before),
            out_specs=[own, par_out, own, par_out] + [grad] * 2,
            scratch_shapes=[
                pltpu.SMEM((SLOTS,), jnp.int32),
                pltpu.VMEM((NG, PAIRS, 2 * BLK, HD), LOW),
                pltpu.VMEM((NG, PAIRS, 2 * BLK, HD), LOW),
                pltpu.VMEM((NG, PAIRS, HD, 2 * BLK), LOW),
                pltpu.VMEM((NG, PAIRS, HD, 2 * BLK), LOW),
                pltpu.VMEM((NG, rows, HD), LOW),
                pltpu.VMEM((NG, rows, HD), LOW),
                pltpu.VMEM((NG, HD, rows), LOW),
                pltpu.VMEM((NG, PAIRS, 2 * BLK, rows), LOW),
                pltpu.VMEM((NG, 2 * BLK, rows), LOW),
                pltpu.VMEM((NG, 2 * BLK, rows), LOW),
                pltpu.VMEM((NG, 8, rows), F32),
                pltpu.VMEM((NG, PAIRS, 8, rows), F32),
                pltpu.VMEM((NG, 8, rows), F32),
                pltpu.VMEM((NG, 8, rows), F32),
                pltpu.VMEM((NG, HD, rows), F32),
                pltpu.VMEM((NG, HD, rows), F32),
                pltpu.VMEM((NG, SLOTS, BLK, HD), F32),
                pltpu.VMEM((NG, SLOTS, BLK, HD), F32),
            ],
        ),
        out_shape=[own_shape, par_shape, own_shape, par_shape] + [grad_shape] * 2,
        input_output_aliases={8: 0, 9: 2} if before else {},
        compiler_params=pltpu.CompilerParams(
            dimension_semantics=("arbitrary",), vmem_limit_bytes=48 * 2**20
        ),
        cost_estimate=pl.CostEstimate(
            flops=6 * 2 * PER * rows * 2 * 4 * BLK * HD * 4,
            bytes_accessed=8 * BLK * PER * QW * 2,
            transcendentals=PER * rows * 2 * 4 * BLK,
        ),
        name="tree_attention",
    )(place, parents, labels, q, q_par, g, g_par, kv, *before)


def weight_kernel(x, dv, out):
    tokens = 2 * NZ * BLK
    out[...] = dot_tn(x[...].reshape(tokens, -1), dv[...].reshape(tokens, -1)).astype(LOW)


def weight_partial(x, dv):
    tall, wide, step = x.shape[2], dv.shape[2], 256
    return pl.pallas_call(
        weight_kernel,
        grid=(tall // step,),
        in_specs=[
            pl.BlockSpec((2 * NZ, BLK, step), lambda i: (0, 0, i)),
            pl.BlockSpec((2 * NZ, BLK, wide), lambda i: (0, 0, 0)),
        ],
        out_specs=pl.BlockSpec((step, wide), lambda i: (i, 0)),
        out_shape=jax.ShapeDtypeStruct((tall, wide), LOW),
        cost_estimate=pl.CostEstimate(
            flops=2 * NZ * 2 * BLK * tall * wide, bytes_accessed=NZ * 2 * BLK * (tall + wide) * 2, transcendentals=0
        ),
        name="weight_partial",
    )(x, dv)


def kv_kernel(k, v, out):
    for half in range(2):
        at = slice(half * HALF * HD, (half + 1) * HALF * HD)
        out[half, 0] = k[:, at]
        out[half, 1] = v[:, at]


def kv_sends(k, v):
    width = HALF * HD
    row = pl.BlockSpec((BLK, 2 * width), lambda i: (0, 0))
    return pl.pallas_call(
        kv_kernel,
        grid=(NY,),
        in_specs=[row, row],
        out_specs=pl.BlockSpec((2, 2, BLK, width), lambda i: (i, 0, 0, 0)),
        out_shape=jax.ShapeDtypeStruct((SLOTS, 2, BLK, width), LOW),
        name="kv_sends",
    )(k, v)


def x_kernel(x, out):
    piece = x.shape[1] // (NX * NZ)
    for i in range(NX):
        part = x[:, pl.ds((i * NZ + pl.program_id(0)) * piece, piece)]
        for e in range(2):
            out[e, :, i * piece : (i + 1) * piece] = part


def x_sends(x):
    wide = x.shape[1] // NZ
    return pl.pallas_call(
        x_kernel,
        grid=(NZ,),
        in_specs=[pl.BlockSpec(x.shape, lambda i: (0, 0))],
        out_specs=pl.BlockSpec((2, BLK, wide), lambda i: (i, 0, 0)),
        out_shape=jax.ShapeDtypeStruct((2 * NZ, BLK, wide), LOW),
        name="x_sends",
    )(x)


def sum_kernel(parts, total, sends):
    width = parts.shape[2]
    for half in range(2):
        acc = parts[half].astype(F32)
        for i in range(1, NY):
            acc = acc + parts[2 * i + half].astype(F32)
        acc = acc.astype(LOW)
        total[:, half * width : (half + 1) * width] = acc
        for i in range(NZ):
            sends[2 * i + half] = acc


def sum_blocks(parts):
    rows, width = parts.shape[1:]
    return pl.pallas_call(
        sum_kernel,
        out_shape=[
            jax.ShapeDtypeStruct((rows, 2 * width), LOW),
            jax.ShapeDtypeStruct((2 * NZ, rows, width), LOW),
        ],
        name="sum_blocks",
    )(parts)


def finish_kernel(parts, out):
    width = parts.shape[2]
    for half in range(2):
        acc = parts[half].astype(F32)
        for i in range(1, NX * NY):
            acc = acc + parts[2 * i + half].astype(F32)
        out[:, half * width : (half + 1) * width] = acc * (16 * SLOTS * BLK) ** -0.5


def finish_weight(parts):
    rows, width = parts.shape[1:]
    return pl.pallas_call(
        finish_kernel, out_shape=jax.ShapeDtypeStruct((rows, 2 * width), F32), name="finish_weight"
    )(parts)


def device(x, z, y, c):
    return (x * NZ + z) * SLOTS + y * 2 + c


def per_device(query_rows, key_rows, value_rows, layer_input, out_grad, parents, labels):
    ctx = lax.axis_index("ctx")
    y, c = ctx // 2, ctx % 2
    place = jnp.stack([y, c]).astype(jnp.int32)
    q, k, v, g, x = query_rows[0], key_rows[0], value_rows[0], out_grad[0], layer_input[0]
    along_z = [[device(i, j, m, n) for j in range(NZ) for n in range(2)] for i in range(NX) for m in range(NY)]
    across = [[device(i, j, m, n) for i in range(NX) for m in range(NY) for n in range(2)] for j in range(NZ)]

    def swap(a):
        return lax.ppermute(a, "ctx", [(i, i ^ 1) for i in range(SLOTS)])

    def exchange(a, groups):
        return lax.all_to_all(a, ("dp", "ctx"), 0, 0, axis_index_groups=groups)

    def cols(a, start, width):
        return lax.dynamic_slice_in_dim(a, start, width, 1)

    at = (1 - c) * HALF * QW
    kv = lax.all_to_all(kv_sends(k, v), "ctx", 0, 0)
    q_par = swap(cols(q, at, HALF * QW))
    g_par = swap(cols(g, at, HALF * QW))
    x_all = exchange(x_sends(x), along_z)
    o_own, o_par, dq_own, dq_par, dk, dv = attention(0, place, parents, labels, q, q_par, g, g_par, kv, ())
    dv_terms = lax.all_to_all(dv, "ctx", 0, 0)
    dk, dv_terms = lax.optimization_barrier((dk, dv_terms))
    value_grad, dv_sends = sum_blocks(dv_terms)
    dv_all = exchange(dv_sends, along_z)
    key_grad, _ = sum_blocks(lax.all_to_all(dk, "ctx", 0, 0))
    partial = weight_partial(x_all, dv_all)
    weight_grad = finish_weight(exchange(partial.reshape(2 * NX * NY, -1, partial.shape[1]), across))
    out = lax.dynamic_update_slice_in_dim(o_own, swap(o_par), at, 1)
    query_grad = lax.dynamic_update_slice_in_dim(dq_own, swap(dq_par), at, 1)
    return out[None], query_grad[None], key_grad[None], value_grad[None], weight_grad


def solution(mesh):
    rows = P("dp", "ctx", None)
    return jax.shard_map(
        per_device,
        mesh=mesh,
        in_specs=(rows,) * 5 + (P("dp", None), P("dp", None)),
        out_specs=(rows,) * 4 + (P(("dp", "ctx"), None),),
        check_vma=False,
    )
```

profile of v0, /device:TPU:1, one launch (start us, length us, event | category | flops | bytes accessed | tf_op | source)
XLA Modules:
  0.0 180.7 jit_solution(2001757911983912673)
XLA Ops:
  0.6 2.9 %kv_sends.1 = bf16[8,2,128,512]{3,2,1,0:T(8,128)(2,1)} custom-call(bf16[128,1024]{1,0:T(8,128)(2,1)} %bitcast.24, bf16[128,1024]{1,0:T(8,128)(2,1)} %bitcast.25), custom_call_target="tpu_custom_call" | custom-call | tf_op jit(solution)/shard_map/kv_sends/pallas_call | solution.py:280
  3.5 6.0 %all-to-all-start = ((bf16[8,2,128,512]{3,2,1,0:T(8,128)(2,1)}), bf16[8,2,128,512]{3,2,1,0:T(8,128)(2,1)S(1)}, u32[]{:S(2)}, u32[]{:S(2)}) async-start(bf16[8,2,128,512]{3,2,1,0:T(8,128)(2,1)} %kv_sends.1), calls=%async_computation | async-start | bytes 4194304 | tf_op jit(solution)/shard_map/all_to_all | solution.py:372
  9.5 2.3 %dynamic-slice_bitcast_fusion.1 = bf16[128,4096]{1,0:T(8,128)(2,1)} fusion(bf16[1,128,8192]{2,1,0:T(8,128)(2,1)} %param.7, s32[]{:T(128)S(6)} %select_n.19), kind=kLoop, calls=%fused_computation.3 | loop fusion | bytes 2097156 | tf_op jit(solution)/shard_map/dynamic_slice | solution.py:369
  11.8 2.3 %dynamic-slice_bitcast_fusion = bf16[128,4096]{1,0:T(8,128)(2,1)} fusion(bf16[1,128,8192]{2,1,0:T(8,128)(2,1)} %param.11, s32[]{:T(128)S(6)} %select_n.19), kind=kLoop, calls=%fused_computation.2 | loop fusion | bytes 2097156 | tf_op jit(solution)/shard_map/dynamic_slice | solution.py:369
  14.7 2.6 %collective-permute-done.1.g_par = bf16[128,4096]{1,0:T(8,128)(2,1)} collective-permute-done((bf16[128,4096]{1,0:T(8,128)(2,1)}, bf16[128,4096]{1,0:T(8,128)(2,1)}, u32[]{:S(2)}, u32[]{:S(2)}) %collective-permute-start.1) | collective-permute-done | bytes 1048608 | tf_op jit(solution)/shard_map/ppermute | solution.py:363
  17.3 18.6 %all-to-all-done.kv = bf16[8,2,128,512]{3,2,1,0:T(8,128)(2,1)S(1)} async-done(((bf16[8,2,128,512]{3,2,1,0:T(8,128)(2,1)}), bf16[8,2,128,512]{3,2,1,0:T(8,128)(2,1)S(1)}, u32[]{:S(2)}, u32[]{:S(2)}) %all-to-all-start) | async-done | bytes 2097184 | tf_op jit(solution)/shard_map/all_to_all | solution.py:372
  37.2 16.8 %tree_attention.1 = (bf16[128,8192]{1,0:T(8,128)(2,1)}, bf16[128,4096]{1,0:T(8,128)(2,1)S(1)}, bf16[128,8192]{1,0:T(8,128)(2,1)}, bf16[128,4096]{1,0:T(8,128)(2,...) custom-call(s32[2]{0:T(128)S(1)} %pad_add_fusion.place, s32[1,8]{1,0:T(1,128)S(1)} %copy-done, ...), custom_call_target="tpu_custom_call" | custom-call | flops 25769803776 | bytes 8388608 | tf_op jit(solution)/shard_map/tree_attention/pallas_call | solution.py:204
  53.9 4.3 %all-to-all-start.1 = ((bf16[8,128,512]{2,1,0:T(8,128)(2,1)}), bf16[8,128,512]{2,1,0:T(8,128)(2,1)S(1)}, u32[]{:S(2)}, u32[]{:S(2)}) async-start(bf16[8,128,512]{2,1,0:T(8,128)(2,1)} %get-tuple-element.21), calls=%async_computation.1 | async-start | bytes 2097152 | tf_op jit(solution)/shard_map/all_to_all | solution.py:377
  58.3 3.1 %x_sends.1 = bf16[8,128,1024]{2,1,0:T(8,128)(2,1)} custom-call(bf16[128,4096]{1,0:T(8,128)(2,1)} %bitcast.21), custom_call_target="tpu_custom_call" | custom-call | tf_op jit(solution)/shard_map/x_sends/pallas_call | solution.py:300
  61.4 12.0 %all-to-all-done.1.parts = bf16[8,128,512]{2,1,0:T(8,128)(2,1)S(1)} async-done(((bf16[8,128,512]{2,1,0:T(8,128)(2,1)}), bf16[8,128,512]{2,1,0:T(8,128)(2,1)S(1)}, u32[]{:S(2)}, u32[]{:S(2)}) %all-to-all-start.1) | async-done | bytes 1048608 | tf_op jit(solution)/shard_map/all_to_all | solution.py:377
  74.4 15.1 %all-to-all-start.3 = ((bf16[8,128,1024]{2,1,0:T(8,128)(2,1)}), bf16[8,128,1024]{2,1,0:T(8,128)(2,1)}, u32[]{:S(2)}, u32[]{:S(2)}) async-start(bf16[8,128,1024]{2,1,0:T(8,128)(2,1)} %x_sends.1), calls=%async_computation.3 | async-start | bytes 4194304 | tf_op jit(solution)/shard_map/all_to_all | solution.py:366
  89.4 2.4 %sum_blocks.3 = (bf16[128,1024]{1,0:T(8,128)(2,1)}, bf16[8,128,512]{2,1,0:T(8,128)(2,1)}) custom-call(bf16[8,128,512]{2,1,0:T(8,128)(2,1)} %copy-done.3), custom_call_target="tpu_custom_call" | custom-call | tf_op jit(solution)/shard_map/sum_blocks/pallas_call | solution.py:324
  91.9 24.0 %all-to-all-done.3.x = bf16[8,128,1024]{2,1,0:T(8,128)(2,1)} async-done(((bf16[8,128,1024]{2,1,0:T(8,128)(2,1)}), bf16[8,128,1024]{2,1,0:T(8,128)(2,1)}, u32[]{:S(2)}, u32[]{:S(2)}) %all-to-all-start.3) | async-done | bytes 2097184 | tf_op jit(solution)/shard_map/all_to_all | solution.py:366
  115.9 4.3 %all-to-all-start.4 = ((bf16[8,128,512]{2,1,0:T(8,128)(2,1)}), bf16[8,128,512]{2,1,0:T(8,128)(2,1)S(1)}, u32[]{:S(2)}, u32[]{:S(2)}) async-start(bf16[8,128,512]{2,1,0:T(8,128)(2,1)} %get-tuple-element.26), calls=%async_computation.4 | async-start | bytes 2097152 | tf_op jit(solution)/shard_map/all_to_all | solution.py:366
  120.4 14.9 %all-to-all-done.4.dv = bf16[8,128,512]{2,1,0:T(8,128)(2,1)S(1)} async-done(((bf16[8,128,512]{2,1,0:T(8,128)(2,1)}), bf16[8,128,512]{2,1,0:T(8,128)(2,1)S(1)}, u32[]{:S(2)}, u32[]{:S(2)}) %all-to-all-start.4) | async-done | bytes 1048608 | tf_op jit(solution)/shard_map/all_to_all | solution.py:366
  136.3 4.3 %all-to-all-start.2 = ((bf16[8,128,512]{2,1,0:T(8,128)(2,1)}), bf16[8,128,512]{2,1,0:T(8,128)(2,1)S(1)}, u32[]{:S(2)}, u32[]{:S(2)}) async-start(bf16[8,128,512]{2,1,0:T(8,128)(2,1)} %get-tuple-element.22), calls=%async_computation.2 | async-start | bytes 2097152 | tf_op jit(solution)/shard_map/all_to_all | solution.py:381
  140.8 4.8 %weight_partial.1 = bf16[1024,512]{1,0:T(8,128)(2,1)} custom-call(bf16[8,128,1024]{2,1,0:T(8,128)(2,1)} %all-to-all-done.3.x, bf16[8,128,512]{2,1,0:T(8,128)(2,1)} %copy-done.4), custom_call_target="tpu_custom_call" | custom-call | flops 1073741824 | bytes 3145728 | tf_op jit(solution)/shard_map/weight_partial/pallas_call | solution.py:254
  145.6 10.1 %all-to-all-done.2.parts = bf16[8,128,512]{2,1,0:T(8,128)(2,1)S(1)} async-done(((bf16[8,128,512]{2,1,0:T(8,128)(2,1)}), bf16[8,128,512]{2,1,0:T(8,128)(2,1)S(1)}, u32[]{:S(2)}, u32[]{:S(2)}) %all-to-all-start.2) | async-done | bytes 1048608 | tf_op jit(solution)/shard_map/all_to_all | solution.py:381
  155.7 6.0 %all-to-all-start.5 = ((bf16[32,32,512]{2,1,0:T(8,128)(2,1)}), bf16[32,32,512]{2,1,0:T(8,128)(2,1)}, u32[]{:S(2)}, u32[]{:S(2)}) async-start(bf16[32,32,512]{2,1,0:T(8,128)(2,1)} %bitcast.20), calls=%async_computation.5 | async-start | bytes 2097152 | tf_op jit(solution)/shard_map/all_to_all | solution.py:366
  161.7 2.3 %bitcast_dynamic-update-slice_fusion.1 = bf16[1,128,8192]{2,1,0:T(8,128)(2,1)} fusion(bf16[1,128,8192]{2,1,0:T(8,128)(2,1)} %bitcast.26, s32[]{:T(128)S(6)} %select_n.19, bf16[128,4096]{1,0:T(8,128)(2,1)} %collective-permute-done.2), kind=kLoop, calls=%fused_computation.1 | loop fusion | bytes 2097156 | tf_op jit(solution)/shard_map/dynamic_update_slice | solution.py:384
  164.0 2.3 %bitcast_dynamic-update-slice_fusion = bf16[1,128,8192]{2,1,0:T(8,128)(2,1)} fusion(bf16[1,128,8192]{2,1,0:T(8,128)(2,1)} %bitcast.10, s32[]{:T(128)S(6)} %select_n.19, bf16[128,4096]{1,0:T(8,128)(2,1)} %collective-permute-done.3), kind=kLoop, calls=%fused_computation | loop fusion | bytes 2097156 | tf_op jit(solution)/shard_map/dynamic_update_slice | solution.py:385
  166.3 2.4 %sum_blocks.2 = (bf16[128,1024]{1,0:T(8,128)(2,1)}, bf16[8,128,512]{2,1,0:T(8,128)(2,1)}) custom-call(bf16[8,128,512]{2,1,0:T(8,128)(2,1)} %copy-done.2), custom_call_target="tpu_custom_call" | custom-call | tf_op jit(solution)/shard_map/sum_blocks/pallas_call | solution.py:324
  168.7 10.0 %all-to-all-done.5.parts = bf16[32,32,512]{2,1,0:T(8,128)(2,1)} async-done(((bf16[32,32,512]{2,1,0:T(8,128)(2,1)}), bf16[32,32,512]{2,1,0:T(8,128)(2,1)}, u32[]{:S(2)}, u32[]{:S(2)}) %all-to-all-start.5) | async-done | bytes 1048608 | tf_op jit(solution)/shard_map/all_to_all | solution.py:366
  178.7 2.0 %finish_weight.1 = f32[32,1024]{1,0:T(8,128)} custom-call(bf16[32,32,512]{2,1,0:T(8,128)(2,1)} %all-to-all-done.5.parts), custom_call_target="tpu_custom_call" | custom-call | tf_op jit(solution)/shard_map/finish_weight/pallas_call | solution.py:345
  (20 shorter events, 4.3 us)
Async XLA Ops:
  3.5 32.3 %all-to-all-start = ((bf16[8,2,128,512]{3,2,1,0:T(8,128)(2,1)}), bf16[8,2,128,512]{3,2,1,0:T(8,128)(2,1)S(1)}, u32[]{:S(2)}, u32[]{:S(2)}) async-start(bf16[8,2,128,512]{3,2,1,0:T(8,128)(2,1)} %kv_sends.1), calls=%async_computation | async-start | bytes 4194304 | tf_op jit(solution)/shard_map/all_to_all | solution.py:372
  9.5 27.7 %copy-start = (s32[1,8]{1,0:T(1,128)S(1)}, s32[1,8]{1,0:T(1,128)}, u32[]{:S(2)}) copy-start(s32[1,8]{1,0:T(1,128)} %parents.1) | copy-start | bytes 100
  9.5 27.7 %copy-start.1 = (s32[1,8]{1,0:T(1,128)S(1)}, s32[1,8]{1,0:T(1,128)}, u32[]{:S(2)}) copy-start(s32[1,8]{1,0:T(1,128)} %labels.1) | copy-start | bytes 100
  11.8 2.9 %collective-permute-start = (bf16[128,4096]{1,0:T(8,128)(2,1)}, bf16[128,4096]{1,0:T(8,128)(2,1)S(1)}, u32[]{:S(2)}, u32[]{:S(2)}) collective-permute-start(bf16[128,4096]{1,0:T(8,128)(2,1)} %dynamic-slice_bitcast_fusion.1), channel_id=1, source_target_pairs={{0,1},{1,0},{2,3},{3,2},{4,5},{5,4},{6,7},{7,6},{8,9},{9,8},{10,11... | collective-permute-start | bytes 3145736 | tf_op jit(solution)/shard_map/ppermute | solution.py:363
  14.1 3.1 %collective-permute-start.1 = (bf16[128,4096]{1,0:T(8,128)(2,1)}, bf16[128,4096]{1,0:T(8,128)(2,1)}, u32[]{:S(2)}, u32[]{:S(2)}) collective-permute-start(bf16[128,4096]{1,0:T(8,128)(2,1)} %dynamic-slice_bitcast_fusion), channel_id=1, source_target_pairs={{0,1},{1,0},{2,3},{3,2},{4,5},{5,4},{6,7},{7,6},{8,9},{9,8},{10,11... | collective-permute-start | bytes 3145736 | tf_op jit(solution)/shard_map/ppermute | solution.py:363
  35.8 1.3 copy-start.5
  53.9 19.4 %all-to-all-start.1 = ((bf16[8,128,512]{2,1,0:T(8,128)(2,1)}), bf16[8,128,512]{2,1,0:T(8,128)(2,1)S(1)}, u32[]{:S(2)}, u32[]{:S(2)}) async-start(bf16[8,128,512]{2,1,0:T(8,128)(2,1)} %get-tuple-element.21), calls=%async_computation.1 | async-start | bytes 2097152 | tf_op jit(solution)/shard_map/all_to_all | solution.py:377
  73.4 1.0 copy-start.3
  74.4 41.5 %all-to-all-start.3 = ((bf16[8,128,1024]{2,1,0:T(8,128)(2,1)}), bf16[8,128,1024]{2,1,0:T(8,128)(2,1)}, u32[]{:S(2)}, u32[]{:S(2)}) async-start(bf16[8,128,1024]{2,1,0:T(8,128)(2,1)} %x_sends.1), calls=%async_computation.3 | async-start | bytes 4194304 | tf_op jit(solution)/shard_map/all_to_all | solution.py:366
  115.9 19.4 %all-to-all-start.4 = ((bf16[8,128,512]{2,1,0:T(8,128)(2,1)}), bf16[8,128,512]{2,1,0:T(8,128)(2,1)S(1)}, u32[]{:S(2)}, u32[]{:S(2)}) async-start(bf16[8,128,512]{2,1,0:T(8,128)(2,1)} %get-tuple-element.26), calls=%async_computation.4 | async-start | bytes 2097152 | tf_op jit(solution)/shard_map/all_to_all | solution.py:366
  120.2 41.5 %collective-permute-start.2 = (bf16[128,4096]{1,0:T(8,128)(2,1)S(1)}, bf16[128,4096]{1,0:T(8,128)(2,1)}, u32[]{:S(2)}, u32[]{:S(2)}) collective-permute-start(bf16[128,4096]{1,0:T(8,128)(2,1)S(1)} %get-tuple-element.17), channel_id=1, source_target_pairs={{0,1},{1,0},{2,3},{3,2},{4,5},{5,4},{6,7},{7,6},{8,9},{9,8},{10,11... | collective-permute-start | bytes 3145736 | tf_op jit(solution)/shard_map/ppermute | solution.py:363
  135.3 1.0 copy-start.4
  136.3 19.4 %all-to-all-start.2 = ((bf16[8,128,512]{2,1,0:T(8,128)(2,1)}), bf16[8,128,512]{2,1,0:T(8,128)(2,1)S(1)}, u32[]{:S(2)}, u32[]{:S(2)}) async-start(bf16[8,128,512]{2,1,0:T(8,128)(2,1)} %get-tuple-element.22), calls=%async_computation.2 | async-start | bytes 2097152 | tf_op jit(solution)/shard_map/all_to_all | solution.py:381
  140.6 23.4 %collective-permute-start.3 = (bf16[128,4096]{1,0:T(8,128)(2,1)S(1)}, bf16[128,4096]{1,0:T(8,128)(2,1)}, u32[]{:S(2)}, u32[]{:S(2)}) collective-permute-start(bf16[128,4096]{1,0:T(8,128)(2,1)S(1)} %get-tuple-element.19), channel_id=1, source_target_pairs={{0,1},{1,0},{2,3},{3,2},{4,5},{5,4},{6,7},{7,6},{8,9},{9,8},{10,11... | collective-permute-start | bytes 3145736 | tf_op jit(solution)/shard_map/ppermute | solution.py:363
  155.7 8.3 %copy-start.2 = (bf16[8,128,512]{2,1,0:T(8,128)(2,1)}, bf16[8,128,512]{2,1,0:T(8,128)(2,1)S(1)}, u32[]{:S(2)}) copy-start(bf16[8,128,512]{2,1,0:T(8,128)(2,1)S(1)} %all-to-all-done.2.parts) | copy-start | bytes 3145732
  155.7 22.9 %all-to-all-start.5 = ((bf16[32,32,512]{2,1,0:T(8,128)(2,1)}), bf16[32,32,512]{2,1,0:T(8,128)(2,1)}, u32[]{:S(2)}, u32[]{:S(2)}) async-start(bf16[32,32,512]{2,1,0:T(8,128)(2,1)} %bitcast.20), calls=%async_computation.5 | async-start | bytes 2097152 | tf_op jit(solution)/shard_map/all_to_all | solution.py:366
where the time goes:
time: 181 us
  waiting for transfers between devices  92.1 us (51%)
  starting transfers between devices  40.9 us (23%)
  Pallas kernels  34.5 us (19%)
  local copies, waits for them, and re-layouts  12.5 us (7%)
    all_to_all x3, waiting for transfers between devices, exchange(): return lax.all_to_all(a, ('dp', 'ctx'), 0, 0, axis_index_groups=groups)  48.9 us
    all_to_all x3, starting transfers between devices, exchange(): return lax.all_to_all(a, ('dp', 'ctx'), 0, 0, axis_index_groups=groups)  25.4 us
    all_to_all x1, waiting for transfers between devices, per_device(): kv = lax.all_to_all(kv_sends(k, v), 'ctx', 0, 0)  18.6 us
    pallas_call x1, Pallas kernels, attention(): pl.pallas_call(attention_onward_kernel if before else attention_kernel, g...  16.8 us
    all_to_all x1, waiting for transfers between devices, per_device(): dv_terms = lax.all_to_all(dv, 'ctx', 0, 0)  12 us
    all_to_all x1, waiting for transfers between devices, per_device(): key_grad, _ = sum_blocks(lax.all_to_all(dk, 'ctx', 0, 0))  10.1 us
    all_to_all x1, starting transfers between devices, per_device(): kv = lax.all_to_all(kv_sends(k, v), 'ctx', 0, 0)  5.97 us
    pallas_call x2, Pallas kernels, sum_blocks(): pl.pallas_call(sum_kernel, out_shape=[jax.ShapeDtypeStruct((rows, 2 * wid...  4.84 us
  transfers between devices with their start and end apart: 10, of which 7 were waited for; matrix products, arithmetic and copies ran while one was open for 5% of the time, Pallas kernels for 7%

commit v1 on v0

v1 whole, which is shorter than its diff:
```python
import jax
import jax.numpy as jnp
from jax import lax
from jax.experimental import pallas as pl
from jax.experimental.pallas import tpu as pltpu
from jax.sharding import PartitionSpec as P

HD = 128
BLK = 128
GRP = 8
NY = 4
NZ = 4
NX = 4
HALF = 4
QW = GRP * HD
SLOTS = 2 * NY
PAIRS = 4
NG = 2
LOW = jnp.bfloat16
F32 = jnp.float32
SCALE = HD**-0.5
EXP_SCALE = SCALE * 1.4426950408889634
MASKED = -1e30


def dot_nt(a, b):
    return lax.dot_general(a, b, (((1,), (1,)), ((), ())), preferred_element_type=F32)


def dot_nn(a, b):
    return lax.dot_general(a, b, (((1,), (0,)), ((), ())), preferred_element_type=F32)


def dot_tn(a, b):
    return lax.dot_general(a, b, (((0,), (0,)), ((), ())), preferred_element_type=F32)


def walk(parents, block, chain):
    def above(step, carry):
        current, count = carry
        parent = parents[0, current]
        more = parent != current
        current = jnp.where(more, parent, current)
        chain[step + 1] = current
        return current, count + more.astype(jnp.int32)

    chain[0] = block
    return lax.fori_loop(0, SLOTS - 1, above, (block, jnp.int32(1)))[1]


def fold(a, op):
    while a.shape[0] > 8:
        half = a.shape[0] // 2
        a = op(a[:half], a[half:])
    return a


def causal_mask():
    key_pos = lax.broadcasted_iota(jnp.int32, (BLK, BLK), 0)
    query_pos = lax.broadcasted_iota(jnp.int32, (BLK, BLK), 1)
    causal = jnp.where(key_pos <= query_pos, 0.0, MASKED).astype(F32)
    return jnp.concatenate([causal] * GRP, axis=1)


def block_sign(labels, block):
    return jnp.full((BLK, HD), jnp.where(labels[0, block] == 2, -1.0, 1.0), F32).astype(LOW)


def masked(s, t, count, first, causal):
    second = jnp.where(2 * t + 1 < count, 0.0, MASKED).astype(F32)
    s_a = s[:BLK]
    if first:
        s_a = s_a + causal
    return s_a, s[BLK:] + second


def over_pairs(step, pairs):
    def more(t, carry):
        step(t, False)
        return carry

    step(0, True)
    lax.fori_loop(1, pairs, more, 0)


def forward_kernel(
    place, parents, labels,
    q_own, q_par, g_own, g_par, kv,
    o_own, o_par, dv_out, stats,
    chain, k_pair, vt_pair, q_st, g_st, gt_st, p_st, w_st, m_st, mt_st, l_st, ot_st, dv_acc,
):
    y = place[0]
    c = place[1]
    heads = range(NG)
    dv_acc[...] = jnp.zeros_like(dv_acc)
    causal = causal_mask()

    def one_block(which, block, q_ref, g_ref, o_ref):
        count = walk(parents, block, chain)
        pairs = (count + 1) // 2
        sign = block_sign(labels, block)
        for n in heads:
            for h in range(GRP):
                rows = slice(h * BLK, (h + 1) * BLK)
                cols = slice(n * QW + h * HD, n * QW + (h + 1) * HD)
                q_st[n, rows, :] = q_ref[:, cols]
                g = g_ref[:, cols] * sign
                g_st[n, rows, :] = g
                gt_st[n, :, rows] = g.T

        def scores(t, first):
            for n in heads:
                for e in range(2):
                    s = chain[2 * t + e]
                    rows = slice(e * BLK, (e + 1) * BLK)
                    k_pair[n, t, rows, :] = kv[s, 0, :, n * HD : (n + 1) * HD]
                    vt_pair[n, t, :, rows] = kv[s, 1, :, n * HD : (n + 1) * HD].T
            for n in heads:
                s_a, s_b = masked(dot_nt(k_pair[n, t], q_st[n]), t, count, first, causal)
                top = jnp.max(fold(jnp.maximum(s_a, s_b), jnp.maximum), axis=0, keepdims=True)
                if not first:
                    old = m_st[n, 0:1, :]
                    top = jnp.maximum(top, old)
                    alpha = jnp.exp2((old - top) * EXP_SCALE)
                p_a = jnp.exp2((s_a - top) * EXP_SCALE)
                p_b = jnp.exp2((s_b - top) * EXP_SCALE)
                p_low = jnp.concatenate([p_a.astype(LOW), p_b.astype(LOW)], axis=0)
                p_st[n, t] = p_low
                total = fold(p_a + p_b, jnp.add)
                out = dot_nn(vt_pair[n, t], p_low)
                if first:
                    l_st[n] = total
                    ot_st[n] = out
                else:
                    l_st[n] = l_st[n] * alpha + total
                    ot_st[n] = ot_st[n] * alpha + out
                m_st[n, 0:1, :] = top
                mt_st[n, t, 0:1, :] = top

        over_pairs(scores, pairs)
        for n in heads:
            total = jnp.sum(l_st[n], axis=0, keepdims=True)
            l_st[n, 0:1, :] = 1.0 / total
            stats[n, which, 0:1, :] = m_st[n, 0:1, :] * EXP_SCALE + jnp.log2(total)
        for h in range(GRP):
            for n in heads:
                cols = slice(h * BLK, (h + 1) * BLK)
                out = (ot_st[n, :, cols] * l_st[n, 0:1, cols]).astype(LOW)
                o_ref[:, n * QW + h * HD : n * QW + (h + 1) * HD] = out.T
                stats[n, which, 1:2, cols] = jnp.sum(
                    gt_st[n, :, cols].astype(F32) * out.astype(F32), axis=0, keepdims=True
                )

        def values(t, first):
            for n in heads:
                f = jnp.exp2((mt_st[n, t, 0:1, :] - m_st[n, 0:1, :]) * EXP_SCALE) * l_st[n, 0:1, :]
                w_st[n] = (p_st[n, t].astype(F32) * f).astype(LOW)
            for n in heads:
                dv = dot_nn(w_st[n], g_st[n])
                for e in range(2):
                    dv_acc[n, chain[2 * t + e]] += dv[e * BLK : (e + 1) * BLK, :]

        over_pairs(values, pairs)

    one_block(0, 2 * y + c, q_own, g_own, o_own)
    one_block(1, 2 * y + 1 - c, q_par, g_par, o_par)
    for s in range(SLOTS):
        for n in heads:
            dv_out[s, :, n * HD : (n + 1) * HD] = dv_acc[n, s].astype(LOW)


def backward_kernel(
    place, parents, labels,
    q_own, q_par, g_own, g_par, kv, stats,
    dq_own, dq_par, dk_out,
    chain, k_pair, v_pair, kt_pair, q_st, g_st, ds_st, dqt_st, dk_acc,
):
    y = place[0]
    c = place[1]
    heads = range(NG)
    dk_acc[...] = jnp.zeros_like(dk_acc)
    causal = causal_mask()

    def one_block(which, block, q_ref, g_ref, dq_ref):
        count = walk(parents, block, chain)
        sign = block_sign(labels, block)
        for n in heads:
            for h in range(GRP):
                rows = slice(h * BLK, (h + 1) * BLK)
                cols = slice(n * QW + h * HD, n * QW + (h + 1) * HD)
                q_st[n, rows, :] = q_ref[:, cols]
                g_st[n, rows, :] = g_ref[:, cols] * sign

        def grads(t, first):
            for n in heads:
                for e in range(2):
                    s = chain[2 * t + e]
                    rows = slice(e * BLK, (e + 1) * BLK)
                    k = kv[s, 0, :, n * HD : (n + 1) * HD]
                    k_pair[n, rows, :] = k
                    kt_pair[n, :, rows] = k.T
                    v_pair[n, rows, :] = kv[s, 1, :, n * HD : (n + 1) * HD]
            for n in heads:
                s_a, s_b = masked(dot_nt(k_pair[n], q_st[n]), t, count, first, causal)
                dp = dot_nt(v_pair[n], g_st[n])
                lse, inner = stats[n, which, 0:1, :], stats[n, which, 1:2, :]
                ds_a = jnp.exp2(s_a * EXP_SCALE - lse) * (dp[:BLK] - inner)
                ds_b = jnp.exp2(s_b * EXP_SCALE - lse) * (dp[BLK:] - inner)
                ds = jnp.concatenate([ds_a.astype(LOW), ds_b.astype(LOW)], axis=0)
                ds_st[n] = ds
                dq = dot_nn(kt_pair[n], ds)
                if first:
                    dqt_st[n] = dq
                else:
                    dqt_st[n] += dq
            for n in heads:
                dk = dot_nn(ds_st[n], q_st[n])
                for e in range(2):
                    dk_acc[n, chain[2 * t + e]] += dk[e * BLK : (e + 1) * BLK, :]

        over_pairs(grads, (count + 1) // 2)
        for h in range(GRP):
            for n in heads:
                cols = slice(h * BLK, (h + 1) * BLK)
                dq_ref[:, n * QW + h * HD : n * QW + (h + 1) * HD] = (dqt_st[n, :, cols] * SCALE).astype(LOW).T

    one_block(0, 2 * y + c, q_own, g_own, dq_own)
    one_block(1, 2 * y + 1 - c, q_par, g_par, dq_par)
    for s in range(SLOTS):
        for n in heads:
            dk_out[s, :, n * HD : (n + 1) * HD] = (dk_acc[n, s] * SCALE).astype(LOW)


ROWS = GRP * BLK
OWN = pl.BlockSpec((BLK, NG * QW), lambda i, place, par, lab: (0, place[1] * (HALF // NG) + i))
PARTNER = pl.BlockSpec((BLK, NG * QW), lambda i, place, par, lab: (0, i))
KEYS = pl.BlockSpec((SLOTS, 2, BLK, NG * HD), lambda i, place, par, lab: (0, 0, 0, i))
GRADS = pl.BlockSpec((SLOTS, BLK, NG * HD), lambda i, place, par, lab: (0, 0, i))
STATS = pl.BlockSpec((NG, 2, 8, ROWS), lambda i, place, par, lab: (i, 0, 0, 0))
OWN_SHAPE = jax.ShapeDtypeStruct((BLK, 2 * HALF * QW), LOW)
PARTNER_SHAPE = jax.ShapeDtypeStruct((BLK, HALF * QW), LOW)
GRADS_SHAPE = jax.ShapeDtypeStruct((SLOTS, BLK, HALF * HD), LOW)
STATS_SHAPE = jax.ShapeDtypeStruct((HALF, 2, 8, ROWS), F32)


def attention_call(kernel, name, products, in_specs, out_specs, out_shape, scratch):
    return pl.pallas_call(
        kernel,
        grid_spec=pltpu.PrefetchScalarGridSpec(
            num_scalar_prefetch=3,
            grid=(HALF // NG,),
            in_specs=in_specs,
            out_specs=out_specs,
            scratch_shapes=[pltpu.SMEM((SLOTS,), jnp.int32)] + [pltpu.VMEM(*s) for s in scratch],
        ),
        out_shape=out_shape,
        compiler_params=pltpu.CompilerParams(dimension_semantics=("arbitrary",), vmem_limit_bytes=48 * 2**20),
        cost_estimate=pl.CostEstimate(
            flops=4 * products * 2 * HALF * ROWS * 2 * 4 * BLK * HD,
            bytes_accessed=8 * BLK * HALF * QW,
            transcendentals=HALF * ROWS * 2 * 4 * BLK,
        ),
        name=name,
    )


def forward(*args):
    return attention_call(
        forward_kernel, "tree_forward", 3,
        [OWN, PARTNER, OWN, PARTNER, KEYS],
        [OWN, PARTNER, GRADS, STATS],
        [OWN_SHAPE, PARTNER_SHAPE, GRADS_SHAPE, STATS_SHAPE],
        [
            ((NG, PAIRS, 2 * BLK, HD), LOW),
            ((NG, PAIRS, HD, 2 * BLK), LOW),
            ((NG, ROWS, HD), LOW),
            ((NG, ROWS, HD), LOW),
            ((NG, HD, ROWS), LOW),
            ((NG, PAIRS, 2 * BLK, ROWS), LOW),
            ((NG, 2 * BLK, ROWS), LOW),
            ((NG, 8, ROWS), F32),
            ((NG, PAIRS, 8, ROWS), F32),
            ((NG, 8, ROWS), F32),
            ((NG, HD, ROWS), F32),
            ((NG, SLOTS, BLK, HD), F32),
        ],
    )(*args)


def backward(*args):
    return attention_call(
        backward_kernel, "tree_backward", 4,
        [OWN, PARTNER, OWN, PARTNER, KEYS, STATS],
        [OWN, PARTNER, GRADS],
        [OWN_SHAPE, PARTNER_SHAPE, GRADS_SHAPE],
        [
            ((NG, 2 * BLK, HD), LOW),
            ((NG, 2 * BLK, HD), LOW),
            ((NG, HD, 2 * BLK), LOW),
            ((NG, ROWS, HD), LOW),
            ((NG, ROWS, HD), LOW),
            ((NG, 2 * BLK, ROWS), LOW),
            ((NG, HD, ROWS), F32),
            ((NG, SLOTS, BLK, HD), F32),
        ],
    )(*args)


def weight_kernel(place, x_own, x_other, dv, out):
    tokens = NZ * BLK
    c = place[1]
    own = dv[:, pl.ds(c, 1)].reshape(tokens, -1)
    other = dv[:, pl.ds(1 - c, 1)].reshape(tokens, -1)
    total = dot_tn(x_own[...].reshape(tokens, -1), own) + dot_tn(x_other[...].reshape(tokens, -1), other)
    out[...] = total.astype(LOW)


def weight_partial(place, x_own, x_other, dv):
    tall, wide, step = x_own.shape[2], dv.shape[3], 256
    x_spec = pl.BlockSpec((NZ, BLK, step), lambda i, place: (0, 0, i))
    return pl.pallas_call(
        weight_kernel,
        grid_spec=pltpu.PrefetchScalarGridSpec(
            num_scalar_prefetch=1,
            grid=(tall // step,),
            in_specs=[x_spec, x_spec, pl.BlockSpec((NZ, 2, BLK, wide), lambda i, place: (0, 0, 0, 0))],
            out_specs=pl.BlockSpec((step, wide), lambda i, place: (i, 0)),
        ),
        out_shape=jax.ShapeDtypeStruct((tall, wide), LOW),
        cost_estimate=pl.CostEstimate(
            flops=2 * NZ * 2 * BLK * tall * wide, bytes_accessed=NZ * 2 * BLK * (tall + wide) * 2, transcendentals=0
        ),
        name="weight_partial",
    )(place, x_own, x_other, dv)


def kv_kernel(k, v, out):
    for half in range(2):
        at = slice(half * HALF * HD, (half + 1) * HALF * HD)
        out[half, 0] = k[:, at]
        out[half, 1] = v[:, at]


def kv_sends(k, v):
    width = HALF * HD
    row = pl.BlockSpec((BLK, 2 * width), lambda i: (0, 0))
    return pl.pallas_call(
        kv_kernel,
        grid=(NY,),
        in_specs=[row, row],
        out_specs=pl.BlockSpec((2, 2, BLK, width), lambda i: (i, 0, 0, 0)),
        out_shape=jax.ShapeDtypeStruct((SLOTS, 2, BLK, width), LOW),
        name="kv_sends",
    )(k, v)


def x_kernel(x, out):
    piece = x.shape[1] // (NX * NZ)
    for j in range(NZ):
        for i in range(NX):
            at = (i * NZ + j) * piece
            out[j, :, i * piece : (i + 1) * piece] = x[:, at : at + piece]


def x_sends(x):
    return pl.pallas_call(
        x_kernel,
        out_shape=jax.ShapeDtypeStruct((NZ, BLK, x.shape[1] // NZ), LOW),
        name="x_sends",
    )(x)


def sum_kernel(terms, out):
    for e in range(2):
        acc = terms[0, e].astype(F32)
        for i in range(1, NY):
            acc = acc + terms[i, e].astype(F32)
        for i in range(NZ):
            out[i, e] = acc.astype(LOW)


def sum_blocks(terms):
    return pl.pallas_call(
        sum_kernel, out_shape=jax.ShapeDtypeStruct((NZ,) + terms.shape[1:], LOW), name="sum_blocks"
    )(terms)


def finish_kernel(parts, out):
    width = parts.shape[2]
    for half in range(2):
        acc = parts[half].astype(F32)
        for i in range(1, NX * NY):
            acc = acc + parts[2 * i + half].astype(F32)
        out[:, half * width : (half + 1) * width] = acc * (16 * SLOTS * BLK) ** -0.5


def finish_weight(parts):
    rows, width = parts.shape[1:]
    return pl.pallas_call(
        finish_kernel, out_shape=jax.ShapeDtypeStruct((rows, 2 * width), F32), name="finish_weight"
    )(parts)


def device(x, z, y, c):
    return (x * NZ + z) * SLOTS + y * 2 + c


def per_device(query_rows, key_rows, value_rows, layer_input, out_grad, parents, labels):
    ctx = lax.axis_index("ctx")
    y, c = ctx // 2, ctx % 2
    place = jnp.stack([y, c]).astype(jnp.int32)
    q, k, v, g, x = query_rows[0], key_rows[0], value_rows[0], out_grad[0], layer_input[0]
    along_y = [[2 * m + n for m in range(NY)] for n in range(2)]
    along_z = [[i * NZ + j for j in range(NZ)] for i in range(NX)]
    across = [[device(i, j, m, n) for i in range(NX) for m in range(NY) for n in range(2)] for j in range(NZ)]

    def swap(a):
        return lax.ppermute(a, "ctx", [(i, i ^ 1) for i in range(SLOTS)])

    def earlier(a, d):
        return lax.ppermute(a, "ctx", [(i + 2 * d, i) for i in range(SLOTS - 2 * d)])

    def cols(a, start, width):
        return lax.dynamic_slice_in_dim(a, start, width, 1)

    def pick(a, i):
        return lax.dynamic_index_in_dim(a, i, 0, keepdims=False)

    at = (1 - c) * HALF * QW
    kv = lax.all_to_all(kv_sends(k, v), "ctx", 0, 0)
    q_par = swap(cols(q, at, HALF * QW))
    g_par = swap(cols(g, at, HALF * QW))
    x, _ = lax.optimization_barrier((x, kv))
    x_own = lax.all_to_all(x_sends(x), "dp", 0, 0, axis_index_groups=along_z)
    o_own, o_par, dv, stats = forward(place, parents, labels, q, q_par, g, g_par, kv)
    dv, x_own = lax.optimization_barrier((dv, x_own))
    dv = lax.all_to_all(dv.reshape(NY, 2, BLK, HALF * HD), "ctx", 0, 0, axis_index_groups=along_y)
    x_other = swap(x_own)
    o_swapped = swap(o_par)
    dq_own, dq_par, dk = backward(place, parents, labels, q, q_par, g, g_par, kv, stats)
    dv, dk = lax.optimization_barrier((dv, dk))
    dv_sends = sum_blocks(dv)
    dv_all = lax.all_to_all(dv_sends, "dp", 0, 0, axis_index_groups=along_z)
    dk = dk.reshape(NY, 2, BLK, HALF * HD)
    dk_sum = pick(dk, y).astype(F32)
    for d in range(1, NY):
        dk_sum = dk_sum + earlier(pick(dk, jnp.maximum(y - d, 0)), d).astype(F32)
    dk_sum = dk_sum.astype(LOW)
    partial = weight_partial(place, x_own, x_other, dv_all).reshape(2 * NX * NY, -1, HALF * HD)
    weight_grad = finish_weight(lax.all_to_all(partial, ("dp", "ctx"), 0, 0, axis_index_groups=across))
    out = lax.dynamic_update_slice_in_dim(o_own, o_swapped, at, 1)
    query_grad = lax.dynamic_update_slice_in_dim(dq_own, swap(dq_par), at, 1)
    both = jnp.stack([dk_sum, dv_sends[0]], axis=1)
    mine, other = pick(both, c), swap(pick(both, 1 - c))
    both = jnp.concatenate([jnp.where(c == 0, mine, other), jnp.where(c == 0, other, mine)], axis=-1)
    return out[None], query_grad[None], both[0][None], both[1][None], weight_grad


def solution(mesh):
    rows = P("dp", "ctx", None)
    return jax.shard_map(
        per_device,
        mesh=mesh,
        in_specs=(rows,) * 5 + (P("dp", None), P("dp", None)),
        out_specs=(rows,) * 4 + (P(("dp", "ctx"), None),),
        check_vma=False,
    )
```

time: 181 us -> 144 us (0.80)
  waiting for transfers between devices: 92.1 us -> 45.7 us
  starting transfers between devices: 40.9 us -> 47.6 us
  Pallas kernels: 34.5 us -> 37 us
    all_to_all x5 -> x4, waiting for transfers between devices: 71 us -> 18.4 us  [the longest x1 13.7 us: per_device(): lax.all_to_all(partial, ('dp', 'ctx'), 0, 0, axis_index_groups=across)]
    all_to_all x1, waiting for transfers between devices: 18.6 us -> 23.7 us  [per_device(): kv = lax.all_to_all(kv_sends(k, v), 'ctx', 0, 0)]
    ppermute x4 -> x6, starting transfers between devices: 0.88 us -> 5.87 us  [swap(): return lax.ppermute(a, 'ctx', [(i, i ^ 1) for i in range(SLOTS)])]
    ppermute x0 -> x3, starting transfers between devices: none -> 3.85 us  [earlier(): lax.ppermute(a, 'ctx', [(i + 2 * d, i) for i in range(SLOTS - 2 * d)])]
    ppermute x0 -> x3, waiting for transfers between devices: none -> 3.6 us  [earlier(): lax.ppermute(a, 'ctx', [(i + 2 * d, i) for i in range(SLOTS - 2 * d)])]
    dynamic_slice x2, local copies, waits for them, and re-layouts: 4.62 us -> 1.13 us  [cols(): return lax.dynamic_slice_in_dim(a, start, width, 1)]
    pallas_call x5, Pallas kernels: 29.6 us -> 32.1 us  [the longest x1 11.7 us: forward(): attention_call(forward_kernel, 'tree_forward', 3, [OWN, PARTNER, OWN, PAR...]
    ppermute x4 -> x6, waiting for transfers between devices: 2.56 us -> 0.02 us  [swap(): return lax.ppermute(a, 'ctx', [(i, i ^ 1) for i in range(SLOTS)])]
  transfers between devices with their start and end apart: 10 -> 14, of which waited for: 7 -> 7; matrix products, arithmetic and copies ran while one was open for 5% -> 6% of each run, Pallas kernels for 7% -> 22%
where the time goes in v1:
time: 144 us; the launch traced here: 143 us
  starting transfers between devices  47.6 us (33%)
  waiting for transfers between devices  45.7 us (32%)
  Pallas kernels  37 us (26%)
  local copies, waits for them, and re-layouts  10.8 us (8%)
    all_to_all x1, waiting for transfers between devices, per_device(): kv = lax.all_to_all(kv_sends(k, v), 'ctx', 0, 0)  23.7 us
    all_to_all x1, starting transfers between devices, per_device(): lax.all_to_all(partial, ('dp', 'ctx'), 0, 0, axis_index_groups=across)  15.9 us
    all_to_all x1, waiting for transfers between devices, per_device(): lax.all_to_all(partial, ('dp', 'ctx'), 0, 0, axis_index_groups=across)  13.7 us
    pallas_call x1, Pallas kernels, forward(): attention_call(forward_kernel, 'tree_forward', 3, [OWN, PARTNER, OWN, PAR...  11.7 us
    pallas_call x1, Pallas kernels, backward(): attention_call(backward_kernel, 'tree_backward', 4, [OWN, PARTNER, OWN, P...  10.3 us
    all_to_all x1, starting transfers between devices, per_device(): dv_all = lax.all_to_all(dv_sends, 'dp', 0, 0, axis_index_groups=along_z)  6.38 us
    all_to_all x1, starting transfers between devices, per_device(): kv = lax.all_to_all(kv_sends(k, v), 'ctx', 0, 0)  6.1 us
    ppermute x6, starting transfers between devices, swap(): return lax.ppermute(a, 'ctx', [(i, i ^ 1) for i in range(SLOTS)])  5.87 us
  transfers between devices with their start and end apart: 14, of which 7 were waited for; matrix products, arithmetic and copies ran while one was open for 6% of the time, Pallas kernels for 22%

profile of v1, /device:TPU:1, one launch (start us, length us, event | category | flops | bytes accessed | tf_op | source)
XLA Modules:
  0.0 143.1 jit_solution(771986497094751006)
XLA Ops:
  0.6 2.9 %kv_sends.1 = bf16[8,2,128,512]{3,2,1,0:T(8,128)(2,1)} custom-call(bf16[128,1024]{1,0:T(8,128)(2,1)} %bitcast.49, bf16[128,1024]{1,0:T(8,128)(2,1)} %bitcast.50), custom_call_target="tpu_custom_call" | custom-call | tf_op jit(solution)/shard_map/kv_sends/pallas_call | solution.py:347
  3.5 6.1 %all-to-all-start = ((bf16[8,2,128,512]{3,2,1,0:T(8,128)(2,1)}), bf16[8,2,128,512]{3,2,1,0:T(8,128)(2,1)}, u32[]{:S(2)}, u32[]{:S(2)}) async-start(bf16[8,2,128,512]{3,2,1,0:T(8,128)(2,1)} %kv_sends.1), calls=%async_computation | async-start | bytes 4194304 | tf_op jit(solution)/shard_map/all_to_all | solution.py:430
  9.8 1.4 copy-done.6
  12.3 23.7 %all-to-all-done.kv = bf16[8,2,128,512]{3,2,1,0:T(8,128)(2,1)} async-done(((bf16[8,2,128,512]{3,2,1,0:T(8,128)(2,1)}), bf16[8,2,128,512]{3,2,1,0:T(8,128)(2,1)}, u32[]{:S(2)}, u32[]{:S(2)}) %all-to-all-start) | async-done | bytes 2097184 | tf_op jit(solution)/shard_map/all_to_all | solution.py:430
  36.1 2.4 %x_sends.1 = bf16[4,128,1024]{2,1,0:T(8,128)(2,1)} custom-call(bf16[128,4096]{1,0:T(8,128)(2,1)} %bitcast.44), custom_call_target="tpu_custom_call" | custom-call | tf_op jit(solution)/shard_map/x_sends/pallas_call | solution.py:366
  38.4 5.0 %all-to-all-start.1 = ((bf16[4,128,1024]{2,1,0:T(8,128)(2,1)}), bf16[4,128,1024]{2,1,0:T(8,128)(2,1)}, u32[]{:S(2)}, u32[]{:S(2)}) async-start(bf16[4,128,1024]{2,1,0:T(8,128)(2,1)} %x_sends.1), calls=%async_computation.1 | async-start | bytes 2097152 | tf_op jit(solution)/shard_map/all_to_all | solution.py:434
  43.5 11.7 %tree_forward.1 = (bf16[128,8192]{1,0:T(8,128)(2,1)}, bf16[128,4096]{1,0:T(8,128)(2,1)}, bf16[8,128,512]{2,1,0:T(8,128)(2,1)}, f32[4,2,8,1024]{3,2,1,0:T(8,128)S(1)}) custom-call(s32[2]{0:T(128)S(1)} %pad_add_fusion.place, s32[1,8]{1,0:T(1,128)S(1)} %copy-done.1, s32[1,8]{1,0:T(1,128)S(1)} %copy-done.2, bf16[128,8192]{1,0:T(8,128)(2,1)} %bitcast.45, ...), custom_call_target="tpu_custom_call" | custom-call | flops 12884901888 | bytes 4194304 | tf_op jit(solution)/shard_map/tree_forward/pallas_call | solution.py:268
  57.5 4.4 %all-to-all-start.2 = ((bf16[4,2,128,512]{3,2,1,0:T(8,128)(2,1)}), bf16[4,2,128,512]{3,2,1,0:T(8,128)(2,1)}, u32[]{:S(2)}, u32[]{:S(2)}) async-start(bf16[4,2,128,512]{3,2,1,0:T(8,128)(2,1)} %bitcast.13), calls=%async_computation.2 | async-start | bytes 2097152 | tf_op jit(solution)/shard_map/all_to_all | solution.py:437
  62.0 10.3 %tree_backward.1 = (bf16[128,8192]{1,0:T(8,128)(2,1)}, bf16[128,4096]{1,0:T(8,128)(2,1)}, bf16[8,128,512]{2,1,0:T(8,128)(2,1)S(1)}) custom-call(s32[2]{0:T(128)S(1)} %pad_add_fusion.place, s32[1,8]{1,0:T(1,128)S(1)} %copy-done.1, s32[1,8]{1,0:T(1,128)S(1)} %copy-done.2, bf16[128,8192]{1,0:T(8,128)(2,1)} %bitcast.46, ...), custom_call_target="tpu_custom_call" | custom-call | flops 17179869184 | bytes 4194304 | tf_op jit(solution)/shard_map/tree_backward/pallas_call | solution.py:291
  72.2 2.1 %collective-permute-start.3 = (bf16[128,4096]{1,0:T(8,128)(2,1)}, bf16[128,4096]{1,0:T(8,128)(2,1)}, u32[]{:S(2)}, u32[]{:S(2)}) collective-permute-start(bf16[128,4096]{1,0:T(8,128)(2,1)} %get-tuple-element.21), channel_id=1, source_target_pairs={{0,1},{1,0},{2,3},{3,2},{4,5},{5,4},{6,7},{7,6},{8,9},{9,8},{10,11... | collective-permute-start | bytes 3145736 | tf_op jit(solution)/shard_map/ppermute | solution.py:418
  77.1 1.3 collective-permute-start.5
  78.4 2.3 %sum_blocks.1 = bf16[4,2,128,512]{3,2,1,0:T(8,128)(2,1)} custom-call(bf16[4,2,128,512]{3,2,1,0:T(8,128)(2,1)} %all-to-all-done.2.terms), custom_call_target="tpu_custom_call" | custom-call | tf_op jit(solution)/shard_map/sum_blocks/pallas_call | solution.py:383
  80.7 6.4 %all-to-all-start.3 = ((bf16[4,2,128,512]{3,2,1,0:T(8,128)(2,1)}), bf16[4,2,128,512]{3,2,1,0:T(8,128)(2,1)S(1)}, u32[]{:S(2)}, u32[]{:S(2)}) async-start(bf16[4,2,128,512]{3,2,1,0:T(8,128)(2,1)} %sum_blocks.1), calls=%async_computation.3 | async-start | bytes 2097152 | tf_op jit(solution)/shard_map/all_to_all | solution.py:443
  87.1 1.3 collective-permute-start.4
  88.4 2.3 %bitcast_dynamic-update-slice_fusion.1 = bf16[1,128,8192]{2,1,0:T(8,128)(2,1)} fusion(bf16[1,128,8192]{2,1,0:T(8,128)(2,1)} %bitcast.52, s32[]{:T(128)S(6)} %select_n.45, bf16[128,4096]{1,0:T(8,128)(2,1)} %collective-permute-done.2), kind=kLoop, calls=%fused_computation.1 | loop fusion | bytes 2097156 | tf_op jit(solution)/shard_map/dynamic_update_slice | solution.py:451
  91.6 2.0 %collective-permute-done.6 = bf16[2,128,512]{2,1,0:T(8,128)(2,1)S(1)} collective-permute-done((bf16[2,128,512]{2,1,0:T(8,128)(2,1)}, bf16[2,128,512]{2,1,0:T(8,128)(2,1)S(1)}, u32[]{:S(2)}, u32[]{:S(2)}) %collective-permute-start.6) | collective-permute-done | bytes 262176 | tf_op jit(solution)/shard_map/ppermute | solution.py:421
  93.6 1.6 %collective-permute-done.4 = bf16[2,128,512]{2,1,0:T(8,128)(2,1)S(1)} collective-permute-done((bf16[2,128,512]{2,1,0:T(8,128)(2,1)S(1)}, bf16[2,128,512]{2,1,0:T(8,128)(2,1)S(1)}, u32[]{:S(2)}, u32[]{:S(2)}) %collective-permute-start.4) | collective-permute-done | bytes 262176 | tf_op jit(solution)/shard_map/ppermute | solution.py:421
  95.4 2.5 %collective-permute-start.7 = (bf16[2,128,512]{2,1,0:T(8,128)(2,1)S(1)}, bf16[2,128,512]{2,1,0:T(8,128)(2,1)S(1)}, u32[]{:S(2)}, u32[]{:S(2)}) collective-permute-start(bf16[2,128,512]{2,1,0:T(8,128)(2,1)S(1)} %fusion.6), channel_id=1, source_target_pairs={{0,1},{1,0},{2,3},{3,2},{4,5},{5,4},{6,7},{7,6},{8,9},{9,8},{10,11... | collective-permute-start | bytes 786440 | tf_op jit(solution)/shard_map/ppermute | solution.py:418
  98.0 2.7 %all-to-all-done.3.dv = bf16[4,2,128,512]{3,2,1,0:T(8,128)(2,1)S(1)} async-done(((bf16[4,2,128,512]{3,2,1,0:T(8,128)(2,1)}), bf16[4,2,128,512]{3,2,1,0:T(8,128)(2,1)S(1)}, u32[]{:S(2)}, u32[]{:S(2)}) %all-to-all-start.3) | async-done | bytes 1048608 | tf_op jit(solution)/shard_map/all_to_all | solution.py:443
  101.7 5.5 %weight_partial.1 = bf16[1024,512]{1,0:T(8,128)(2,1)} custom-call(s32[2]{0:T(128)} %copy-done, bf16[4,128,1024]{2,1,0:T(8,128)(2,1)} %all-to-all-done.1.x_own, bf16[4,128,1024]{2,1,0:T(8,128)(2,1)} %collective-permute-done.8.x_other, bf16[4,2,128,512]{3,2,1,0:T(8,128)(2,1)} %copy-done.3), custom_call_target="tpu_custom_call" | custom-call | flops 1073741824 | bytes 3145728 | tf_op jit(solution)/shard_map/weight_partial/pallas_call | solution.py:321
  107.2 15.9 %all-to-all-start.4 = ((bf16[32,32,512]{2,1,0:T(8,128)(2,1)}), bf16[32,32,512]{2,1,0:T(8,128)(2,1)S(1)}, u32[]{:S(2)}, u32[]{:S(2)}) async-start(bf16[32,32,512]{2,1,0:T(8,128)(2,1)} %bitcast.43), calls=%async_computation.4 | async-start | bytes 2097152 | tf_op jit(solution)/shard_map/all_to_all | solution.py:450
  123.1 2.3 %bitcast_dynamic-update-slice_fusion = bf16[1,128,8192]{2,1,0:T(8,128)(2,1)} fusion(bf16[1,128,8192]{2,1,0:T(8,128)(2,1)} %bitcast.51, s32[]{:T(128)S(6)} %select_n.45, bf16[128,4096]{1,0:T(8,128)(2,1)} %collective-permute-done.3), kind=kLoop, calls=%fused_computation | loop fusion | bytes 2097156 | tf_op jit(solution)/shard_map/dynamic_update_slice | solution.py:452
  126.3 13.7 %all-to-all-done.4.parts = bf16[32,32,512]{2,1,0:T(8,128)(2,1)S(1)} async-done(((bf16[32,32,512]{2,1,0:T(8,128)(2,1)}), bf16[32,32,512]{2,1,0:T(8,128)(2,1)S(1)}, u32[]{:S(2)}, u32[]{:S(2)}) %all-to-all-start.4) | async-done | bytes 1048608 | tf_op jit(solution)/shard_map/all_to_all | solution.py:450
  141.0 2.0 %finish_weight.1 = f32[32,1024]{1,0:T(8,128)} custom-call(bf16[32,32,512]{2,1,0:T(8,128)(2,1)} %copy-done.4), custom_call_target="tpu_custom_call" | custom-call | tf_op jit(solution)/shard_map/finish_weight/pallas_call | solution.py:399
  (36 shorter events, 10.5 us)
Async XLA Ops:
  3.5 6.1 %copy-start.5 = (bf16[1,128,8192]{2,1,0:T(8,128)(2,1)S(1)}, bf16[1,128,8192]{2,1,0:T(8,128)(2,1)}, u32[]{:S(2)}) copy-start(bf16[1,128,8192]{2,1,0:T(8,128)(2,1)} %param.7) | copy-start | bytes 6291460
  3.5 32.5 %all-to-all-start = ((bf16[8,2,128,512]{3,2,1,0:T(8,128)(2,1)}), bf16[8,2,128,512]{3,2,1,0:T(8,128)(2,1)}, u32[]{:S(2)}, u32[]{:S(2)}) async-start(bf16[8,2,128,512]{3,2,1,0:T(8,128)(2,1)} %kv_sends.1), calls=%async_computation | async-start | bytes 4194304 | tf_op jit(solution)/shard_map/all_to_all | solution.py:430
  9.6 1.6 %copy-start.6 = (bf16[1,128,8192]{2,1,0:T(8,128)(2,1)S(1)}, bf16[1,128,8192]{2,1,0:T(8,128)(2,1)}, u32[]{:S(2)}) copy-start(bf16[1,128,8192]{2,1,0:T(8,128)(2,1)} %param.11) | copy-start | bytes 6291460
  9.7 33.7 %collective-permute-start = (bf16[128,4096]{1,0:T(8,128)(2,1)S(1)}, bf16[128,4096]{1,0:T(8,128)(2,1)S(1)}, u32[]{:S(2)}, u32[]{:S(2)}) collective-permute-start(bf16[128,4096]{1,0:T(8,128)(2,1)S(1)} %dynamic-slice_bitcast_fusion.1), channel_id=1, source_target_pairs={{0,1},{1,0},{2,3},{3,2},{4,5},{5,4},{6,7},{7,6},{8,9},{9,8},{10,11... | collective-permute-start | bytes 3145736 | tf_op jit(solution)/shard_map/ppermute | solution.py:418
  12.3 31.2 %collective-permute-start.1 = (bf16[128,4096]{1,0:T(8,128)(2,1)}, bf16[128,4096]{1,0:T(8,128)(2,1)S(1)}, u32[]{:S(2)}, u32[]{:S(2)}) collective-permute-start(bf16[128,4096]{1,0:T(8,128)(2,1)} %dynamic-slice_bitcast_fusion), channel_id=1, source_target_pairs={{0,1},{1,0},{2,3},{3,2},{4,5},{5,4},{6,7},{7,6},{8,9},{9,8},{10,11... | collective-permute-start | bytes 3145736 | tf_op jit(solution)/shard_map/ppermute | solution.py:418
  12.3 49.6 %copy-start = (s32[2]{0:T(128)}, s32[2]{0:T(128)S(1)}, u32[]{:S(2)}) copy-start(s32[2]{0:T(128)S(1)} %pad_add_fusion.place) | copy-start | bytes 28
  36.1 7.4 %copy-start.1 = (s32[1,8]{1,0:T(1,128)S(1)}, s32[1,8]{1,0:T(1,128)}, u32[]{:S(2)}) copy-start(s32[1,8]{1,0:T(1,128)} %parents.3) | copy-start | bytes 100
  36.1 7.4 %copy-start.2 = (s32[1,8]{1,0:T(1,128)S(1)}, s32[1,8]{1,0:T(1,128)}, u32[]{:S(2)}) copy-start(s32[1,8]{1,0:T(1,128)} %labels.3) | copy-start | bytes 100
  38.4 19.1 %all-to-all-start.1 = ((bf16[4,128,1024]{2,1,0:T(8,128)(2,1)}), bf16[4,128,1024]{2,1,0:T(8,128)(2,1)}, u32[]{:S(2)}, u32[]{:S(2)}) async-start(bf16[4,128,1024]{2,1,0:T(8,128)(2,1)} %x_sends.1), calls=%async_computation.1 | async-start | bytes 2097152 | tf_op jit(solution)/shard_map/all_to_all | solution.py:434
  55.1 31.9 %collective-permute-start.2 = (bf16[128,4096]{1,0:T(8,128)(2,1)}, bf16[128,4096]{1,0:T(8,128)(2,1)}, u32[]{:S(2)}, u32[]{:S(2)}) collective-permute-start(bf16[128,4096]{1,0:T(8,128)(2,1)} %get-tuple-element.18), channel_id=1, source_target_pairs={{0,1},{1,0},{2,3},{3,2},{4,5},{5,4},{6,7},{7,6},{8,9},{9,8},{10,11... | collective-permute-start | bytes 3145736 | tf_op jit(solution)/shard_map/ppermute | solution.py:418
  57.5 17.5 %all-to-all-start.2 = ((bf16[4,2,128,512]{3,2,1,0:T(8,128)(2,1)}), bf16[4,2,128,512]{3,2,1,0:T(8,128)(2,1)}, u32[]{:S(2)}, u32[]{:S(2)}) async-start(bf16[4,2,128,512]{3,2,1,0:T(8,128)(2,1)} %bitcast.13), calls=%async_computation.2 | async-start | bytes 2097152 | tf_op jit(solution)/shard_map/all_to_all | solution.py:437
  72.2 50.9 %collective-permute-start.3 = (bf16[128,4096]{1,0:T(8,128)(2,1)}, bf16[128,4096]{1,0:T(8,128)(2,1)}, u32[]{:S(2)}, u32[]{:S(2)}) collective-permute-start(bf16[128,4096]{1,0:T(8,128)(2,1)} %get-tuple-element.21), channel_id=1, source_target_pairs={{0,1},{1,0},{2,3},{3,2},{4,5},{5,4},{6,7},{7,6},{8,9},{9,8},{10,11... | collective-permute-start | bytes 3145736 | tf_op jit(solution)/shard_map/ppermute | solution.py:418
  74.3 23.6 %collective-permute-start.8 = (bf16[4,128,1024]{2,1,0:T(8,128)(2,1)}, bf16[4,128,1024]{2,1,0:T(8,128)(2,1)}, u32[]{:S(2)}, u32[]{:S(2)}) collective-permute-start(bf16[4,128,1024]{2,1,0:T(8,128)(2,1)} %all-to-all-done.1.x_own), channel_id=1, source_target_pairs={{0,1},{1,0},{2,3},{3,2},{4,5},{5,4},{6,7},{7,6},{8,9},{9,8},{10,11... | collective-permute-start | bytes 3145736 | tf_op jit(solution)/shard_map/ppermute | solution.py:418
  75.8 17.8 %collective-permute-start.6 = (bf16[2,128,512]{2,1,0:T(8,128)(2,1)}, bf16[2,128,512]{2,1,0:T(8,128)(2,1)S(1)}, u32[]{:S(2)}, u32[]{:S(2)}) collective-permute-start(bf16[2,128,512]{2,1,0:T(8,128)(2,1)} %get-tuple-element.30), channel_id=1, source_target_pairs={{6,0},{7,1},{14,8},{15,9},{22,16},{23,17},{30,24},{31,25},{38,32},... | collective-permute-start | bytes 786440 | tf_op jit(solution)/shard_map/ppermute | solution.py:421
  77.1 16.5 %collective-permute-start.5 = (bf16[2,128,512]{2,1,0:T(8,128)(2,1)S(1)}, bf16[2,128,512]{2,1,0:T(8,128)(2,1)S(1)}, u32[]{:S(2)}, u32[]{:S(2)}) collective-permute-start(bf16[2,128,512]{2,1,0:T(8,128)(2,1)S(1)} %get-tuple-element.31), channel_id=1, source_target_pairs={{4,0},{5,1},{6,2},{7,3},{12,8},{13,9},{14,10},{15,11},{20,16},{21,... | collective-permute-start | bytes 786440 | tf_op jit(solution)/shard_map/ppermute | solution.py:421
  80.7 20.0 %all-to-all-start.3 = ((bf16[4,2,128,512]{3,2,1,0:T(8,128)(2,1)}), bf16[4,2,128,512]{3,2,1,0:T(8,128)(2,1)S(1)}, u32[]{:S(2)}, u32[]{:S(2)}) async-start(bf16[4,2,128,512]{3,2,1,0:T(8,128)(2,1)} %sum_blocks.1), calls=%async_computation.3 | async-start | bytes 2097152 | tf_op jit(solution)/shard_map/all_to_all | solution.py:443
  87.1 8.2 %collective-permute-start.4 = (bf16[2,128,512]{2,1,0:T(8,128)(2,1)S(1)}, bf16[2,128,512]{2,1,0:T(8,128)(2,1)S(1)}, u32[]{:S(2)}, u32[]{:S(2)}) collective-permute-start(bf16[2,128,512]{2,1,0:T(8,128)(2,1)S(1)} %get-tuple-element.29), channel_id=1, source_target_pairs={{2,0},{3,1},{4,2},{5,3},{6,4},{7,5},{10,8},{11,9},{12,10},{13,11},... | collective-permute-start | bytes 786440 | tf_op jit(solution)/shard_map/ppermute | solution.py:421
  95.4 30.0 %collective-permute-start.7 = (bf16[2,128,512]{2,1,0:T(8,128)(2,1)S(1)}, bf16[2,128,512]{2,1,0:T(8,128)(2,1)S(1)}, u32[]{:S(2)}, u32[]{:S(2)}) collective-permute-start(bf16[2,128,512]{2,1,0:T(8,128)(2,1)S(1)} %fusion.6), channel_id=1, source_target_pairs={{0,1},{1,0},{2,3},{3,2},{4,5},{5,4},{6,7},{7,6},{8,9},{9,8},{10,11... | collective-permute-start | bytes 786440 | tf_op jit(solution)/shard_map/ppermute | solution.py:418
  100.7 1.0 copy-start.3
  107.2 32.8 %all-to-all-start.4 = ((bf16[32,32,512]{2,1,0:T(8,128)(2,1)}), bf16[32,32,512]{2,1,0:T(8,128)(2,1)S(1)}, u32[]{:S(2)}, u32[]{:S(2)}) async-start(bf16[32,32,512]{2,1,0:T(8,128)(2,1)} %bitcast.43), calls=%async_computation.4 | async-start | bytes 2097152 | tf_op jit(solution)/shard_map/all_to_all | solution.py:450
  140.0 1.0 copy-start.4

commit v2 on v1

--- a/solution.py
+++ b/solution.py
@@ -306,24 +306,27 @@
     )(*args)
 
 
-def weight_kernel(place, x_own, x_other, dv, out):
-    tokens = NZ * BLK
-    c = place[1]
-    own = dv[:, pl.ds(c, 1)].reshape(tokens, -1)
-    other = dv[:, pl.ds(1 - c, 1)].reshape(tokens, -1)
-    total = dot_tn(x_own[...].reshape(tokens, -1), own) + dot_tn(x_other[...].reshape(tokens, -1), other)
+def weight_kernel(place, *refs):
+    x_own, x_other, dv, out = refs[:NZ], refs[NZ : 2 * NZ], refs[-2], refs[-1]
+    c, z = place[1], place[2]
+    total = None
+    for d in range(NZ):
+        src = lax.rem(z + NZ - d, NZ)
+        x = jnp.concatenate([x_own[d][...], x_other[d][...]], axis=1)
+        term = dot_nn(x, jnp.concatenate([dv[src, c], dv[src, 1 - c]], axis=0))
+        total = term if total is None else total + term
     out[...] = total.astype(LOW)
 
 
 def weight_partial(place, x_own, x_other, dv):
-    tall, wide, step = x_own.shape[2], dv.shape[3], 256
-    x_spec = pl.BlockSpec((NZ, BLK, step), lambda i, place: (0, 0, i))
+    tall, wide, step = x_own[0].shape[0], dv.shape[3], 512
+    x_spec = pl.BlockSpec((step, BLK), lambda i, place: (i, 0))
     return pl.pallas_call(
         weight_kernel,
         grid_spec=pltpu.PrefetchScalarGridSpec(
             num_scalar_prefetch=1,
             grid=(tall // step,),
-            in_specs=[x_spec, x_spec, pl.BlockSpec((NZ, 2, BLK, wide), lambda i, place: (0, 0, 0, 0))],
+            in_specs=[x_spec] * (2 * NZ) + [pl.BlockSpec((NZ, 2, BLK, wide), lambda i, place: (0, 0, 0, 0))],
             out_specs=pl.BlockSpec((step, wide), lambda i, place: (i, 0)),
         ),
         out_shape=jax.ShapeDtypeStruct((tall, wide), LOW),
@@ -331,7 +334,7 @@
             flops=2 * NZ * 2 * BLK * tall * wide, bytes_accessed=NZ * 2 * BLK * (tall + wide) * 2, transcendentals=0
         ),
         name="weight_partial",
-    )(place, x_own, x_other, dv)
+    )(place, *x_own, *x_other, dv)
 
 
 def kv_kernel(k, v, out):
@@ -354,20 +357,28 @@
     )(k, v)
 
 
-def x_kernel(x, out):
+def x_kernel(place, x, *outs):
     piece = x.shape[1] // (NX * NZ)
-    for j in range(NZ):
+    for d in range(NZ):
+        to = lax.rem(place[2] + d, NZ)
         for i in range(NX):
-            at = (i * NZ + j) * piece
-            out[j, :, i * piece : (i + 1) * piece] = x[:, at : at + piece]
-
-
-def x_sends(x):
+            at = pl.multiple_of((i * NZ + to) * piece, piece)
+            outs[d][i * piece : (i + 1) * piece, :] = x[:, pl.ds(at, piece)].T
+
+
+def x_sends(place, x):
+    tall = x.shape[1] // NZ
     return pl.pallas_call(
         x_kernel,
-        out_shape=jax.ShapeDtypeStruct((NZ, BLK, x.shape[1] // NZ), LOW),
+        grid_spec=pltpu.PrefetchScalarGridSpec(
+            num_scalar_prefetch=1,
+            grid=(1,),
+            in_specs=[pl.BlockSpec(x.shape, lambda i, place: (0, 0))],
+            out_specs=[pl.BlockSpec((tall, BLK), lambda i, place: (0, 0))] * NZ,
+        ),
+        out_shape=[jax.ShapeDtypeStruct((tall, BLK), LOW)] * NZ,
         name="x_sends",
-    )(x)
+    )(place, x)
 
 
 def sum_kernel(terms, out):
@@ -407,8 +418,8 @@
 
 def per_device(query_rows, key_rows, value_rows, layer_input, out_grad, parents, labels):
     ctx = lax.axis_index("ctx")
-    y, c = ctx // 2, ctx % 2
-    place = jnp.stack([y, c]).astype(jnp.int32)
+    y, c, z = ctx // 2, ctx % 2, lax.axis_index("dp") % NZ
+    place = jnp.stack([y, c, z]).astype(jnp.int32)
     q, k, v, g, x = query_rows[0], key_rows[0], value_rows[0], out_grad[0], layer_input[0]
     along_y = [[2 * m + n for m in range(NY)] for n in range(2)]
     along_z = [[i * NZ + j for j in range(NZ)] for i in range(NX)]
@@ -417,35 +428,33 @@
     def swap(a):
         return lax.ppermute(a, "ctx", [(i, i ^ 1) for i in range(SLOTS)])
 
-    def earlier(a, d):
-        return lax.ppermute(a, "ctx", [(i + 2 * d, i) for i in range(SLOTS - 2 * d)])
-
     def cols(a, start, width):
         return lax.dynamic_slice_in_dim(a, start, width, 1)
 
     def pick(a, i):
         return lax.dynamic_index_in_dim(a, i, 0, keepdims=False)
+
+    def further(a, d):
+        return lax.ppermute(a, "dp", [(i, i // NZ * NZ + (i + d) % NZ) for i in range(NX * NZ)])
 
     at = (1 - c) * HALF * QW
     kv = lax.all_to_all(kv_sends(k, v), "ctx", 0, 0)
     q_par = swap(cols(q, at, HALF * QW))
     g_par = swap(cols(g, at, HALF * QW))
-    x, _ = lax.optimization_barrier((x, kv))
-    x_own = lax.all_to_all(x_sends(x), "dp", 0, 0, axis_index_groups=along_z)
+    x_own = x_sends(place, x)
+    x_own = [x_own[0]] + [further(x_own[d], d) for d in range(1, NZ)]
+    x_other = [swap(a) for a in x_own]
+    kv, x_own, x_other = lax.optimization_barrier((kv, x_own, x_other))
     o_own, o_par, dv, stats = forward(place, parents, labels, q, q_par, g, g_par, kv)
-    dv, x_own = lax.optimization_barrier((dv, x_own))
     dv = lax.all_to_all(dv.reshape(NY, 2, BLK, HALF * HD), "ctx", 0, 0, axis_index_groups=along_y)
-    x_other = swap(x_own)
     o_swapped = swap(o_par)
     dq_own, dq_par, dk = backward(place, parents, labels, q, q_par, g, g_par, kv, stats)
     dv, dk = lax.optimization_barrier((dv, dk))
     dv_sends = sum_blocks(dv)
+    dv_sends, dk, dq_par = lax.optimization_barrier((dv_sends, dk, dq_par))
     dv_all = lax.all_to_all(dv_sends, "dp", 0, 0, axis_index_groups=along_z)
     dk = dk.reshape(NY, 2, BLK, HALF * HD)
-    dk_sum = pick(dk, y).astype(F32)
-    for d in range(1, NY):
-        dk_sum = dk_sum + earlier(pick(dk, jnp.maximum(y - d, 0)), d).astype(F32)
-    dk_sum = dk_sum.astype(LOW)
+    dk_sum = lax.psum_scatter(dk, "ctx", scatter_dimension=0, axis_index_groups=along_y)
     partial = weight_partial(place, x_own, x_other, dv_all).reshape(2 * NX * NY, -1, HALF * HD)
     weight_grad = finish_weight(lax.all_to_all(partial, ("dp", "ctx"), 0, 0, axis_index_groups=across))
     out = lax.dynamic_update_slice_in_dim(o_own, o_swapped, at, 1)

time: 144 us -> 149 us (1.035); the launches traced: 143 us -> 146 us
  between operations: 0.76 us -> 14.2 us
  starting transfers between devices: 47.6 us -> 39.7 us
  waiting for transfers between devices: 45.7 us -> 40.7 us
    all_to_all x1, waiting for transfers between devices: 23.7 us -> 0.01 us  [per_device(): kv = lax.all_to_all(kv_sends(k, v), 'ctx', 0, 0)]
    all_to_all x1, waiting for transfers between devices: 2.73 us -> 11.6 us  [per_device(): dv_all = lax.all_to_all(dv_sends, 'dp', 0, 0, axis_index_groups=along_z)]
    ppermute x3, waiting for transfers between devices: 3.6 us -> 10.2 us  [further(): lax.ppermute(a, 'dp', [(i, i // NZ * NZ + (i + d) % NZ) for i in range(NX...]
    all_to_all x1, starting transfers between devices: 15.9 us -> 10.5 us  [per_device(): lax.all_to_all(partial, ('dp', 'ctx'), 0, 0, axis_index_groups=across)]
    all_to_all x1 -> x0, starting transfers between devices: 5.03 us -> none  [per_device(): x_own = lax.all_to_all(x_sends(x), 'dp', 0, 0, axis_index_groups=along_z)]
    all_to_all x1, waiting for transfers between devices: 0.71 us -> 4.56 us  [per_device(): lax.all_to_all(dv.reshape(NY, 2, BLK, HALF * HD), 'ctx', 0, 0, axis_index...]
    all_to_all x1, starting transfers between devices: 4.43 us -> 7.87 us  [per_device(): lax.all_to_all(dv.reshape(NY, 2, BLK, HALF * HD), 'ctx', 0, 0, axis_index...]
    ppermute x3, starting transfers between devices: 3.85 us -> 5.67 us  [further(): lax.ppermute(a, 'dp', [(i, i // NZ * NZ + (i + d) % NZ) for i in range(NX...]
  transfers between devices with their start and end apart: 14 -> 17, of which waited for: 7 -> 7; matrix products, arithmetic and copies ran while one was open for 6% -> 6% of each run, Pallas kernels for 22% -> 15%
where the time goes in v2:
time: 149 us; the launch traced here: 146 us
  waiting for transfers between devices  40.7 us (27%)
  starting transfers between devices  39.7 us (27%)
  Pallas kernels  37 us (25%)
  between operations  14.2 us (10%)
  local copies, waits for them, and re-layouts  11.8 us (8%)
  other arithmetic  2.53 us (2%)
    all_to_all x1, waiting for transfers between devices, per_device(): lax.all_to_all(partial, ('dp', 'ctx'), 0, 0, axis_index_groups=across)  13.3 us
    all_to_all x1, waiting for transfers between devices, per_device(): dv_all = lax.all_to_all(dv_sends, 'dp', 0, 0, axis_index_groups=along_z)  11.6 us
    pallas_call x1, Pallas kernels, forward(): attention_call(forward_kernel, 'tree_forward', 3, [OWN, PARTNER, OWN, PAR...  11.6 us
    all_to_all x1, starting transfers between devices, per_device(): lax.all_to_all(partial, ('dp', 'ctx'), 0, 0, axis_index_groups=across)  10.5 us
    pallas_call x1, Pallas kernels, backward(): attention_call(backward_kernel, 'tree_backward', 4, [OWN, PARTNER, OWN, P...  10.3 us
    ppermute x3, waiting for transfers between devices, further(): lax.ppermute(a, 'dp', [(i, i // NZ * NZ + (i + d) % NZ) for i in range(NX...  10.2 us
    all_to_all x1, starting transfers between devices, per_device(): lax.all_to_all(dv.reshape(NY, 2, BLK, HALF * HD), 'ctx', 0, 0, axis_index...  7.87 us
    all_to_all x1, starting transfers between devices, per_device(): kv = lax.all_to_all(kv_sends(k, v), 'ctx', 0, 0)  6.1 us
  transfers between devices with their start and end apart: 17, of which 7 were waited for; matrix products, arithmetic and copies ran while one was open for 6% of the time, Pallas kernels for 15%

profile of v2, /device:TPU:1, one launch (start us, length us, event | category | flops | bytes accessed | tf_op | source)
XLA Modules:
  0.0 145.9 jit_solution(10226216647286303474)
XLA Ops:
  7.2 2.9 %kv_sends.1 = bf16[8,2,128,512]{3,2,1,0:T(8,128)(2,1)} custom-call(bf16[128,1024]{1,0:T(8,128)(2,1)} %bitcast.40, bf16[128,1024]{1,0:T(8,128)(2,1)} %bitcast.41), custom_call_target="tpu_custom_call" | custom-call | tf_op jit(solution)/shard_map/kv_sends/pallas_call | solution.py:350
  10.1 6.1 %all-to-all-start = ((bf16[8,2,128,512]{3,2,1,0:T(8,128)(2,1)}), bf16[8,2,128,512]{3,2,1,0:T(8,128)(2,1)}, u32[]{:S(2)}, u32[]{:S(2)}) async-start(bf16[8,2,128,512]{3,2,1,0:T(8,128)(2,1)} %kv_sends.1), calls=%async_computation | async-start | bytes 4194304 | tf_op jit(solution)/shard_map/all_to_all | solution.py:441
  16.4 1.4 copy-done.8
  17.7 1.0 dynamic-slice_bitcast_fusion
  19.4 3.0 %x_sends.1 = (bf16[1024,128]{1,0:T(8,128)(2,1)}, bf16[1024,128]{1,0:T(8,128)(2,1)}, bf16[1024,128]{1,0:T(8,128)(2,1)}, bf16[1024,128]{1,0:T(8,128)(2,1)}) custom-call(s32[3]{0:T(128)} %pad_add_fusion.place, bf16[128,4096]{1,0:T(8,128)(2,1)} %bitcast.33), custom_call_target="tpu_custom_call" | custom-call | tf_op jit(solution)/shard_map/x_sends/pallas_call | solution.py:371
  22.5 1.6 %collective-permute-start.2 = (bf16[1024,128]{1,0:T(8,128)(2,1)}, bf16[1024,128]{1,0:T(8,128)(2,1)S(1)}, u32[]{:S(2)}, u32[]{:S(2)}) collective-permute-start(bf16[1024,128]{1,0:T(8,128)(2,1)} %get-tuple-element.31), channel_id=1, source_target_pairs={{0,8},{8,16},{16,24},{24,0},{32,40},{40,48},{48,56},{56,32},{64,72... | collective-permute-start | bytes 786440 | tf_op jit(solution)/shard_map/ppermute | solution.py:438
  24.1 3.3 %collective-permute-start.3 = (bf16[1024,128]{1,0:T(8,128)(2,1)}, bf16[1024,128]{1,0:T(8,128)(2,1)S(1)}, u32[]{:S(2)}, u32[]{:S(2)}) collective-permute-start(bf16[1024,128]{1,0:T(8,128)(2,1)} %get-tuple-element.32), channel_id=1, source_target_pairs={{0,16},{8,24},{16,0},{24,8},{32,48},{40,56},{48,32},{56,40},{64,80... | collective-permute-start | bytes 786440 | tf_op jit(solution)/shard_map/ppermute | solution.py:438
  28.1 4.6 %collective-permute-done.2.refs_1_ = bf16[1024,128]{1,0:T(8,128)(2,1)S(1)} collective-permute-done((bf16[1024,128]{1,0:T(8,128)(2,1)}, bf16[1024,128]{1,0:T(8,128)(2,1)S(1)}, u32[]{:S(2)}, u32[]{:S(2)}) %collective-permute-start.2) | collective-permute-done | bytes 262176 | tf_op jit(solution)/shard_map/ppermute | solution.py:438
  33.7 5.6 %collective-permute-done.3.refs_2_ = bf16[1024,128]{1,0:T(8,128)(2,1)S(1)} collective-permute-done((bf16[1024,128]{1,0:T(8,128)(2,1)}, bf16[1024,128]{1,0:T(8,128)(2,1)S(1)}, u32[]{:S(2)}, u32[]{:S(2)}) %collective-permute-start.3) | collective-permute-done | bytes 262176 | tf_op jit(solution)/shard_map/ppermute | solution.py:438
  39.3 1.2 collective-permute-start.6
  43.8 11.6 %tree_forward.1 = (bf16[128,8192]{1,0:T(8,128)(2,1)}, bf16[128,4096]{1,0:T(8,128)(2,1)}, bf16[8,128,512]{2,1,0:T(8,128)(2,1)}, f32[4,2,8,1024]{3,2,1,0:T(8,128)S(1)}) custom-call(s32[3]{0:T(128)S(1)} %copy-done, s32[1,8]{1,0:T(1,128)S(1)} %copy-done.2, s32[1,8]{1,0:T(1,128)S(1)} %copy-done.3, bf16[128,8192]{1,0:T(8,128)(2,1)} %bitcast.36, ...), custom_call_target="tpu_custom_call" | custom-call | flops 12884901888 | bytes 4194304 | tf_op jit(solution)/shard_map/tree_forward/pallas_call | solution.py:268
  55.8 7.9 %all-to-all-start.1 = ((bf16[4,2,128,512]{3,2,1,0:T(8,128)(2,1)}), bf16[4,2,128,512]{3,2,1,0:T(8,128)(2,1)}, u32[]{:S(2)}, u32[]{:S(2)}) async-start(bf16[4,2,128,512]{3,2,1,0:T(8,128)(2,1)} %bitcast.13), calls=%async_computation.1 | async-start | bytes 2097152 | tf_op jit(solution)/shard_map/all_to_all | solution.py:449
  63.7 10.3 %tree_backward.1 = (bf16[128,8192]{1,0:T(8,128)(2,1)}, bf16[128,4096]{1,0:T(8,128)(2,1)S(1)}, bf16[8,128,512]{2,1,0:T(8,128)(2,1)}) custom-call(s32[3]{0:T(128)S(1)} %copy-done.1, s32[1,8]{1,0:T(1,128)S(1)} %copy-done.2, s32[1,8]{1,0:T(1,128)S(1)} %copy-done.3, bf16[128,8192]{1,0:T(8,128)(2,1)} %bitcast.37, ...), custom_call_target="tpu_custom_call" | custom-call | flops 17179869184 | bytes 4194304 | tf_op jit(solution)/shard_map/tree_backward/pallas_call | solution.py:291
  74.0 4.6 %all-to-all-done.1.terms = bf16[4,2,128,512]{3,2,1,0:T(8,128)(2,1)} async-done(((bf16[4,2,128,512]{3,2,1,0:T(8,128)(2,1)}), bf16[4,2,128,512]{3,2,1,0:T(8,128)(2,1)}, u32[]{:S(2)}, u32[]{:S(2)}) %all-to-all-start.1) | async-done | bytes 1048608 | tf_op jit(solution)/shard_map/all_to_all | solution.py:449
  78.5 2.3 %sum_blocks.1 = bf16[4,2,128,512]{3,2,1,0:T(8,128)(2,1)} custom-call(bf16[4,2,128,512]{3,2,1,0:T(8,128)(2,1)} %all-to-all-done.1.terms), custom_call_target="tpu_custom_call" | custom-call | tf_op jit(solution)/shard_map/sum_blocks/pallas_call | solution.py:394
  80.9 1.4 collective-permute-start.10
  82.3 4.8 %all-to-all-start.2 = ((bf16[4,2,128,512]{3,2,1,0:T(8,128)(2,1)}), bf16[4,2,128,512]{3,2,1,0:T(8,128)(2,1)S(1)}, u32[]{:S(2)}, u32[]{:S(2)}) async-start(bf16[4,2,128,512]{3,2,1,0:T(8,128)(2,1)} %sum_blocks.1), calls=%async_computation.3 | async-start | bytes 2097152 | tf_op jit(solution)/shard_map/all_to_all | solution.py:455
  88.0 2.3 %bitcast_dynamic-update-slice_fusion.1 = bf16[1,128,8192]{2,1,0:T(8,128)(2,1)} fusion(bf16[1,128,8192]{2,1,0:T(8,128)(2,1)} %bitcast.43, s32[]{:T(128)S(6)} %select_n.43, bf16[128,4096]{1,0:T(8,128)(2,1)} %collective-permute-done.9), kind=kLoop, calls=%fused_computation.1 | loop fusion | bytes 2097156 | tf_op jit(solution)/shard_map/dynamic_update_slice | solution.py:460
  90.3 11.6 %all-to-all-done.2.refs_8_ = bf16[4,2,128,512]{3,2,1,0:T(8,128)(2,1)S(1)} async-done(((bf16[4,2,128,512]{3,2,1,0:T(8,128)(2,1)}), bf16[4,2,128,512]{3,2,1,0:T(8,128)(2,1)S(1)}, u32[]{:S(2)}, u32[]{:S(2)}) %all-to-all-start.2) | async-done | bytes 1048608 | tf_op jit(solution)/shard_map/all_to_all | solution.py:455
  103.0 4.8 %weight_partial.1 = bf16[1024,512]{1,0:T(8,128)(2,1)} custom-call(s32[3]{0:T(128)} %pad_add_fusion.place, bf16[1024,128]{1,0:T(8,128)(2,1)} %get-tuple-element.47.refs_0_, bf16[1024,128]{1,0:T(8,128)(2,1)} %copy-done.9, bf16[1024,128]{1,0:T(8,128)(2,1)} %copy-done.10, bf16[1024,128]{1,0:T(8,128)(2,1)} %copy-done.11, bf16[1024,128]{1,0:T(8,128)(2,1)} %copy-done.12, ...), custom_call_target="tpu_custom_call" | custom-call | flops 1073741824 | bytes 3145728 | tf_op jit(solution)/shard_map/weight_partial/pallas_call | solution.py:324
  107.8 10.5 %all-to-all-start.3 = ((bf16[32,32,512]{2,1,0:T(8,128)(2,1)}), bf16[32,32,512]{2,1,0:T(8,128)(2,1)S(1)}, u32[]{:S(2)}, u32[]{:S(2)}) async-start(bf16[32,32,512]{2,1,0:T(8,128)(2,1)} %bitcast.32), calls=%async_computation.4 | async-start | bytes 2097152 | tf_op jit(solution)/shard_map/all_to_all | solution.py:459
  119.6 2.3 %bitcast_dynamic-update-slice_fusion = bf16[1,128,8192]{2,1,0:T(8,128)(2,1)} fusion(bf16[1,128,8192]{2,1,0:T(8,128)(2,1)} %bitcast.42, s32[]{:T(128)S(6)} %select_n.43, bf16[128,4096]{1,0:T(8,128)(2,1)} %collective-permute-done.10), kind=kLoop, calls=%fused_computation | loop fusion | bytes 2097156 | tf_op jit(solution)/shard_map/dynamic_update_slice | solution.py:461
  121.9 13.3 %all-to-all-done.3.parts = bf16[32,32,512]{2,1,0:T(8,128)(2,1)S(1)} async-done(((bf16[32,32,512]{2,1,0:T(8,128)(2,1)}), bf16[32,32,512]{2,1,0:T(8,128)(2,1)S(1)}, u32[]{:S(2)}, u32[]{:S(2)}) %all-to-all-start.3) | async-done | bytes 1048608 | tf_op jit(solution)/shard_map/all_to_all | solution.py:459
  136.1 2.0 %finish_weight.1 = f32[32,1024]{1,0:T(8,128)} custom-call(bf16[32,32,512]{2,1,0:T(8,128)(2,1)} %copy-done.5), custom_call_target="tpu_custom_call" | custom-call | tf_op jit(solution)/shard_map/finish_weight/pallas_call | solution.py:410
  (57 shorter events, 11.3 us)
Async XLA Ops:
  10.0 6.1 %copy-start.7 = (bf16[1,128,8192]{2,1,0:T(8,128)(2,1)S(1)}, bf16[1,128,8192]{2,1,0:T(8,128)(2,1)}, u32[]{:S(2)}) copy-start(bf16[1,128,8192]{2,1,0:T(8,128)(2,1)} %param.7) | copy-start | bytes 6291460
  10.1 33.1 %all-to-all-start = ((bf16[8,2,128,512]{3,2,1,0:T(8,128)(2,1)}), bf16[8,2,128,512]{3,2,1,0:T(8,128)(2,1)}, u32[]{:S(2)}, u32[]{:S(2)}) async-start(bf16[8,2,128,512]{3,2,1,0:T(8,128)(2,1)} %kv_sends.1), calls=%async_computation | async-start | bytes 4194304 | tf_op jit(solution)/shard_map/all_to_all | solution.py:441
  16.2 26.9 %copy-start.2 = (s32[1,8]{1,0:T(1,128)S(1)}, s32[1,8]{1,0:T(1,128)}, u32[]{:S(2)}) copy-start(s32[1,8]{1,0:T(1,128)} %parents.3) | copy-start | bytes 100
  16.2 26.9 %copy-start.3 = (s32[1,8]{1,0:T(1,128)S(1)}, s32[1,8]{1,0:T(1,128)}, u32[]{:S(2)}) copy-start(s32[1,8]{1,0:T(1,128)} %labels.3) | copy-start | bytes 100
  16.3 26.9 %collective-permute-start = (bf16[128,4096]{1,0:T(8,128)(2,1)S(1)}, bf16[128,4096]{1,0:T(8,128)(2,1)S(1)}, u32[]{:S(2)}, u32[]{:S(2)}) collective-permute-start(bf16[128,4096]{1,0:T(8,128)(2,1)S(1)} %dynamic-slice_bitcast_fusion.1), channel_id=1, source_target_pairs={{0,1},{1,0},{2,3},{3,2},{4,5},{5,4},{6,7},{7,6},{8,9},{9,8},{10,11... | collective-permute-start | bytes 3145736 | tf_op jit(solution)/shard_map/ppermute | solution.py:429
  18.8 24.3 %collective-permute-start.1 = (bf16[128,4096]{1,0:T(8,128)(2,1)}, bf16[128,4096]{1,0:T(8,128)(2,1)S(1)}, u32[]{:S(2)}, u32[]{:S(2)}) collective-permute-start(bf16[128,4096]{1,0:T(8,128)(2,1)} %dynamic-slice_bitcast_fusion), channel_id=1, source_target_pairs={{0,1},{1,0},{2,3},{3,2},{4,5},{5,4},{6,7},{7,6},{8,9},{9,8},{10,11... | collective-permute-start | bytes 3145736 | tf_op jit(solution)/shard_map/ppermute | solution.py:429
  22.5 10.3 %collective-permute-start.2 = (bf16[1024,128]{1,0:T(8,128)(2,1)}, bf16[1024,128]{1,0:T(8,128)(2,1)S(1)}, u32[]{:S(2)}, u32[]{:S(2)}) collective-permute-start(bf16[1024,128]{1,0:T(8,128)(2,1)} %get-tuple-element.31), channel_id=1, source_target_pairs={{0,8},{8,16},{16,24},{24,0},{32,40},{40,48},{48,56},{56,32},{64,72... | collective-permute-start | bytes 786440 | tf_op jit(solution)/shard_map/ppermute | solution.py:438
  24.1 15.1 %collective-permute-start.3 = (bf16[1024,128]{1,0:T(8,128)(2,1)}, bf16[1024,128]{1,0:T(8,128)(2,1)S(1)}, u32[]{:S(2)}, u32[]{:S(2)}) collective-permute-start(bf16[1024,128]{1,0:T(8,128)(2,1)} %get-tuple-element.32), channel_id=1, source_target_pairs={{0,16},{8,24},{16,0},{24,8},{32,48},{40,56},{48,32},{56,40},{64,80... | collective-permute-start | bytes 786440 | tf_op jit(solution)/shard_map/ppermute | solution.py:438
  27.4 13.1 %collective-permute-start.4 = (bf16[1024,128]{1,0:T(8,128)(2,1)}, bf16[1024,128]{1,0:T(8,128)(2,1)S(1)}, u32[]{:S(2)}, u32[]{:S(2)}) collective-permute-start(bf16[1024,128]{1,0:T(8,128)(2,1)} %get-tuple-element.33), channel_id=1, source_target_pairs={{0,24},{8,0},{16,8},{24,16},{32,56},{40,32},{48,40},{56,48},{64,88... | collective-permute-start | bytes 786440 | tf_op jit(solution)/shard_map/ppermute | solution.py:438
  32.8 6.5 %copy-start.9 = (bf16[1024,128]{1,0:T(8,128)(2,1)}, bf16[1024,128]{1,0:T(8,128)(2,1)S(1)}, u32[]{:S(2)}) copy-start(bf16[1024,128]{1,0:T(8,128)(2,1)S(1)} %collective-permute-done.2.refs_1_) | copy-start | bytes 786436
  32.8 7.8 %collective-permute-start.5 = (bf16[1024,128]{1,0:T(8,128)(2,1)}, bf16[1024,128]{1,0:T(8,128)(2,1)S(1)}, u32[]{:S(2)}, u32[]{:S(2)}) collective-permute-start(bf16[1024,128]{1,0:T(8,128)(2,1)} %get-tuple-element.47.refs_0_), channel_id=1, source_target_pairs={{0,1},{1,0},{2,3},{3,2},{4,5},{5,4},{6,7},{7,6},{8,9},{9,8},{10,11... | collective-permute-start | bytes 786440 | tf_op jit(solution)/shard_map/ppermute | solution.py:429
  39.3 2.4 %copy-start.10 = (bf16[1024,128]{1,0:T(8,128)(2,1)}, bf16[1024,128]{1,0:T(8,128)(2,1)S(1)}, u32[]{:S(2)}) copy-start(bf16[1024,128]{1,0:T(8,128)(2,1)S(1)} %collective-permute-done.3.refs_2_) | copy-start | bytes 786436
  39.3 2.4 %collective-permute-start.6 = (bf16[1024,128]{1,0:T(8,128)(2,1)S(1)}, bf16[1024,128]{1,0:T(8,128)(2,1)S(1)}, u32[]{:S(2)}, u32[]{:S(2)}) collective-permute-start(bf16[1024,128]{1,0:T(8,128)(2,1)S(1)} %collective-permute-done.2.refs_1_), channel_id=1, source_target_pairs={{0,1},{1,0},{2,3},{3,2},{4,5},{5,4},{6,7},{7,6},{8,9},{9,8},{10,11... | collective-permute-start | bytes 786440 | tf_op jit(solution)/shard_map/ppermute | solution.py:429
  40.5 1.5 %collective-permute-start.7 = (bf16[1024,128]{1,0:T(8,128)(2,1)S(1)}, bf16[1024,128]{1,0:T(8,128)(2,1)S(1)}, u32[]{:S(2)}, u32[]{:S(2)}) collective-permute-start(bf16[1024,128]{1,0:T(8,128)(2,1)S(1)} %collective-permute-done.3.refs_2_), channel_id=1, source_target_pairs={{0,1},{1,0},{2,3},{3,2},{4,5},{5,4},{6,7},{7,6},{8,9},{9,8},{10,11... | collective-permute-start | bytes 786440 | tf_op jit(solution)/shard_map/ppermute | solution.py:429
  40.6 2.5 %collective-permute-start.8 = (bf16[1024,128]{1,0:T(8,128)(2,1)S(1)}, bf16[1024,128]{1,0:T(8,128)(2,1)}, u32[]{:S(2)}, u32[]{:S(2)}) collective-permute-start(bf16[1024,128]{1,0:T(8,128)(2,1)S(1)} %collective-permute-done.4.refs_3_), channel_id=1, source_target_pairs={{0,1},{1,0},{2,3},{3,2},{4,5},{5,4},{6,7},{7,6},{8,9},{9,8},{10,11... | collective-permute-start | bytes 786440 | tf_op jit(solution)/shard_map/ppermute | solution.py:429
  55.4 8.2 %copy-start.1 = (s32[3]{0:T(128)S(1)}, s32[3]{0:T(128)}, u32[]{:S(2)}) copy-start(s32[3]{0:T(128)} %pad_add_fusion.place) | copy-start | bytes 40
  55.4 32.6 %collective-permute-start.9 = (bf16[128,4096]{1,0:T(8,128)(2,1)}, bf16[128,4096]{1,0:T(8,128)(2,1)}, u32[]{:S(2)}, u32[]{:S(2)}) collective-permute-start(bf16[128,4096]{1,0:T(8,128)(2,1)} %get-tuple-element.36), channel_id=1, source_target_pairs={{0,1},{1,0},{2,3},{3,2},{4,5},{5,4},{6,7},{7,6},{8,9},{9,8},{10,11... | collective-permute-start | bytes 3145736 | tf_op jit(solution)/shard_map/ppermute | solution.py:429
  55.8 22.7 %all-to-all-start.1 = ((bf16[4,2,128,512]{3,2,1,0:T(8,128)(2,1)}), bf16[4,2,128,512]{3,2,1,0:T(8,128)(2,1)}, u32[]{:S(2)}, u32[]{:S(2)}) async-start(bf16[4,2,128,512]{3,2,1,0:T(8,128)(2,1)} %bitcast.13), calls=%async_computation.1 | async-start | bytes 2097152 | tf_op jit(solution)/shard_map/all_to_all | solution.py:449
  63.7 54.6 %reduce-scatter.2.cloned.1.call-start = ((), (), s32[]{:S(2)}) async-start(), calls=%async_computation.5 | async-start | bytes 1310720 | tf_op jit(solution)/shard_map/reduce_scatter | solution.py:457
  80.9 38.7 %collective-permute-start.10 = (bf16[128,4096]{1,0:T(8,128)(2,1)S(1)}, bf16[128,4096]{1,0:T(8,128)(2,1)}, u32[]{:S(2)}, u32[]{:S(2)}) collective-permute-start(bf16[128,4096]{1,0:T(8,128)(2,1)S(1)} %get-tuple-element.44), channel_id=1, source_target_pairs={{0,1},{1,0},{2,3},{3,2},{4,5},{5,4},{6,7},{7,6},{8,9},{9,8},{10,11... | collective-permute-start | bytes 3145736 | tf_op jit(solution)/shard_map/ppermute | solution.py:429
  82.3 19.7 %all-to-all-start.2 = ((bf16[4,2,128,512]{3,2,1,0:T(8,128)(2,1)}), bf16[4,2,128,512]{3,2,1,0:T(8,128)(2,1)S(1)}, u32[]{:S(2)}, u32[]{:S(2)}) async-start(bf16[4,2,128,512]{3,2,1,0:T(8,128)(2,1)} %sum_blocks.1), calls=%async_computation.3 | async-start | bytes 2097152 | tf_op jit(solution)/shard_map/all_to_all | solution.py:455
  107.8 27.4 %all-to-all-start.3 = ((bf16[32,32,512]{2,1,0:T(8,128)(2,1)}), bf16[32,32,512]{2,1,0:T(8,128)(2,1)S(1)}, u32[]{:S(2)}, u32[]{:S(2)}) async-start(bf16[32,32,512]{2,1,0:T(8,128)(2,1)} %bitcast.32), calls=%async_computation.4 | async-start | bytes 2097152 | tf_op jit(solution)/shard_map/all_to_all | solution.py:459
  118.3 19.9 %copy-start.6 = (bf16[1,2,128,512]{3,2,1,0:T(8,128)(2,1)S(1)}, bf16[1,2,128,512]{3,2,1,0:T(8,128)(2,1)}, u32[]{:S(2)}) copy-start(bf16[1,2,128,512]{3,2,1,0:T(8,128)(2,1)} %reduce-scatter.2.cloned.1.call-done) | copy-start | bytes 786436
  119.3 18.9 %collective-permute-start.11 = (bf16[2,128,512]{2,1,0:T(8,128)(2,1)S(1)}, bf16[2,128,512]{2,1,0:T(8,128)(2,1)S(1)}, u32[]{:S(2)}, u32[]{:S(2)}) collective-permute-start(bf16[2,128,512]{2,1,0:T(8,128)(2,1)S(1)} %fusion.2), channel_id=1, source_target_pairs={{0,1},{1,0},{2,3},{3,2},{4,5},{5,4},{6,7},{7,6},{8,9},{9,8},{10,11... | collective-permute-start | bytes 786440 | tf_op jit(solution)/shard_map/ppermute | solution.py:429
  (8 other events, 8.7 us)
Sparse Core Ops, SparseCore 0:
  81.0 25.2 reduce-scatter.1

commit v3 on v2

v3 whole, which is shorter than its diff:
```python
import jax
import jax.numpy as jnp
from jax import lax
from jax.experimental import pallas as pl
from jax.experimental.pallas import tpu as pltpu
from jax.sharding import PartitionSpec as P

HD = 128
BLK = 128
GRP = 8
NY = 4
NZ = 4
NX = 4
HALF = 4
QW = GRP * HD
SLOTS = 2 * NY
PAIRS = 4
NG = 2
LOW = jnp.bfloat16
F32 = jnp.float32
SCALE = HD**-0.5
EXP_SCALE = SCALE * 1.4426950408889634
MASKED = -1e30
LIGHT = pl.CostEstimate(flops=1, bytes_accessed=1, transcendentals=0)


def dot_nt(a, b):
    return lax.dot_general(a, b, (((1,), (1,)), ((), ())), preferred_element_type=F32)


def dot_nn(a, b):
    return lax.dot_general(a, b, (((1,), (0,)), ((), ())), preferred_element_type=F32)


def dot_tn(a, b):
    return lax.dot_general(a, b, (((0,), (0,)), ((), ())), preferred_element_type=F32)


def walk(parents, block, chain):
    def above(step, carry):
        current, count = carry
        parent = parents[0, current]
        more = parent != current
        current = jnp.where(more, parent, current)
        chain[step + 1] = current
        return current, count + more.astype(jnp.int32)

    chain[0] = block
    return lax.fori_loop(0, SLOTS - 1, above, (block, jnp.int32(1)))[1]


def fold(a, op):
    while a.shape[0] > 8:
        half = a.shape[0] // 2
        a = op(a[:half], a[half:])
    return a


def causal_mask():
    key_pos = lax.broadcasted_iota(jnp.int32, (BLK, BLK), 0)
    query_pos = lax.broadcasted_iota(jnp.int32, (BLK, BLK), 1)
    causal = jnp.where(key_pos <= query_pos, 0.0, MASKED).astype(F32)
    return jnp.concatenate([causal] * GRP, axis=1)


def block_sign(labels, block):
    return jnp.full((BLK, HD), jnp.where(labels[0, block] == 2, -1.0, 1.0), F32).astype(LOW)


def masked(s, t, count, first, causal):
    second = jnp.where(2 * t + 1 < count, 0.0, MASKED).astype(F32)
    s_a = s[:BLK]
    if first:
        s_a = s_a + causal
    return s_a, s[BLK:] + second


def over_pairs(step, pairs):
    def more(t, carry):
        step(t, False)
        return carry

    step(0, True)
    lax.fori_loop(1, pairs, more, 0)


def values_kernel(
    place, parents, labels,
    q_own, q_par, g_own, g_par, keys,
    dv_out, stats,
    chain, k_pair, q_st, g_st, p_st, w_st, m_st, mt_st, l_st, dv_acc,
):
    y = place[0]
    c = place[1]
    heads = range(NG)
    dv_acc[...] = jnp.zeros_like(dv_acc)
    causal = causal_mask()

    def one_block(which, block, q_ref, g_ref):
        count = walk(parents, block, chain)
        pairs = (count + 1) // 2
        sign = block_sign(labels, block)
        for n in heads:
            for h in range(GRP):
                rows = slice(h * BLK, (h + 1) * BLK)
                cols = slice(n * QW + h * HD, n * QW + (h + 1) * HD)
                q_st[n, rows, :] = q_ref[:, cols]
                g_st[n, rows, :] = g_ref[:, cols] * sign

        def scores(t, first):
            for n in heads:
                for e in range(2):
                    k_pair[n, e * BLK : (e + 1) * BLK, :] = keys[chain[2 * t + e], :, n * HD : (n + 1) * HD]
            for n in heads:
                s_a, s_b = masked(dot_nt(k_pair[n], q_st[n]), t, count, first, causal)
                top = jnp.max(fold(jnp.maximum(s_a, s_b), jnp.maximum), axis=0, keepdims=True)
                if not first:
                    old = m_st[n, 0:1, :]
                    top = jnp.maximum(top, old)
                    alpha = jnp.exp2((old - top) * EXP_SCALE)
                p_a = jnp.exp2((s_a - top) * EXP_SCALE)
                p_b = jnp.exp2((s_b - top) * EXP_SCALE)
                p_st[n, t] = jnp.concatenate([p_a.astype(LOW), p_b.astype(LOW)], axis=0)
                total = fold(p_a + p_b, jnp.add)
                if first:
                    l_st[n] = total
                else:
                    l_st[n] = l_st[n] * alpha + total
                m_st[n, 0:1, :] = top
                mt_st[n, t, 0:1, :] = top

        over_pairs(scores, pairs)
        for n in heads:
            total = jnp.sum(l_st[n], axis=0, keepdims=True)
            l_st[n, 0:1, :] = 1.0 / total
            stats[n, which, 0:1, :] = m_st[n, 0:1, :] * EXP_SCALE + jnp.log2(total)

        def values(t, first):
            for n in heads:
                f = jnp.exp2((mt_st[n, t, 0:1, :] - m_st[n, 0:1, :]) * EXP_SCALE) * l_st[n, 0:1, :]
                w_st[n] = (p_st[n, t].astype(F32) * f).astype(LOW)
            for n in heads:
                dv = dot_nn(w_st[n], g_st[n])
                for e in range(2):
                    dv_acc[n, chain[2 * t + e]] += dv[e * BLK : (e + 1) * BLK, :]

        over_pairs(values, pairs)

    one_block(0, 2 * y + c, q_own, g_own)
    one_block(1, 2 * y + 1 - c, q_par, g_par)
    for s in range(SLOTS):
        for n in heads:
            dv_out[s, :, n * HD : (n + 1) * HD] = dv_acc[n, s].astype(LOW)


def output_kernel(
    place, parents, labels,
    q_own, q_par, g_own, g_par, keys, vals, stats,
    o_own, o_par, dq_own, dq_par, dk_out,
    chain, k_pair, v_pair, kt_pair, vt_pair, q_st, g_st, gt_st, w_st, ds_st, in_st, ot_st, dqt_st, dk_acc,
):
    y = place[0]
    c = place[1]
    heads = range(NG)
    dk_acc[...] = jnp.zeros_like(dk_acc)
    causal = causal_mask()

    def one_block(which, block, q_ref, g_ref, o_ref, dq_ref):
        count = walk(parents, block, chain)
        pairs = (count + 1) // 2
        sign = block_sign(labels, block)
        for n in heads:
            for h in range(GRP):
                rows = slice(h * BLK, (h + 1) * BLK)
                cols = slice(n * QW + h * HD, n * QW + (h + 1) * HD)
                q_st[n, rows, :] = q_ref[:, cols]
                g = g_ref[:, cols] * sign
                g_st[n, rows, :] = g
                gt_st[n, :, rows] = g.T

        def outputs(t, first):
            for n in heads:
                for e in range(2):
                    s = chain[2 * t + e]
                    rows = slice(e * BLK, (e + 1) * BLK)
                    k = keys[s, :, n * HD : (n + 1) * HD]
                    v = vals[s, :, n * HD : (n + 1) * HD]
                    k_pair[n, t, rows, :] = k
                    v_pair[n, t, rows, :] = v
                    kt_pair[n, t, :, rows] = k.T
                    vt_pair[n, t, :, rows] = v.T
            for n in heads:
                s_a, s_b = masked(dot_nt(k_pair[n, t], q_st[n]), t, count, first, causal)
                lse = stats[n, which, 0:1, :]
                w_a = jnp.exp2(s_a * EXP_SCALE - lse).astype(LOW)
                w_b = jnp.exp2(s_b * EXP_SCALE - lse).astype(LOW)
                w = jnp.concatenate([w_a, w_b], axis=0)
                w_st[n, t] = w
                out = dot_nn(vt_pair[n, t], w)
                if first:
                    ot_st[n] = out
                else:
                    ot_st[n] += out

        over_pairs(outputs, pairs)
        for h in range(GRP):
            for n in heads:
                cols = slice(h * BLK, (h + 1) * BLK)
                out = ot_st[n, :, cols].astype(LOW)
                o_ref[:, n * QW + h * HD : n * QW + (h + 1) * HD] = out.T
                in_st[n, 0:1, cols] = jnp.sum(
                    gt_st[n, :, cols].astype(F32) * out.astype(F32), axis=0, keepdims=True
                )

        def grads(t, first):
            for n in heads:
                dp = dot_nn(v_pair[n, t], gt_st[n])
                ds = (w_st[n, t].astype(F32) * (dp - in_st[n, 0:1, :])).astype(LOW)
                ds_st[n] = ds
                dq = dot_nn(kt_pair[n, t], ds)
                if first:
                    dqt_st[n] = dq
                else:
                    dqt_st[n] += dq
            for n in heads:
                dk = dot_nn(ds_st[n], q_st[n])
                for e in range(2):
                    dk_acc[n, chain[2 * t + e]] += dk[e * BLK : (e + 1) * BLK, :]

        over_pairs(grads, pairs)
        for h in range(GRP):
            for n in heads:
                cols = slice(h * BLK, (h + 1) * BLK)
                dq_ref[:, n * QW + h * HD : n * QW + (h + 1) * HD] = (dqt_st[n, :, cols] * SCALE).astype(LOW).T

    one_block(0, 2 * y + c, q_own, g_own, o_own, dq_own)
    one_block(1, 2 * y + 1 - c, q_par, g_par, o_par, dq_par)
    for s in range(SLOTS):
        for n in heads:
            dk_out[s, :, n * HD : (n + 1) * HD] = (dk_acc[n, s] * SCALE).astype(LOW)


def output_onward_kernel(*refs):
    output_kernel(*refs[:10], *refs[13:])


ROWS = GRP * BLK


def attention_call(kernel, name, steps, in_specs, out_specs, out_shape, scratch, aliases={}):
    return pl.pallas_call(
        kernel,
        grid_spec=pltpu.PrefetchScalarGridSpec(
            num_scalar_prefetch=3,
            grid=(steps,),
            in_specs=in_specs,
            out_specs=out_specs,
            scratch_shapes=[pltpu.SMEM((SLOTS,), jnp.int32)] + [pltpu.VMEM(*s) for s in scratch],
        ),
        out_shape=out_shape,
        input_output_aliases=aliases,
        compiler_params=pltpu.CompilerParams(dimension_semantics=("arbitrary",), vmem_limit_bytes=48 * 2**20),
        cost_estimate=LIGHT,
        name=name,
    )


def own_spec(start):
    return pl.BlockSpec((BLK, NG * QW), lambda i, place, par, lab: (0, place[1] * (HALF // NG) + start + i))


def partner_spec(start):
    return pl.BlockSpec((BLK, NG * QW), lambda i, place, par, lab: (0, start + i))


def blocks_spec(start):
    return pl.BlockSpec((SLOTS, BLK, NG * HD), lambda i, place, par, lab: (0, 0, start + i))


def stats_spec(start):
    return pl.BlockSpec((NG, 2, 8, ROWS), lambda i, place, par, lab: (start + i, 0, 0, 0))


def value_gradient(*args):
    own, partner = own_spec(0), partner_spec(0)
    return attention_call(
        values_kernel, "tree_values", HALF // NG,
        [own, partner, own, partner, blocks_spec(0)],
        [blocks_spec(0), stats_spec(0)],
        [jax.ShapeDtypeStruct((SLOTS, BLK, HALF * HD), LOW), jax.ShapeDtypeStruct((HALF, 2, 8, ROWS), F32)],
        [
            ((NG, 2 * BLK, HD), LOW),
            ((NG, ROWS, HD), LOW),
            ((NG, ROWS, HD), LOW),
            ((NG, PAIRS, 2 * BLK, ROWS), LOW),
            ((NG, 2 * BLK, ROWS), LOW),
            ((NG, 8, ROWS), F32),
            ((NG, PAIRS, 8, ROWS), F32),
            ((NG, 8, ROWS), F32),
            ((NG, SLOTS, BLK, HD), F32),
        ],
    )(*args)


def output_and_gradients(start, before, *args):
    own, partner, partner_out = own_spec(start), partner_spec(start), partner_spec(0)
    own_shape = jax.ShapeDtypeStruct((BLK, 2 * HALF * QW), LOW)
    partner_shape = jax.ShapeDtypeStruct((BLK, NG * QW), LOW)
    return attention_call(
        output_onward_kernel if before else output_kernel, "tree_outputs", 1,
        [own, partner, own, partner, blocks_spec(start), blocks_spec(start), stats_spec(start)]
        + [pl.BlockSpec(memory_space=pl.ANY)] * len(before),
        [own, partner_out, own, partner_out, blocks_spec(start)],
        [own_shape, partner_shape, own_shape, partner_shape, jax.ShapeDtypeStruct((SLOTS, BLK, HALF * HD), LOW)],
        [
            ((NG, PAIRS, 2 * BLK, HD), LOW),
            ((NG, PAIRS, 2 * BLK, HD), LOW),
            ((NG, PAIRS, HD, 2 * BLK), LOW),
            ((NG, PAIRS, HD, 2 * BLK), LOW),
            ((NG, ROWS, HD), LOW),
            ((NG, ROWS, HD), LOW),
            ((NG, HD, ROWS), LOW),
            ((NG, PAIRS, 2 * BLK, ROWS), LOW),
            ((NG, 2 * BLK, ROWS), LOW),
            ((NG, 8, ROWS), F32),
            ((NG, HD, ROWS), F32),
            ((NG, HD, ROWS), F32),
            ((NG, SLOTS, BLK, HD), F32),
        ],
        {10: 0, 11: 2, 12: 4} if before else {},
    )(*args, *before)


def weight_kernel(place, *refs):
    x_own, x_other, dv, out, x_all = refs[:NZ], refs[NZ : 2 * NZ], refs[-3], refs[-2], refs[-1]
    c, z = place[1], place[2]
    for d in range(NZ):
        src = lax.rem(z + NZ - d, NZ)
        for x, core in ((x_own[d], c), (x_other[d], 1 - c)):
            x_all[:, pl.ds(pl.multiple_of((2 * src + core) * BLK, BLK), BLK)] = x[...]
    out[...] = dot_nn(x_all[...], dv[...].reshape(2 * NZ * BLK, -1)).astype(LOW)


def weight_partial(place, x_own, x_other, dv):
    tall, wide, step = x_own[0].shape[0], dv.shape[3], 256
    x_spec = pl.BlockSpec((step, BLK), lambda i, place: (i, 0))
    return pl.pallas_call(
        weight_kernel,
        grid_spec=pltpu.PrefetchScalarGridSpec(
            num_scalar_prefetch=1,
            grid=(tall // step,),
            in_specs=[x_spec] * (2 * NZ) + [pl.BlockSpec((NZ, 2, BLK, wide), lambda i, place: (0, 0, 0, 0))],
            out_specs=pl.BlockSpec((step, wide), lambda i, place: (i, 0)),
            scratch_shapes=[pltpu.VMEM((step, 2 * NZ * BLK), LOW)],
        ),
        out_shape=jax.ShapeDtypeStruct((tall, wide), LOW),
        compiler_params=pltpu.CompilerParams(vmem_limit_bytes=60 * 2**20),
        cost_estimate=LIGHT,
        name="weight_partial",
    )(place, *x_own, *x_other, dv)


def halves_kernel(rows, out, done):
    width = out.shape[2]
    copies = [
        pltpu.make_async_copy(rows.at[:, pl.ds(i % 2 * width, width)], out.at[i], done.at[i]) for i in range(SLOTS)
    ]
    for copy in copies:
        copy.start()
    for copy in copies:
        copy.wait()


def halves(rows):
    width = rows.shape[1] // 2
    return pl.pallas_call(
        halves_kernel,
        out_shape=jax.ShapeDtypeStruct((SLOTS, BLK, width), LOW),
        out_specs=pl.BlockSpec(memory_space=pl.ANY),
        scratch_shapes=[pltpu.SemaphoreType.DMA((SLOTS,))],
        cost_estimate=LIGHT,
        name="halves",
    )(rows)


def run_copies(pairs, done):
    copies = [pltpu.make_async_copy(a, b, done.at[i]) for i, (a, b) in enumerate(pairs)]
    for copy in copies:
        copy.start()
    for copy in copies:
        copy.wait()


def partner_kernel(place, q, g, q_out, g_out, done):
    width = HALF * QW
    at = pl.multiple_of((1 - place[1]) * width, width)
    step = BLK // 4
    pairs = []
    for a, b in ((q, q_out), (g, g_out)):
        for i in range(4):
            rows = pl.ds(i * step, step)
            pairs.append((a.at[rows, pl.ds(at, width)], b.at[rows, :]))
    run_copies(pairs, done)


def partner_halves(place, q, g):
    out = jax.ShapeDtypeStruct((BLK, HALF * QW), LOW)
    anywhere = pl.BlockSpec(memory_space=pl.ANY)
    return pl.pallas_call(
        partner_kernel,
        grid_spec=pltpu.PrefetchScalarGridSpec(
            num_scalar_prefetch=1,
            grid=(1,),
            in_specs=[anywhere] * 2,
            out_specs=[anywhere] * 2,
            scratch_shapes=[pltpu.SemaphoreType.DMA((8,))],
        ),
        out_shape=[out, out],
        cost_estimate=LIGHT,
        name="partner_halves",
    )(place, q, g)


def fill_kernel(place, o_before, dq_before, o_a, o_b, dq_a, dq_b, o_all, dq_all, done):
    width = NG * QW
    pairs = []
    for whole, parts in ((o_all, (o_a, o_b)), (dq_all, (dq_a, dq_b))):
        for i, part in enumerate(parts):
            at = pl.multiple_of((1 - place[1]) * HALF * QW + i * width, width)
            for j in range(2):
                rows = pl.ds(j * BLK // 2, BLK // 2)
                pairs.append((part.at[rows, :], whole.at[rows, pl.ds(at, width)]))
    run_copies(pairs, done)


def fill_partner(place, o_all, dq_all, o_parts, dq_parts):
    anywhere = pl.BlockSpec(memory_space=pl.ANY)
    return pl.pallas_call(
        fill_kernel,
        grid_spec=pltpu.PrefetchScalarGridSpec(
            num_scalar_prefetch=1,
            grid=(1,),
            in_specs=[anywhere] * 6,
            out_specs=[anywhere] * 2,
            scratch_shapes=[pltpu.SemaphoreType.DMA((8,))],
        ),
        out_shape=[jax.ShapeDtypeStruct(o_all.shape, LOW)] * 2,
        input_output_aliases={1: 0, 2: 1},
        cost_estimate=LIGHT,
        name="fill_partner",
    )(place, o_all, dq_all, *o_parts, *dq_parts)


def split_kernel(place, dk, r1, r2, r3, dv, after, mine, other):
    c = place[1]
    for out, e in ((mine, c), (other, 1 - c)):
        acc = dk[0, e].astype(F32)
        for r in (r1, r2, r3):
            acc = acc + r[e].astype(F32)
        out[0] = acc.astype(LOW)
        out[1] = dv[0, e]


def split_grads(place, dk, received, dv, after):
    width = dk.shape[3]
    pair = pl.BlockSpec((2, BLK, width), lambda i, place: (0, 0, 0))
    return pl.pallas_call(
        split_kernel,
        grid_spec=pltpu.PrefetchScalarGridSpec(
            num_scalar_prefetch=1,
            grid=(1,),
            in_specs=[pl.BlockSpec((1, 2, BLK, width), lambda i, place: (place[0], 0, 0, 0))]
            + [pair] * 3
            + [pl.BlockSpec((1, 2, BLK, width), lambda i, place: (0, 0, 0, 0)), pl.BlockSpec(memory_space=pl.ANY)],
            out_specs=[pair, pair],
        ),
        out_shape=[jax.ShapeDtypeStruct((2, BLK, width), LOW)] * 2,
        cost_estimate=LIGHT,
        name="split_grads",
    )(place, dk, *received, dv, after)


def join_kernel(place, mine, other, key_grad, value_grad):
    width = mine.shape[2]
    for i, out in enumerate((key_grad, value_grad)):
        out[:, pl.ds(pl.multiple_of(place[1] * width, width), width)] = mine[i]
        out[:, pl.ds(pl.multiple_of((1 - place[1]) * width, width), width)] = other[i]


def join_grads(place, mine, other):
    width = mine.shape[2]
    pair = pl.BlockSpec((2, BLK, width), lambda i, place: (0, 0, 0))
    rows = pl.BlockSpec((BLK, 2 * width), lambda i, place: (0, 0))
    return pl.pallas_call(
        join_kernel,
        grid_spec=pltpu.PrefetchScalarGridSpec(
            num_scalar_prefetch=1, grid=(1,), in_specs=[pair, pair], out_specs=[rows, rows]
        ),
        out_shape=[jax.ShapeDtypeStruct((BLK, 2 * width), LOW)] * 2,
        cost_estimate=LIGHT,
        name="join_grads",
    )(place, mine, other)


def x_kernel(place, x, *outs):
    piece = x.shape[1] // (NX * NZ)
    for d in range(NZ):
        to = lax.rem(place[2] + d, NZ)
        for i in range(NX):
            at = pl.multiple_of((i * NZ + to) * piece, piece)
            outs[d][i * piece : (i + 1) * piece, :] = x[:, pl.ds(at, piece)].T


def x_sends(place, x):
    tall = x.shape[1] // NZ
    return pl.pallas_call(
        x_kernel,
        grid_spec=pltpu.PrefetchScalarGridSpec(
            num_scalar_prefetch=1,
            grid=(1,),
            in_specs=[pl.BlockSpec(x.shape, lambda i, place: (0, 0))],
            out_specs=[pl.BlockSpec((tall, BLK), lambda i, place: (0, 0))] * NZ,
        ),
        out_shape=[jax.ShapeDtypeStruct((tall, BLK), LOW)] * NZ,
        cost_estimate=LIGHT,
        name="x_sends",
    )(place, x)


def sum_kernel(terms, out, total, done):
    for e in range(2):
        acc = terms[0, e].astype(F32)
        for i in range(1, NY):
            acc = acc + terms[i, e].astype(F32)
        total[e] = acc.astype(LOW)
    copies = [pltpu.make_async_copy(total, out.at[i], done.at[i]) for i in range(NZ)]
    for copy in copies:
        copy.start()
    for copy in copies:
        copy.wait()


def sum_blocks(terms):
    return pl.pallas_call(
        sum_kernel,
        out_shape=jax.ShapeDtypeStruct((NZ,) + terms.shape[1:], LOW),
        out_specs=pl.BlockSpec(memory_space=pl.ANY),
        scratch_shapes=[pltpu.VMEM(terms.shape[1:], LOW), pltpu.SemaphoreType.DMA((NZ,))],
        compiler_params=pltpu.CompilerParams(vmem_limit_bytes=60 * 2**20),
        cost_estimate=LIGHT,
        name="sum_blocks",
    )(terms)


def finish_kernel(parts, out):
    width = parts.shape[2]
    for half in range(2):
        acc = parts[half].astype(F32)
        for i in range(1, NX * NY):
            acc = acc + parts[2 * i + half].astype(F32)
        out[:, half * width : (half + 1) * width] = acc * (16 * SLOTS * BLK) ** -0.5


def finish_weight(parts):
    rows, width = parts.shape[1:]
    return pl.pallas_call(
        finish_kernel,
        out_shape=jax.ShapeDtypeStruct((rows, 2 * width), F32),
        compiler_params=pltpu.CompilerParams(vmem_limit_bytes=60 * 2**20),
        cost_estimate=LIGHT,
        name="finish_weight",
    )(parts)


def device(x, z, y, c):
    return (x * NZ + z) * SLOTS + y * 2 + c


def per_device(query_rows, key_rows, value_rows, layer_input, out_grad, parents, labels):
    ctx = lax.axis_index("ctx")
    y, c, z = ctx // 2, ctx % 2, lax.axis_index("dp") % NZ
    place = jnp.stack([y, c, z]).astype(jnp.int32)
    q, k, v, g, x = query_rows[0], key_rows[0], value_rows[0], out_grad[0], layer_input[0]
    along_y = [[2 * m + n for m in range(NY)] for n in range(2)]
    along_z = [[i * NZ + j for j in range(NZ)] for i in range(NX)]
    across = [[device(i, j, m, n) for i in range(NX) for m in range(NY) for n in range(2)] for j in range(NZ)]

    def swap(a):
        return lax.ppermute(a, "ctx", [(i, i ^ 1) for i in range(SLOTS)])

    def pick(a, i):
        return lax.dynamic_index_in_dim(a, i, 0, keepdims=False)

    def further(a, d):
        return lax.ppermute(a, "dp", [(i, i // NZ * NZ + (i + d) % NZ) for i in range(NX * NZ)])

    def earlier(a, d):
        return lax.ppermute(a, "ctx", [(i + 2 * d, i) for i in range(SLOTS - 2 * d)])

    keys = lax.all_to_all(halves(k), "ctx", 0, 0)
    q_par, g_par = [swap(a) for a in partner_halves(place, q, g)]
    x_own = x_sends(place, x)
    v_sends = halves(v)
    x_own = [x_own[0]] + [further(x_own[d], d) for d in range(1, NZ)]
    keys, v_sends, x_own[1], x_own[3] = lax.optimization_barrier((keys, v_sends, x_own[1], x_own[3]))
    vals = lax.all_to_all(v_sends, "ctx", 0, 0)
    dv, stats = value_gradient(place, parents, labels, q, q_par, g, g_par, keys)
    dv, vals, x_own = lax.optimization_barrier((dv, vals, x_own))
    dv = lax.all_to_all(dv.reshape(NY, 2, BLK, HALF * HD), "ctx", 0, 0, axis_index_groups=along_y)
    args = (place, parents, labels, q, q_par, g, g_par, keys, vals, stats)
    o_own, o_par, dq_own, dq_par, dk = output_and_gradients(0, (), *args)
    o_pars, dq_pars = [o_par], [dq_par]
    dv, dk, x_own = lax.optimization_barrier((dv, dk, x_own))
    x_other = [swap(a) for a in x_own]
    dv_sends = sum_blocks(dv)
    dv_sends, dk = lax.optimization_barrier((dv_sends, dk))
    dv_all = lax.all_to_all(dv_sends, "dp", 0, 0, axis_index_groups=along_z)
    o_own, o_par, dq_own, dq_par, dk = output_and_gradients(1, (o_own, dq_own, dk), *args)
    o_pars, dq_pars = o_pars + [o_par], dq_pars + [dq_par]
    dk = dk.reshape(NY, 2, BLK, HALF * HD)
    received = [earlier(pick(dk, jnp.maximum(y - d, 0)), d) for d in range(1, NY)]
    partial = weight_partial(place, x_own, x_other, dv_all).reshape(2 * NX * NY, -1, HALF * HD)
    after, o_pars, dq_pars = lax.optimization_barrier((partial, o_pars, dq_pars))
    o_pars, dq_pars = [swap(a) for a in o_pars], [swap(a) for a in dq_pars]
    weight_grad = finish_weight(lax.all_to_all(partial, ("dp", "ctx"), 0, 0, axis_index_groups=across))
    out, query_grad = fill_partner(place, o_own, dq_own, o_pars, dq_pars)
    mine, other = split_grads(place, dk, received, dv_sends, after)
    key_grad, value_grad = join_grads(place, mine, swap(other))
    return out[None], query_grad[None], key_grad[None], value_grad[None], weight_grad


def solution(mesh):
    rows = P("dp", "ctx", None)
    return jax.shard_map(
        per_device,
        mesh=mesh,
        in_specs=(rows,) * 5 + (P("dp", None), P("dp", None)),
        out_specs=(rows,) * 4 + (P(("dp", "ctx"), None),),
        check_vma=False,
    )
```

time: 149 us -> 267 us (1.79)
  Pallas kernels: 37 us -> 177 us
  between operations: 14.2 us -> 0.93 us
  local copies, waits for them, and re-layouts: 11.8 us -> 6.99 us
  waiting for transfers between devices: 40.7 us -> 36.6 us
  starting transfers between devices: 39.7 us -> 42.6 us
    pallas_call x3 -> x9, Pallas kernels: 24.8 us -> 164 us  [the longest x1 65.4 us: partner_halves(): pl.pallas_call(partner_kernel, grid_spec=pltpu.PrefetchScalarGridSpec(num...]
    ppermute x0 -> x3, waiting for transfers between devices: none -> 14.1 us  [earlier(): lax.ppermute(a, 'ctx', [(i + 2 * d, i) for i in range(SLOTS - 2 * d)])]
    all_to_all x1, waiting for transfers between devices: 13.3 us -> 0.01 us  [per_device(): lax.all_to_all(partial, ('dp', 'ctx'), 0, 0, axis_index_groups=across)]
    ppermute x3, waiting for transfers between devices: 10.2 us -> 0.01 us  [further(): lax.ppermute(a, 'dp', [(i, i // NZ * NZ + (i + d) % NZ) for i in range(NX...]
    all_to_all x1 -> x2, starting transfers between devices: 6.1 us -> 11.1 us  [the longest x1 5.98 us: per_device(): keys = lax.all_to_all(halves(k), 'ctx', 0, 0)]
    all_to_all x1 -> x2, waiting for transfers between devices: 0.01 us -> 4.91 us  [the longest x1 4.91 us: per_device(): vals = lax.all_to_all(v_sends, 'ctx', 0, 0)]
    dynamic_update_slice x2 -> x0, local copies, waits for them, and re-layouts: 4.58 us -> none  [the longest x1 2.29 us: per_device(): out = lax.dynamic_update_slice_in_dim(o_own, o_swapped, at, 1)]
    ppermute x0 -> x3, starting transfers between devices: none -> 3.88 us  [earlier(): lax.ppermute(a, 'ctx', [(i + 2 * d, i) for i in range(SLOTS - 2 * d)])]
  transfers between devices with their start and end apart: 17 -> 22, of which waited for: 7 -> 11; matrix products, arithmetic and copies ran while one was open for 6% -> 0% of each run, Pallas kernels for 15% -> 62%
where the time goes in v3:
time: 267 us; the launch traced here: 265 us
  Pallas kernels  177 us (66%)
  starting transfers between devices  42.6 us (16%)
  waiting for transfers between devices  36.6 us (14%)
  local copies, waits for them, and re-layouts  6.99 us (3%)
    pallas_call x1, Pallas kernels, partner_halves(): pl.pallas_call(partner_kernel, grid_spec=pltpu.PrefetchScalarGridSpec(num...  65.4 us
    pallas_call x1, Pallas kernels, fill_partner(): pl.pallas_call(fill_kernel, grid_spec=pltpu.PrefetchScalarGridSpec(num_sc...  65.4 us
    pallas_call x2, Pallas kernels, output_and_gradients(): attention_call(output_onward_kernel if before else output_kernel, 'tree_o...  16.1 us
    ppermute x3, waiting for transfers between devices, earlier(): lax.ppermute(a, 'ctx', [(i + 2 * d, i) for i in range(SLOTS - 2 * d)])  14.1 us
    all_to_all x1, waiting for transfers between devices, per_device(): dv_all = lax.all_to_all(dv_sends, 'dp', 0, 0, axis_index_groups=along_z)  8.93 us
    all_to_all x1, starting transfers between devices, per_device(): lax.all_to_all(partial, ('dp', 'ctx'), 0, 0, axis_index_groups=across)  7.82 us
    pallas_call x1, Pallas kernels, value_gradient(): attention_call(values_kernel, 'tree_values', HALF // NG, [own, partner, o...  7.66 us
    unnamed x34, local copies, waits for them, and re-layouts  6.94 us
  transfers between devices with their start and end apart: 22, of which 11 were waited for; matrix products, arithmetic and copies ran while one was open for 0% of the time, Pallas kernels for 62%

profile of v3, /device:TPU:1, one launch (start us, length us, event | category | flops | bytes accessed | tf_op | source)
XLA Modules:
  0.0 265.0 jit_solution(3768847538065283740)
XLA Ops:
  0.6 2.0 halves.2
  2.7 6.0 %all-to-all-start = ((bf16[8,128,512]{2,1,0:T(8,128)(2,1)}), bf16[8,128,512]{2,1,0:T(8,128)(2,1)S(1)}, u32[]{:S(2)}, u32[]{:S(2)}) async-start(bf16[8,128,512]{2,1,0:T(8,128)(2,1)} %halves.2), calls=%async_computation | async-start | bytes 2097152 | tf_op jit(solution)/shard_map/all_to_all | solution.py:600
  9.3 3.1 %x_sends.1 = (bf16[1024,128]{1,0:T(8,128)(2,1)}, bf16[1024,128]{1,0:T(8,128)(2,1)}, bf16[1024,128]{1,0:T(8,128)(2,1)}, bf16[1024,128]{1,0:T(8,128)(2,1)}) custom-call(s32[3]{0:T(128)} %pad_add_fusion.place.refs_0_, bf16[128,4096]{1,0:T(8,128)(2,1)} %bitcast.36), custom_call_target="tpu_custom_call" | custom-call | flops 1 | bytes 1 | tf_op jit(solution)/shard_map/x_sends/pallas_call | solution.py:516
  14.0 2.1 collective-permute-start.3
  16.1 65.4 %partner_halves.1 = (bf16[128,4096]{1,0:T(8,128)(2,1)}, bf16[128,4096]{1,0:T(8,128)(2,1)}) custom-call(s32[3]{0:T(128)} %pad_add_fusion.place.refs_0_, bf16[128,8192]{1,0:T(8,128)(2,1)} %bitcast.24, bf16[128,8192]{1,0:T(8,128)(2,1)} %bitcast.28), custom_call_target="tpu_custom_call" | custom-call | flops 1 | bytes 1 | tf_op jit(solution)/shard_map/partner_halves/pallas_call | solution.py:409
  84.2 5.1 %all-to-all-start.1 = ((bf16[8,128,512]{2,1,0:T(8,128)(2,1)}), bf16[8,128,512]{2,1,0:T(8,128)(2,1)}, u32[]{:S(2)}, u32[]{:S(2)}) async-start(bf16[8,128,512]{2,1,0:T(8,128)(2,1)} %halves.3), calls=%async_computation.1 | async-start | bytes 2097152 | tf_op jit(solution)/shard_map/all_to_all | solution.py:606
  90.9 7.7 %tree_values.1 = (bf16[8,128,512]{2,1,0:T(8,128)(2,1)S(1)}, f32[4,2,8,1024]{3,2,1,0:T(8,128)S(1)}) custom-call(s32[3]{0:T(128)S(1)} %copy-done.4, s32[1,8]{1,0:T(1,128)S(1)} %copy-done.6, s32[1,8]{1,0:T(1,128)S(1)} %copy-done.7, bf16[128,8192]{1,0:T(8,128)(2,1)} %bitcast.25, bf16[128,4096]{1,0:T(8,128)(2,1)S(1)} %collective-permute-done.q_par.refs_4_, ...), custom_call_target="tpu_custom_call" | custom-call | flops 1 | bytes 1 | tf_op jit(solution)/shard_map/tree_values/pallas_call | solution.py:286
  99.6 4.9 %all-to-all-done.1.vals.refs_8_ = bf16[8,128,512]{2,1,0:T(8,128)(2,1)} async-done(((bf16[8,128,512]{2,1,0:T(8,128)(2,1)}), bf16[8,128,512]{2,1,0:T(8,128)(2,1)}, u32[]{:S(2)}, u32[]{:S(2)}) %all-to-all-start.1) | async-done | bytes 1048608 | tf_op jit(solution)/shard_map/all_to_all | solution.py:606
  104.5 4.2 %all-to-all-start.2 = ((bf16[4,2,128,512]{3,2,1,0:T(8,128)(2,1)}), bf16[4,2,128,512]{3,2,1,0:T(8,128)(2,1)}, u32[]{:S(2)}, u32[]{:S(2)}) async-start(bf16[4,2,128,512]{3,2,1,0:T(8,128)(2,1)} %bitcast.23), calls=%async_computation.2 | async-start | bytes 2097152 | tf_op jit(solution)/shard_map/all_to_all | solution.py:609
  108.7 8.0 %tree_outputs.2 = (bf16[128,8192]{1,0:T(8,128)(2,1)}, bf16[128,2048]{1,0:T(8,128)(2,1)}, bf16[128,8192]{1,0:T(8,128)(2,1)}, bf16[128,2048]{1,0:T(8,128)(2,1)}, bf16[8,128,512]{2,1,0:T(8,128)(2,1)S(1)}) custom-call(s32[3]{0:T(128)S(1)} %copy-done.4, s32[1,8]{1,0:T(1,128)S(1)} %copy-done.6, s32[1,8]{1,0:T(1,128)S(1)} %copy-done.7, bf16[128,8192]{1,0:T(8,128)(2,1)} %bitcast.26, ...), custom_call_target="tpu_custom_call" | custom-call | flops 1 | bytes 1 | tf_op jit(solution)/shard_map/tree_outputs/pallas_call | solution.py:309
  117.7 5.3 %all-to-all-done.2.terms = bf16[4,2,128,512]{3,2,1,0:T(8,128)(2,1)} async-done(((bf16[4,2,128,512]{3,2,1,0:T(8,128)(2,1)}), bf16[4,2,128,512]{3,2,1,0:T(8,128)(2,1)}, u32[]{:S(2)}, u32[]{:S(2)}) %all-to-all-start.2) | async-done | bytes 1048608 | tf_op jit(solution)/shard_map/all_to_all | solution.py:609
  123.1 2.4 sum_blocks.1.dv
  125.4 4.3 %all-to-all-start.3 = ((bf16[4,2,128,512]{3,2,1,0:T(8,128)(2,1)}), bf16[4,2,128,512]{3,2,1,0:T(8,128)(2,1)}, u32[]{:S(2)}, u32[]{:S(2)}) async-start(bf16[4,2,128,512]{3,2,1,0:T(8,128)(2,1)} %sum_blocks.1.dv), calls=%async_computation.3 | async-start | bytes 2097152 | tf_op jit(solution)/shard_map/all_to_all | solution.py:617
  134.2 8.9 %all-to-all-done.3.refs_8_ = bf16[4,2,128,512]{3,2,1,0:T(8,128)(2,1)} async-done(((bf16[4,2,128,512]{3,2,1,0:T(8,128)(2,1)}), bf16[4,2,128,512]{3,2,1,0:T(8,128)(2,1)}, u32[]{:S(2)}, u32[]{:S(2)}) %all-to-all-start.3) | async-done | bytes 1048608 | tf_op jit(solution)/shard_map/all_to_all | solution.py:617
  143.1 5.9 %weight_partial.1 = bf16[1024,512]{1,0:T(8,128)(2,1)} custom-call(s32[3]{0:T(128)} %pad_add_fusion.place.refs_0_, bf16[1024,128]{1,0:T(8,128)(2,1)} %get-tuple-element.78.refs_0_, bf16[1024,128]{1,0:T(8,128)(2,1)} %copy-done.12, bf16[1024,128]{1,0:T(8,128)(2,1)} %collective-permute-done.4.refs_2_, bf16[1024,128]{1,0:T(8,128)(2,1)} %collective-permute-done.3.refs_3_, ...), custom_call_target="tpu_custom_call" | custom-call | flops 1 | bytes 1 | tf_op jit(solution)/shard_map/weight_partial/pallas_call | solution.py:347
  149.0 7.8 %all-to-all-start.4 = ((bf16[32,32,512]{2,1,0:T(8,128)(2,1)}), bf16[32,32,512]{2,1,0:T(8,128)(2,1)}, u32[]{:S(2)}, u32[]{:S(2)}) async-start(bf16[32,32,512]{2,1,0:T(8,128)(2,1)} %bitcast.32), calls=%async_computation.4 | async-start | bytes 2097152 | tf_op jit(solution)/shard_map/all_to_all | solution.py:625
  158.1 8.1 %tree_outputs.3 = (bf16[128,8192]{1,0:T(8,128)(2,1)}, bf16[128,2048]{1,0:T(8,128)(2,1)}, bf16[128,8192]{1,0:T(8,128)(2,1)}, bf16[128,2048]{1,0:T(8,128)(2,1)}, bf16[8,128,512]{2,1,0:T(8,128)(2,1)S(1)}) custom-call(s32[3]{0:T(128)S(1)} %copy-done.5, s32[1,8]{1,0:T(1,128)S(1)} %copy-done.6, ...), custom_call_target="tpu_custom_call", output_to_operand_aliasing={{0}: (10, {}), {2}: (11, {}), {4}: (12, {})} | custom-call | flops 1 | bytes 1 | tf_op jit(solution)/shard_map/tree_outputs/pallas_call | solution.py:309
  171.7 5.5 %collective-permute-done.13.r1 = bf16[2,128,512]{2,1,0:T(8,128)(2,1)S(1)} collective-permute-done((bf16[2,128,512]{2,1,0:T(8,128)(2,1)S(1)}, bf16[2,128,512]{2,1,0:T(8,128)(2,1)S(1)}, u32[]{:S(2)}, u32[]{:S(2)}) %collective-permute-start.13) | collective-permute-done | bytes 262176 | tf_op jit(solution)/shard_map/ppermute | solution.py:598
  178.2 3.5 %collective-permute-done.14.r2 = bf16[2,128,512]{2,1,0:T(8,128)(2,1)S(1)} collective-permute-done((bf16[2,128,512]{2,1,0:T(8,128)(2,1)S(1)}, bf16[2,128,512]{2,1,0:T(8,128)(2,1)S(1)}, u32[]{:S(2)}, u32[]{:S(2)}) %collective-permute-start.14) | collective-permute-done | bytes 262176 | tf_op jit(solution)/shard_map/ppermute | solution.py:598
  182.6 5.0 %collective-permute-done.15.r3 = bf16[2,128,512]{2,1,0:T(8,128)(2,1)S(1)} collective-permute-done((bf16[2,128,512]{2,1,0:T(8,128)(2,1)S(1)}, bf16[2,128,512]{2,1,0:T(8,128)(2,1)S(1)}, u32[]{:S(2)}, u32[]{:S(2)}) %collective-permute-start.15) | collective-permute-done | bytes 262176 | tf_op jit(solution)/shard_map/ppermute | solution.py:598
  188.4 2.8 %split_grads.1 = (bf16[2,128,512]{2,1,0:T(8,128)(2,1)}, bf16[2,128,512]{2,1,0:T(8,128)(2,1)}) custom-call(s32[3]{0:T(128)} %pad_add_fusion.place.refs_0_, bf16[4,2,128,512]{3,2,1,0:T(8,128)(2,1)} %bitcast.22, bf16[2,128,512]{2,1,0:T(8,128)(2,1)} %copy-done.13, bf16[2,128,512]{2,1,0:T(8,128)(2,1)} %copy-done.14, bf16[2,128,512]{2,1,0:T(8,128)(2,1)} %copy-done.15, ...), custom_call_target="tpu_custom_call" | custom-call | flops 1 | bytes 1 | tf_op jit(solution)/shard_map/split_grads/pallas_call | solution.py:467
  193.7 2.5 join_grads.1
  197.6 65.4 %fill_partner.1 = (bf16[128,8192]{1,0:T(8,128)(2,1)}, bf16[128,8192]{1,0:T(8,128)(2,1)}) custom-call(s32[3]{0:T(128)} %pad_add_fusion.place.refs_0_, bf16[128,8192]{1,0:T(8,128)(2,1)} %get-tuple-element.76.o_before, bf16[128,8192]{1,0:T(8,128)(2,1)} %get-tuple-element.77.dq_before, ...), custom_call_target="tpu_custom_call", output_to_operand_aliasing={{0}: (1, {}), {1}: (2, {})} | custom-call | flops 1 | bytes 1 | tf_op jit(solution)/shard_map/fill_partner/pallas_call | solution.py:438
  263.0 2.0 finish_weight.1
  (69 shorter events, 26.2 us)
Async XLA Ops:
  2.7 81.5 %all-to-all-start = ((bf16[8,128,512]{2,1,0:T(8,128)(2,1)}), bf16[8,128,512]{2,1,0:T(8,128)(2,1)S(1)}, u32[]{:S(2)}, u32[]{:S(2)}) async-start(bf16[8,128,512]{2,1,0:T(8,128)(2,1)} %halves.2), calls=%async_computation | async-start | bytes 2097152 | tf_op jit(solution)/shard_map/all_to_all | solution.py:600
  12.3 71.8 %collective-permute-start.2 = (bf16[1024,128]{1,0:T(8,128)(2,1)}, bf16[1024,128]{1,0:T(8,128)(2,1)S(1)}, u32[]{:S(2)}, u32[]{:S(2)}) collective-permute-start(bf16[1024,128]{1,0:T(8,128)(2,1)} %get-tuple-element.54), channel_id=1, source_target_pairs={{0,8},{8,16},{16,24},{24,0},{32,40},{40,48},{48,56},{56,32},{64,72... | collective-permute-start | bytes 786440 | tf_op jit(solution)/shard_map/ppermute | solution.py:595
  14.0 70.2 %collective-permute-start.3 = (bf16[1024,128]{1,0:T(8,128)(2,1)}, bf16[1024,128]{1,0:T(8,128)(2,1)}, u32[]{:S(2)}, u32[]{:S(2)}) collective-permute-start(bf16[1024,128]{1,0:T(8,128)(2,1)} %get-tuple-element.55), channel_id=1, source_target_pairs={{0,24},{8,0},{16,8},{24,16},{32,56},{40,32},{48,40},{56,48},{64,88... | collective-permute-start | bytes 786440 | tf_op jit(solution)/shard_map/ppermute | solution.py:595
  81.5 9.4 %copy-start.4 = (s32[3]{0:T(128)S(1)}, s32[3]{0:T(128)}, u32[]{:S(2)}) copy-start(s32[3]{0:T(128)} %pad_add_fusion.place.refs_0_) | copy-start | bytes 40
  81.5 9.3 %collective-permute-start = (bf16[128,4096]{1,0:T(8,128)(2,1)}, bf16[128,4096]{1,0:T(8,128)(2,1)S(1)}, u32[]{:S(2)}, u32[]{:S(2)}) collective-permute-start(bf16[128,4096]{1,0:T(8,128)(2,1)} %get-tuple-element.52), channel_id=1, source_target_pairs={{0,1},{1,0},{2,3},{3,2},{4,5},{5,4},{6,7},{7,6},{8,9},{9,8},{10,11... | collective-permute-start | bytes 3145736 | tf_op jit(solution)/shard_map/ppermute | solution.py:589
  81.9 9.0 %collective-permute-start.1 = (bf16[128,4096]{1,0:T(8,128)(2,1)}, bf16[128,4096]{1,0:T(8,128)(2,1)S(1)}, u32[]{:S(2)}, u32[]{:S(2)}) collective-permute-start(bf16[128,4096]{1,0:T(8,128)(2,1)} %get-tuple-element.53), channel_id=1, source_target_pairs={{0,1},{1,0},{2,3},{3,2},{4,5},{5,4},{6,7},{7,6},{8,9},{9,8},{10,11... | collective-permute-start | bytes 3145736 | tf_op jit(solution)/shard_map/ppermute | solution.py:589
  84.2 20.3 %all-to-all-start.1 = ((bf16[8,128,512]{2,1,0:T(8,128)(2,1)}), bf16[8,128,512]{2,1,0:T(8,128)(2,1)}, u32[]{:S(2)}, u32[]{:S(2)}) async-start(bf16[8,128,512]{2,1,0:T(8,128)(2,1)} %halves.3), calls=%async_computation.1 | async-start | bytes 2097152 | tf_op jit(solution)/shard_map/all_to_all | solution.py:606
  89.3 10.3 %collective-permute-start.4 = (bf16[1024,128]{1,0:T(8,128)(2,1)}, bf16[1024,128]{1,0:T(8,128)(2,1)}, u32[]{:S(2)}, u32[]{:S(2)}) collective-permute-start(bf16[1024,128]{1,0:T(8,128)(2,1)} %get-tuple-element.61), channel_id=1, source_target_pairs={{0,16},{8,24},{16,0},{24,8},{32,48},{40,56},{48,32},{56,40},{64,80... | collective-permute-start | bytes 786440 | tf_op jit(solution)/shard_map/ppermute | solution.py:595
  104.5 18.6 %all-to-all-start.2 = ((bf16[4,2,128,512]{3,2,1,0:T(8,128)(2,1)}), bf16[4,2,128,512]{3,2,1,0:T(8,128)(2,1)}, u32[]{:S(2)}, u32[]{:S(2)}) async-start(bf16[4,2,128,512]{3,2,1,0:T(8,128)(2,1)} %bitcast.23), calls=%async_computation.2 | async-start | bytes 2097152 | tf_op jit(solution)/shard_map/all_to_all | solution.py:609
  125.4 17.7 %all-to-all-start.3 = ((bf16[4,2,128,512]{3,2,1,0:T(8,128)(2,1)}), bf16[4,2,128,512]{3,2,1,0:T(8,128)(2,1)}, u32[]{:S(2)}, u32[]{:S(2)}) async-start(bf16[4,2,128,512]{3,2,1,0:T(8,128)(2,1)} %sum_blocks.1.dv), calls=%async_computation.3 | async-start | bytes 2097152 | tf_op jit(solution)/shard_map/all_to_all | solution.py:617
  129.7 3.4 %collective-permute-start.5 = (bf16[1024,128]{1,0:T(8,128)(2,1)}, bf16[1024,128]{1,0:T(8,128)(2,1)}, u32[]{:S(2)}, u32[]{:S(2)}) collective-permute-start(bf16[1024,128]{1,0:T(8,128)(2,1)} %get-tuple-element.78.refs_0_), channel_id=1, source_target_pairs={{0,1},{1,0},{2,3},{3,2},{4,5},{5,4},{6,7},{7,6},{8,9},{9,8},{10,11... | collective-permute-start | bytes 786440 | tf_op jit(solution)/shard_map/ppermute | solution.py:589
  131.5 1.9 collective-permute-start.6
  131.6 2.2 collective-permute-start.7
  132.1 2.1 collective-permute-start.8
  149.0 114.0 %all-to-all-start.4 = ((bf16[32,32,512]{2,1,0:T(8,128)(2,1)}), bf16[32,32,512]{2,1,0:T(8,128)(2,1)}, u32[]{:S(2)}, u32[]{:S(2)}) async-start(bf16[32,32,512]{2,1,0:T(8,128)(2,1)} %bitcast.32), calls=%async_computation.4 | async-start | bytes 2097152 | tf_op jit(solution)/shard_map/all_to_all | solution.py:625
  167.2 10.0 %collective-permute-start.13 = (bf16[2,128,512]{2,1,0:T(8,128)(2,1)S(1)}, bf16[2,128,512]{2,1,0:T(8,128)(2,1)S(1)}, u32[]{:S(2)}, u32[]{:S(2)}) collective-permute-start(bf16[2,128,512]{2,1,0:T(8,128)(2,1)S(1)} %get-tuple-element.101), channel_id=1, source_target_pairs={{2,0},{3,1},{4,2},{5,3},{6,4},{7,5},{10,8},{11,9},{12,10},{13,11},... | collective-permute-start | bytes 786440 | tf_op jit(solution)/shard_map/ppermute | solution.py:598
  168.5 13.2 %collective-permute-start.14 = (bf16[2,128,512]{2,1,0:T(8,128)(2,1)S(1)}, bf16[2,128,512]{2,1,0:T(8,128)(2,1)S(1)}, u32[]{:S(2)}, u32[]{:S(2)}) collective-permute-start(bf16[2,128,512]{2,1,0:T(8,128)(2,1)S(1)} %get-tuple-element.100), channel_id=1, source_target_pairs={{4,0},{5,1},{6,2},{7,3},{12,8},{13,9},{14,10},{15,11},{20,16},{21,... | collective-permute-start | bytes 786440 | tf_op jit(solution)/shard_map/ppermute | solution.py:598
  169.8 17.9 %collective-permute-start.15 = (bf16[2,128,512]{2,1,0:T(8,128)(2,1)S(1)}, bf16[2,128,512]{2,1,0:T(8,128)(2,1)S(1)}, u32[]{:S(2)}, u32[]{:S(2)}) collective-permute-start(bf16[2,128,512]{2,1,0:T(8,128)(2,1)S(1)} %get-tuple-element.99), channel_id=1, source_target_pairs={{6,0},{7,1},{14,8},{15,9},{22,16},{23,17},{30,24},{31,25},{38,32},... | collective-permute-start | bytes 786440 | tf_op jit(solution)/shard_map/ppermute | solution.py:598
  171.1 25.2 %collective-permute-start.10 = (bf16[128,2048]{1,0:T(8,128)(2,1)}, bf16[128,2048]{1,0:T(8,128)(2,1)S(1)}, u32[]{:S(2)}, u32[]{:S(2)}) collective-permute-start(bf16[128,2048]{1,0:T(8,128)(2,1)} %get-tuple-element.88), channel_id=1, source_target_pairs={{0,1},{1,0},{2,3},{3,2},{4,5},{5,4},{6,7},{7,6},{8,9},{9,8},{10,11... | collective-permute-start | bytes 1572872 | tf_op jit(solution)/shard_map/ppermute | solution.py:589
  171.5 24.8 %collective-permute-start.11 = (bf16[128,2048]{1,0:T(8,128)(2,1)}, bf16[128,2048]{1,0:T(8,128)(2,1)S(1)}, u32[]{:S(2)}, u32[]{:S(2)}) collective-permute-start(bf16[128,2048]{1,0:T(8,128)(2,1)} %get-tuple-element.89), channel_id=1, source_target_pairs={{0,1},{1,0},{2,3},{3,2},{4,5},{5,4},{6,7},{7,6},{8,9},{9,8},{10,11... | collective-permute-start | bytes 1572872 | tf_op jit(solution)/shard_map/ppermute | solution.py:589
  177.2 10.5 %copy-start.13 = (bf16[2,128,512]{2,1,0:T(8,128)(2,1)}, bf16[2,128,512]{2,1,0:T(8,128)(2,1)S(1)}, u32[]{:S(2)}) copy-start(bf16[2,128,512]{2,1,0:T(8,128)(2,1)S(1)} %collective-permute-done.13.r1) | copy-start | bytes 786436
  177.2 19.1 %collective-permute-start.12 = (bf16[128,2048]{1,0:T(8,128)(2,1)}, bf16[128,2048]{1,0:T(8,128)(2,1)S(1)}, u32[]{:S(2)}, u32[]{:S(2)}) collective-permute-start(bf16[128,2048]{1,0:T(8,128)(2,1)} %get-tuple-element.90), channel_id=1, source_target_pairs={{0,1},{1,0},{2,3},{3,2},{4,5},{5,4},{6,7},{7,6},{8,9},{9,8},{10,11... | collective-permute-start | bytes 1572872 | tf_op jit(solution)/shard_map/ppermute | solution.py:589
  181.7 14.6 %collective-permute-start.9 = (bf16[128,2048]{1,0:T(8,128)(2,1)}, bf16[128,2048]{1,0:T(8,128)(2,1)S(1)}, u32[]{:S(2)}, u32[]{:S(2)}) collective-permute-start(bf16[128,2048]{1,0:T(8,128)(2,1)} %get-tuple-element.87), channel_id=1, source_target_pairs={{0,1},{1,0},{2,3},{3,2},{4,5},{5,4},{6,7},{7,6},{8,9},{9,8},{10,11... | collective-permute-start | bytes 1572872 | tf_op jit(solution)/shard_map/ppermute | solution.py:589
  191.2 1.8 collective-permute-start.16
  (15 other events, 49.2 us)

commit v4 on v3

--- a/solution.py
+++ b/solution.py
@@ -342,7 +342,7 @@
 
 
 def weight_partial(place, x_own, x_other, dv):
-    tall, wide, step = x_own[0].shape[0], dv.shape[3], 256
+    tall, wide, step = x_own[0].shape[0], dv.shape[3], 1024
     x_spec = pl.BlockSpec((step, BLK), lambda i, place: (i, 0))
     return pl.pallas_call(
         weight_kernel,
@@ -354,7 +354,7 @@
             scratch_shapes=[pltpu.VMEM((step, 2 * NZ * BLK), LOW)],
         ),
         out_shape=jax.ShapeDtypeStruct((tall, wide), LOW),
-        compiler_params=pltpu.CompilerParams(vmem_limit_bytes=60 * 2**20),
+        compiler_params=pltpu.CompilerParams(vmem_limit_bytes=24 * 2**20),
         cost_estimate=LIGHT,
         name="weight_partial",
     )(place, *x_own, *x_other, dv)
@@ -383,66 +383,51 @@
     )(rows)
 
 
-def run_copies(pairs, done):
-    copies = [pltpu.make_async_copy(a, b, done.at[i]) for i, (a, b) in enumerate(pairs)]
-    for copy in copies:
-        copy.start()
-    for copy in copies:
-        copy.wait()
-
-
-def partner_kernel(place, q, g, q_out, g_out, done):
-    width = HALF * QW
-    at = pl.multiple_of((1 - place[1]) * width, width)
-    step = BLK // 4
-    pairs = []
-    for a, b in ((q, q_out), (g, g_out)):
-        for i in range(4):
-            rows = pl.ds(i * step, step)
-            pairs.append((a.at[rows, pl.ds(at, width)], b.at[rows, :]))
-    run_copies(pairs, done)
+def partner_kernel(place, q, g, q_out, g_out):
+    q_out[...] = q[...]
+    g_out[...] = g[...]
 
 
 def partner_halves(place, q, g):
-    out = jax.ShapeDtypeStruct((BLK, HALF * QW), LOW)
-    anywhere = pl.BlockSpec(memory_space=pl.ANY)
+    src = pl.BlockSpec((BLK, QW), lambda i, place: (0, (1 - place[1]) * HALF + i))
+    dst = pl.BlockSpec((BLK, QW), lambda i, place: (0, i))
     return pl.pallas_call(
         partner_kernel,
         grid_spec=pltpu.PrefetchScalarGridSpec(
-            num_scalar_prefetch=1,
-            grid=(1,),
-            in_specs=[anywhere] * 2,
-            out_specs=[anywhere] * 2,
-            scratch_shapes=[pltpu.SemaphoreType.DMA((8,))],
+            num_scalar_prefetch=1, grid=(HALF,), in_specs=[src] * 2, out_specs=[dst] * 2
         ),
-        out_shape=[out, out],
+        out_shape=[jax.ShapeDtypeStruct((BLK, HALF * QW), LOW)] * 2,
         cost_estimate=LIGHT,
         name="partner_halves",
     )(place, q, g)
 
 
-def fill_kernel(place, o_before, dq_before, o_a, o_b, dq_a, dq_b, o_all, dq_all, done):
-    width = NG * QW
-    pairs = []
-    for whole, parts in ((o_all, (o_a, o_b)), (dq_all, (dq_a, dq_b))):
-        for i, part in enumerate(parts):
-            at = pl.multiple_of((1 - place[1]) * HALF * QW + i * width, width)
-            for j in range(2):
-                rows = pl.ds(j * BLK // 2, BLK // 2)
-                pairs.append((part.at[rows, :], whole.at[rows, pl.ds(at, width)]))
-    run_copies(pairs, done)
+def fill_kernel(place, o_before, dq_before, o_a, o_b, dq_a, dq_b, o_all, dq_all):
+    early = pl.program_id(0) < NG
+
+    @pl.when(early)
+    def _():
+        o_all[...] = o_a[...]
+        dq_all[...] = dq_a[...]
+
+    @pl.when(jnp.logical_not(early))
+    def _():
+        o_all[...] = o_b[...]
+        dq_all[...] = dq_b[...]
 
 
 def fill_partner(place, o_all, dq_all, o_parts, dq_parts):
     anywhere = pl.BlockSpec(memory_space=pl.ANY)
+    first = pl.BlockSpec((BLK, QW), lambda i, place: (0, jnp.minimum(i, NG - 1)))
+    second = pl.BlockSpec((BLK, QW), lambda i, place: (0, jnp.maximum(i - NG, 0)))
+    whole = pl.BlockSpec((BLK, QW), lambda i, place: (0, (1 - place[1]) * HALF + i))
     return pl.pallas_call(
         fill_kernel,
         grid_spec=pltpu.PrefetchScalarGridSpec(
             num_scalar_prefetch=1,
-            grid=(1,),
-            in_specs=[anywhere] * 6,
-            out_specs=[anywhere] * 2,
-            scratch_shapes=[pltpu.SemaphoreType.DMA((8,))],
+            grid=(HALF,),
+            in_specs=[anywhere, anywhere, first, second, first, second],
+            out_specs=[whole, whole],
         ),
         out_shape=[jax.ShapeDtypeStruct(o_all.shape, LOW)] * 2,
         input_output_aliases={1: 0, 2: 1},
@@ -617,6 +602,7 @@
     dv_all = lax.all_to_all(dv_sends, "dp", 0, 0, axis_index_groups=along_z)
     o_own, o_par, dq_own, dq_par, dk = output_and_gradients(1, (o_own, dq_own, dk), *args)
     o_pars, dq_pars = o_pars + [o_par], dq_pars + [dq_par]
+    dv_all, dk = lax.optimization_barrier((dv_all, dk))
     dk = dk.reshape(NY, 2, BLK, HALF * HD)
     received = [earlier(pick(dk, jnp.maximum(y - d, 0)), d) for d in range(1, NY)]
     partial = weight_partial(place, x_own, x_other, dv_all).reshape(2 * NX * NY, -1, HALF * HD)

time: 267 us -> 144 us (0.54)
  Pallas kernels: 177 us -> 54.2 us
  waiting for transfers between devices: 36.6 us -> 28.1 us
  starting transfers between devices: 42.6 us -> 46.8 us
  local copies, waits for them, and re-layouts: 6.99 us -> 11 us
    pallas_call x1, Pallas kernels: 65.4 us -> 4.42 us  [partner_halves(): pl.pallas_call(partner_kernel, grid_spec=pltpu.PrefetchScalarGridSpec(num...]
    pallas_call x1, Pallas kernels: 65.4 us -> 4.75 us  [fill_partner(): pl.pallas_call(fill_kernel, grid_spec=pltpu.PrefetchScalarGridSpec(num_sc...]
    all_to_all x1, waiting for transfers between devices: 8.93 us -> 0.01 us  [per_device(): dv_all = lax.all_to_all(dv_sends, 'dp', 0, 0, axis_index_groups=along_z)]
    ppermute x3, waiting for transfers between devices: 14.1 us -> 20.5 us  [earlier(): lax.ppermute(a, 'ctx', [(i + 2 * d, i) for i in range(SLOTS - 2 * d)])]
    unnamed x34 -> x48, local copies, waits for them, and re-layouts: 6.94 us -> 10.9 us
    ppermute x11, waiting for transfers between devices: 3.41 us -> 0.03 us  [swap(): return lax.ppermute(a, 'ctx', [(i, i ^ 1) for i in range(SLOTS)])]
  transfers between devices with their start and end apart: 22 -> 22, of which waited for: 11 -> 6; matrix products, arithmetic and copies ran while one was open for 0% -> 1% of each run, Pallas kernels for 62% -> 30%
where the time goes in v4:
time: 144 us; the launch traced here: 142 us
  Pallas kernels  54.2 us (38%)
  starting transfers between devices  46.8 us (32%)
  waiting for transfers between devices  28.1 us (20%)
  local copies, waits for them, and re-layouts  11 us (8%)
    ppermute x3, waiting for transfers between devices, earlier(): lax.ppermute(a, 'ctx', [(i + 2 * d, i) for i in range(SLOTS - 2 * d)])  20.5 us
    pallas_call x2, Pallas kernels, output_and_gradients(): attention_call(output_onward_kernel if before else output_kernel, 'tree_o...  15.4 us
    unnamed x48, local copies, waits for them, and re-layouts  10.9 us
    all_to_all x1, starting transfers between devices, per_device(): lax.all_to_all(partial, ('dp', 'ctx'), 0, 0, axis_index_groups=across)  9.32 us
    pallas_call x1, Pallas kernels, value_gradient(): attention_call(values_kernel, 'tree_values', HALF // NG, [own, partner, o...  7.66 us
    ppermute x3, starting transfers between devices, further(): lax.ppermute(a, 'dp', [(i, i // NZ * NZ + (i + d) % NZ) for i in range(NX...  7.36 us
    all_to_all x1, starting transfers between devices, per_device(): keys = lax.all_to_all(halves(k), 'ctx', 0, 0)  5.98 us
    ppermute x11, starting transfers between devices, swap(): return lax.ppermute(a, 'ctx', [(i, i ^ 1) for i in range(SLOTS)])  5.97 us
  transfers between devices with their start and end apart: 22, of which 6 were waited for; matrix products, arithmetic and copies ran while one was open for 1% of the time, Pallas kernels for 30%

profile of v4, /device:TPU:1, one launch (start us, length us, event | category | flops | bytes accessed | tf_op | source)
XLA Modules:
  0.0 141.7 jit_solution(18219652834658371015)
XLA Ops:
  0.6 2.0 %halves.2 = bf16[8,128,512]{2,1,0:T(8,128)(2,1)} custom-call(bf16[128,1024]{1,0:T(8,128)(2,1)} %bitcast.35), custom_call_target="tpu_custom_call" | custom-call | flops 1 | bytes 1 | tf_op jit(solution)/shard_map/halves/pallas_call | solution.py:376
  2.7 6.0 %all-to-all-start = ((bf16[8,128,512]{2,1,0:T(8,128)(2,1)}), bf16[8,128,512]{2,1,0:T(8,128)(2,1)S(1)}, u32[]{:S(2)}, u32[]{:S(2)}) async-start(bf16[8,128,512]{2,1,0:T(8,128)(2,1)} %halves.2), calls=%async_computation | async-start | bytes 2097152 | tf_op jit(solution)/shard_map/all_to_all | solution.py:585
  9.3 3.1 %x_sends.1 = (bf16[1024,128]{1,0:T(8,128)(2,1)}, bf16[1024,128]{1,0:T(8,128)(2,1)}, bf16[1024,128]{1,0:T(8,128)(2,1)}, bf16[1024,128]{1,0:T(8,128)(2,1)}) custom-call(s32[3]{0:T(128)} %pad_add_fusion.place.refs_0_, bf16[128,4096]{1,0:T(8,128)(2,1)} %bitcast.34), custom_call_target="tpu_custom_call" | custom-call | flops 1 | bytes 1 | tf_op jit(solution)/shard_map/x_sends/pallas_call | solution.py:501
  14.0 2.1 %collective-permute-start.3 = (bf16[1024,128]{1,0:T(8,128)(2,1)}, bf16[1024,128]{1,0:T(8,128)(2,1)}, u32[]{:S(2)}, u32[]{:S(2)}) collective-permute-start(bf16[1024,128]{1,0:T(8,128)(2,1)} %get-tuple-element.57), channel_id=1, source_target_pairs={{0,24},{8,0},{16,8},{24,16},{32,56},{40,32},{48,40},{56,48},{64,88... | collective-permute-start | bytes 786440 | tf_op jit(solution)/shard_map/ppermute | solution.py:580
  16.1 4.4 %partner_halves.1 = (bf16[128,4096]{1,0:T(8,128)(2,1)}, bf16[128,4096]{1,0:T(8,128)(2,1)}) custom-call(s32[3]{0:T(128)} %pad_add_fusion.place.refs_0_, bf16[128,8192]{1,0:T(8,128)(2,1)} %bitcast.24, bf16[128,8192]{1,0:T(8,128)(2,1)} %bitcast.28), custom_call_target="tpu_custom_call" | custom-call | flops 1 | bytes 1 | tf_op jit(solution)/shard_map/partner_halves/pallas_call | solution.py:394
  23.8 5.0 %all-to-all-start.1 = ((bf16[8,128,512]{2,1,0:T(8,128)(2,1)}), bf16[8,128,512]{2,1,0:T(8,128)(2,1)}, u32[]{:S(2)}, u32[]{:S(2)}) async-start(bf16[8,128,512]{2,1,0:T(8,128)(2,1)} %halves.3), calls=%async_computation.1 | async-start | bytes 2097152 | tf_op jit(solution)/shard_map/all_to_all | solution.py:591
  28.8 3.6 %collective-permute-start.4 = (bf16[1024,128]{1,0:T(8,128)(2,1)}, bf16[1024,128]{1,0:T(8,128)(2,1)}, u32[]{:S(2)}, u32[]{:S(2)}) collective-permute-start(bf16[1024,128]{1,0:T(8,128)(2,1)} %get-tuple-element.63), channel_id=1, source_target_pairs={{0,16},{8,24},{16,0},{24,8},{32,48},{40,56},{48,32},{56,40},{64,80... | collective-permute-start | bytes 786440 | tf_op jit(solution)/shard_map/ppermute | solution.py:580
  32.4 7.7 %tree_values.1 = (bf16[8,128,512]{2,1,0:T(8,128)(2,1)S(1)}, f32[4,2,8,1024]{3,2,1,0:T(8,128)S(1)}) custom-call(s32[3]{0:T(128)S(1)} %copy-done.8, s32[1,8]{1,0:T(1,128)S(1)} %copy-done.9, s32[1,8]{1,0:T(1,128)S(1)} %copy-done.10, bf16[128,8192]{1,0:T(8,128)(2,1)} %bitcast.25, bf16[128,4096]{1,0:T(8,128)(2,1)S(1)} %collective-permute-done.q_par.refs_4_, ...), custom_call_target="tpu_custom_call" | custom-call | flops 1 | bytes 1 | tf_op jit(solution)/shard_map/tree_values/pallas_call | solution.py:286
  41.0 2.9 %all-to-all-done.1.vals.refs_8_ = bf16[8,128,512]{2,1,0:T(8,128)(2,1)} async-done(((bf16[8,128,512]{2,1,0:T(8,128)(2,1)}), bf16[8,128,512]{2,1,0:T(8,128)(2,1)}, u32[]{:S(2)}, u32[]{:S(2)}) %all-to-all-start.1) | async-done | bytes 1048608 | tf_op jit(solution)/shard_map/all_to_all | solution.py:591
  44.0 4.2 %all-to-all-start.2 = ((bf16[4,2,128,512]{3,2,1,0:T(8,128)(2,1)}), bf16[4,2,128,512]{3,2,1,0:T(8,128)(2,1)}, u32[]{:S(2)}, u32[]{:S(2)}) async-start(bf16[4,2,128,512]{3,2,1,0:T(8,128)(2,1)} %bitcast.23), calls=%async_computation.2 | async-start | bytes 2097152 | tf_op jit(solution)/shard_map/all_to_all | solution.py:594
  48.2 7.7 %tree_outputs.2 = (bf16[128,8192]{1,0:T(8,128)(2,1)}, bf16[128,2048]{1,0:T(8,128)(2,1)S(1)}, bf16[128,8192]{1,0:T(8,128)(2,1)}, bf16[128,2048]{1,0:T(8,128)(2,1)S(1)}, bf16[8,128,512]{2,1,0:T(8,128)(2,1)S(1)}) custom-call(s32[3]{0:T(128)S(1)} %copy-done.8, s32[1,8]{1,0:T(1,128)S(1)} %copy-done.9, s32[1,8]{1,0:T(1,128)S(1)} %copy-done.10, ...), custom_call_target="tpu_custom_call" | custom-call | flops 1 | bytes 1 | tf_op jit(solution)/shard_map/tree_outputs/pallas_call | solution.py:309
  58.5 4.1 %all-to-all-done.2.terms = bf16[4,2,128,512]{3,2,1,0:T(8,128)(2,1)} async-done(((bf16[4,2,128,512]{3,2,1,0:T(8,128)(2,1)}), bf16[4,2,128,512]{3,2,1,0:T(8,128)(2,1)}, u32[]{:S(2)}, u32[]{:S(2)}) %all-to-all-start.2) | async-done | bytes 1048608 | tf_op jit(solution)/shard_map/all_to_all | solution.py:594
  62.6 2.4 %sum_blocks.1.dv = bf16[4,2,128,512]{3,2,1,0:T(8,128)(2,1)} custom-call(bf16[4,2,128,512]{3,2,1,0:T(8,128)(2,1)} %all-to-all-done.2.terms), custom_call_target="tpu_custom_call" | custom-call | flops 1 | bytes 1 | tf_op jit(solution)/shard_map/sum_blocks/pallas_call | solution.py:529
  64.9 5.0 %all-to-all-start.3 = ((bf16[4,2,128,512]{3,2,1,0:T(8,128)(2,1)}), bf16[4,2,128,512]{3,2,1,0:T(8,128)(2,1)}, u32[]{:S(2)}, u32[]{:S(2)}) async-start(bf16[4,2,128,512]{3,2,1,0:T(8,128)(2,1)} %sum_blocks.1.dv), calls=%async_computation.3 | async-start | bytes 2097152 | tf_op jit(solution)/shard_map/all_to_all | solution.py:602
  70.0 2.1 %collective-permute-start.5 = (bf16[1024,128]{1,0:T(8,128)(2,1)}, bf16[1024,128]{1,0:T(8,128)(2,1)}, u32[]{:S(2)}, u32[]{:S(2)}) collective-permute-start(bf16[1024,128]{1,0:T(8,128)(2,1)} %get-tuple-element.80.refs_0_), channel_id=1, source_target_pairs={{0,1},{1,0},{2,3},{3,2},{4,5},{5,4},{6,7},{7,6},{8,9},{9,8},{10,11... | collective-permute-start | bytes 786440 | tf_op jit(solution)/shard_map/ppermute | solution.py:574
  73.8 7.7 %tree_outputs.3 = (bf16[128,8192]{1,0:T(8,128)(2,1)}, bf16[128,2048]{1,0:T(8,128)(2,1)S(1)}, bf16[128,8192]{1,0:T(8,128)(2,1)}, bf16[128,2048]{1,0:T(8,128)(2,1)S(1)}, bf16[8,128,512]{2,1,0:T(8,128)(2,1)S(1)}) custom-call(s32[3]{0:T(128)S(1)} %copy-done.8, s32[1,8]{1,0:T(1,128)S(1)} %copy-done.9, ...), custom_call_target="tpu_custom_call", output_to_operand_aliasing={{0}: (10, {}), {2}: (11, {}), {4}: (12, {})} | custom-call | flops 1 | bytes 1 | tf_op jit(solution)/shard_map/tree_outputs/pallas_call | solution.py:309
  86.0 5.2 %weight_partial.1 = bf16[1024,512]{1,0:T(8,128)(2,1)} custom-call(s32[3]{0:T(128)S(1)} %copy-done.8, bf16[1024,128]{1,0:T(8,128)(2,1)S(1)} %copy-done.5, bf16[1024,128]{1,0:T(8,128)(2,1)S(1)} %copy-done.7, bf16[1024,128]{1,0:T(8,128)(2,1)} %collective-permute-done.4.refs_2_, bf16[1024,128]{1,0:T(8,128)(2,1)} %collective-permute-done.3.refs_3_, ...), custom_call_target="tpu_custom_call" | custom-call | flops 1 | bytes 1 | tf_op jit(solution)/shard_map/weight_partial/pallas_call | solution.py:347
  91.2 9.3 %all-to-all-start.4 = ((bf16[32,32,512]{2,1,0:T(8,128)(2,1)}), bf16[32,32,512]{2,1,0:T(8,128)(2,1)}, u32[]{:S(2)}, u32[]{:S(2)}) async-start(bf16[32,32,512]{2,1,0:T(8,128)(2,1)} %bitcast.9.after), calls=%async_computation.4 | async-start | bytes 2097152 | tf_op jit(solution)/shard_map/all_to_all | solution.py:611
  105.1 14.6 %collective-permute-done.13.r1 = bf16[2,128,512]{2,1,0:T(8,128)(2,1)S(1)} collective-permute-done((bf16[2,128,512]{2,1,0:T(8,128)(2,1)S(1)}, bf16[2,128,512]{2,1,0:T(8,128)(2,1)S(1)}, u32[]{:S(2)}, u32[]{:S(2)}) %collective-permute-start.13) | collective-permute-done | bytes 262176 | tf_op jit(solution)/shard_map/ppermute | solution.py:583
  122.3 5.1 %collective-permute-done.15.r3 = bf16[2,128,512]{2,1,0:T(8,128)(2,1)} collective-permute-done((bf16[2,128,512]{2,1,0:T(8,128)(2,1)S(1)}, bf16[2,128,512]{2,1,0:T(8,128)(2,1)}, u32[]{:S(2)}, u32[]{:S(2)}) %collective-permute-start.15) | collective-permute-done | bytes 262176 | tf_op jit(solution)/shard_map/ppermute | solution.py:583
  127.3 2.8 %split_grads.1 = (bf16[2,128,512]{2,1,0:T(8,128)(2,1)}, bf16[2,128,512]{2,1,0:T(8,128)(2,1)}) custom-call(s32[3]{0:T(128)} %pad_add_fusion.place.refs_0_, bf16[4,2,128,512]{3,2,1,0:T(8,128)(2,1)} %bitcast.21, bf16[2,128,512]{2,1,0:T(8,128)(2,1)} %copy-done.21, bf16[2,128,512]{2,1,0:T(8,128)(2,1)} %copy-done.22, ...), custom_call_target="tpu_custom_call" | custom-call | flops 1 | bytes 1 | tf_op jit(solution)/shard_map/split_grads/pallas_call | solution.py:452
  131.7 4.7 %fill_partner.1 = (bf16[128,8192]{1,0:T(8,128)(2,1)}, bf16[128,8192]{1,0:T(8,128)(2,1)}) custom-call(s32[3]{0:T(128)} %pad_add_fusion.place.refs_0_, bf16[128,8192]{1,0:T(8,128)(2,1)} %get-tuple-element.78.o_before, bf16[128,8192]{1,0:T(8,128)(2,1)} %get-tuple-element.79.dq_before, ...), custom_call_target="tpu_custom_call", output_to_operand_aliasing={{0}: (1, {}), {1}: (2, {})} | custom-call | flops 1 | bytes 1 | tf_op jit(solution)/shard_map/fill_partner/pallas_call | solution.py:424
  137.1 2.5 %join_grads.1 = (bf16[128,1024]{1,0:T(8,128)(2,1)}, bf16[128,1024]{1,0:T(8,128)(2,1)}) custom-call(s32[3]{0:T(128)} %pad_add_fusion.place.refs_0_, bf16[2,128,512]{2,1,0:T(8,128)(2,1)} %get-tuple-element.99.mine, bf16[2,128,512]{2,1,0:T(8,128)(2,1)} %copy-done.23), custom_call_target="tpu_custom_call" | custom-call | flops 1 | bytes 1 | tf_op jit(solution)/shard_map/join_grads/pallas_call | solution.py:479
  139.6 2.0 %finish_weight.1 = f32[32,1024]{1,0:T(8,128)} custom-call(bf16[32,32,512]{2,1,0:T(8,128)(2,1)} %all-to-all-done.4.parts), custom_call_target="tpu_custom_call" | custom-call | flops 1 | bytes 1 | tf_op jit(solution)/shard_map/finish_weight/pallas_call | solution.py:551
  (83 shorter events, 24.6 us)
Async XLA Ops:
  2.7 21.1 %all-to-all-start = ((bf16[8,128,512]{2,1,0:T(8,128)(2,1)}), bf16[8,128,512]{2,1,0:T(8,128)(2,1)S(1)}, u32[]{:S(2)}, u32[]{:S(2)}) async-start(bf16[8,128,512]{2,1,0:T(8,128)(2,1)} %halves.2), calls=%async_computation | async-start | bytes 2097152 | tf_op jit(solution)/shard_map/all_to_all | solution.py:585
  12.4 10.8 %collective-permute-start.2 = (bf16[1024,128]{1,0:T(8,128)(2,1)}, bf16[1024,128]{1,0:T(8,128)(2,1)S(1)}, u32[]{:S(2)}, u32[]{:S(2)}) collective-permute-start(bf16[1024,128]{1,0:T(8,128)(2,1)} %get-tuple-element.56), channel_id=1, source_target_pairs={{0,8},{8,16},{16,24},{24,0},{32,40},{40,48},{48,56},{56,32},{64,72... | collective-permute-start | bytes 786440 | tf_op jit(solution)/shard_map/ppermute | solution.py:580
  14.0 9.2 %collective-permute-start.3 = (bf16[1024,128]{1,0:T(8,128)(2,1)}, bf16[1024,128]{1,0:T(8,128)(2,1)}, u32[]{:S(2)}, u32[]{:S(2)}) collective-permute-start(bf16[1024,128]{1,0:T(8,128)(2,1)} %get-tuple-element.57), channel_id=1, source_target_pairs={{0,24},{8,0},{16,8},{24,16},{32,56},{40,32},{48,40},{56,48},{64,88... | collective-permute-start | bytes 786440 | tf_op jit(solution)/shard_map/ppermute | solution.py:580
  20.6 11.8 %collective-permute-start = (bf16[128,4096]{1,0:T(8,128)(2,1)}, bf16[128,4096]{1,0:T(8,128)(2,1)S(1)}, u32[]{:S(2)}, u32[]{:S(2)}) collective-permute-start(bf16[128,4096]{1,0:T(8,128)(2,1)} %get-tuple-element.54), channel_id=1, source_target_pairs={{0,1},{1,0},{2,3},{3,2},{4,5},{5,4},{6,7},{7,6},{8,9},{9,8},{10,11... | collective-permute-start | bytes 3145736 | tf_op jit(solution)/shard_map/ppermute | solution.py:574
  20.9 11.4 %collective-permute-start.1 = (bf16[128,4096]{1,0:T(8,128)(2,1)}, bf16[128,4096]{1,0:T(8,128)(2,1)S(1)}, u32[]{:S(2)}, u32[]{:S(2)}) collective-permute-start(bf16[128,4096]{1,0:T(8,128)(2,1)} %get-tuple-element.55), channel_id=1, source_target_pairs={{0,1},{1,0},{2,3},{3,2},{4,5},{5,4},{6,7},{7,6},{8,9},{9,8},{10,11... | collective-permute-start | bytes 3145736 | tf_op jit(solution)/shard_map/ppermute | solution.py:574
  23.8 20.2 %all-to-all-start.1 = ((bf16[8,128,512]{2,1,0:T(8,128)(2,1)}), bf16[8,128,512]{2,1,0:T(8,128)(2,1)}, u32[]{:S(2)}, u32[]{:S(2)}) async-start(bf16[8,128,512]{2,1,0:T(8,128)(2,1)} %halves.3), calls=%async_computation.1 | async-start | bytes 2097152 | tf_op jit(solution)/shard_map/all_to_all | solution.py:591
  28.8 12.3 %collective-permute-start.4 = (bf16[1024,128]{1,0:T(8,128)(2,1)}, bf16[1024,128]{1,0:T(8,128)(2,1)}, u32[]{:S(2)}, u32[]{:S(2)}) collective-permute-start(bf16[1024,128]{1,0:T(8,128)(2,1)} %get-tuple-element.63), channel_id=1, source_target_pairs={{0,16},{8,24},{16,0},{24,8},{32,48},{40,56},{48,32},{56,40},{64,80... | collective-permute-start | bytes 786440 | tf_op jit(solution)/shard_map/ppermute | solution.py:580
  44.0 18.6 %all-to-all-start.2 = ((bf16[4,2,128,512]{3,2,1,0:T(8,128)(2,1)}), bf16[4,2,128,512]{3,2,1,0:T(8,128)(2,1)}, u32[]{:S(2)}, u32[]{:S(2)}) async-start(bf16[4,2,128,512]{3,2,1,0:T(8,128)(2,1)} %bitcast.23), calls=%async_computation.2 | async-start | bytes 2097152 | tf_op jit(solution)/shard_map/all_to_all | solution.py:594
  64.9 19.1 %all-to-all-start.3 = ((bf16[4,2,128,512]{3,2,1,0:T(8,128)(2,1)}), bf16[4,2,128,512]{3,2,1,0:T(8,128)(2,1)}, u32[]{:S(2)}, u32[]{:S(2)}) async-start(bf16[4,2,128,512]{3,2,1,0:T(8,128)(2,1)} %sum_blocks.1.dv), calls=%async_computation.3 | async-start | bytes 2097152 | tf_op jit(solution)/shard_map/all_to_all | solution.py:602
  70.0 14.1 %collective-permute-start.5 = (bf16[1024,128]{1,0:T(8,128)(2,1)}, bf16[1024,128]{1,0:T(8,128)(2,1)}, u32[]{:S(2)}, u32[]{:S(2)}) collective-permute-start(bf16[1024,128]{1,0:T(8,128)(2,1)} %get-tuple-element.80.refs_0_), channel_id=1, source_target_pairs={{0,1},{1,0},{2,3},{3,2},{4,5},{5,4},{6,7},{7,6},{8,9},{9,8},{10,11... | collective-permute-start | bytes 786440 | tf_op jit(solution)/shard_map/ppermute | solution.py:574
  72.0 12.0 %collective-permute-start.6 = (bf16[1024,128]{1,0:T(8,128)(2,1)}, bf16[1024,128]{1,0:T(8,128)(2,1)}, u32[]{:S(2)}, u32[]{:S(2)}) collective-permute-start(bf16[1024,128]{1,0:T(8,128)(2,1)} %copy-done.6), channel_id=1, source_target_pairs={{0,1},{1,0},{2,3},{3,2},{4,5},{5,4},{6,7},{7,6},{8,9},{9,8},{10,11... | collective-permute-start | bytes 786440 | tf_op jit(solution)/shard_map/ppermute | solution.py:574
  72.0 12.0 %collective-permute-start.7 = (bf16[1024,128]{1,0:T(8,128)(2,1)}, bf16[1024,128]{1,0:T(8,128)(2,1)}, u32[]{:S(2)}, u32[]{:S(2)}) collective-permute-start(bf16[1024,128]{1,0:T(8,128)(2,1)} %collective-permute-done.4.refs_2_), channel_id=1, source_target_pairs={{0,1},{1,0},{2,3},{3,2},{4,5},{5,4},{6,7},{7,6},{8,9},{9,8},{10,11... | collective-permute-start | bytes 786440 | tf_op jit(solution)/shard_map/ppermute | solution.py:574
  72.5 11.5 %collective-permute-start.8 = (bf16[1024,128]{1,0:T(8,128)(2,1)}, bf16[1024,128]{1,0:T(8,128)(2,1)}, u32[]{:S(2)}, u32[]{:S(2)}) collective-permute-start(bf16[1024,128]{1,0:T(8,128)(2,1)} %collective-permute-done.3.refs_3_), channel_id=1, source_target_pairs={{0,1},{1,0},{2,3},{3,2},{4,5},{5,4},{6,7},{7,6},{8,9},{9,8},{10,11... | collective-permute-start | bytes 786440 | tf_op jit(solution)/shard_map/ppermute | solution.py:574
  91.2 28.5 %copy-start.16 = (bf16[128,2048]{1,0:T(8,128)(2,1)S(1)}, bf16[128,2048]{1,0:T(8,128)(2,1)}, u32[]{:S(2)}) copy-start(bf16[128,2048]{1,0:T(8,128)(2,1)} %copy-done.15) | copy-start | bytes 1572868
  91.2 30.2 %copy-start.12 = (bf16[128,2048]{1,0:T(8,128)(2,1)S(1)}, bf16[128,2048]{1,0:T(8,128)(2,1)}, u32[]{:S(2)}) copy-start(bf16[128,2048]{1,0:T(8,128)(2,1)} %copy-done.11) | copy-start | bytes 1572868
  91.2 48.4 %all-to-all-start.4 = ((bf16[32,32,512]{2,1,0:T(8,128)(2,1)}), bf16[32,32,512]{2,1,0:T(8,128)(2,1)}, u32[]{:S(2)}, u32[]{:S(2)}) async-start(bf16[32,32,512]{2,1,0:T(8,128)(2,1)} %bitcast.9.after), calls=%async_computation.4 | async-start | bytes 2097152 | tf_op jit(solution)/shard_map/all_to_all | solution.py:611
  100.6 19.1 %collective-permute-start.13 = (bf16[2,128,512]{2,1,0:T(8,128)(2,1)S(1)}, bf16[2,128,512]{2,1,0:T(8,128)(2,1)S(1)}, u32[]{:S(2)}, u32[]{:S(2)}) collective-permute-start(bf16[2,128,512]{2,1,0:T(8,128)(2,1)S(1)} %get-tuple-element.105), channel_id=1, source_target_pairs={{2,0},{3,1},{4,2},{5,3},{6,4},{7,5},{10,8},{11,9},{12,10},{13,11},... | collective-permute-start | bytes 786440 | tf_op jit(solution)/shard_map/ppermute | solution.py:583
  101.9 19.4 %collective-permute-start.14 = (bf16[2,128,512]{2,1,0:T(8,128)(2,1)S(1)}, bf16[2,128,512]{2,1,0:T(8,128)(2,1)S(1)}, u32[]{:S(2)}, u32[]{:S(2)}) collective-permute-start(bf16[2,128,512]{2,1,0:T(8,128)(2,1)S(1)} %get-tuple-element.104), channel_id=1, source_target_pairs={{4,0},{5,1},{6,2},{7,3},{12,8},{13,9},{14,10},{15,11},{20,16},{21,... | collective-permute-start | bytes 786440 | tf_op jit(solution)/shard_map/ppermute | solution.py:583
  103.2 24.1 %collective-permute-start.15 = (bf16[2,128,512]{2,1,0:T(8,128)(2,1)S(1)}, bf16[2,128,512]{2,1,0:T(8,128)(2,1)}, u32[]{:S(2)}, u32[]{:S(2)}) collective-permute-start(bf16[2,128,512]{2,1,0:T(8,128)(2,1)S(1)} %get-tuple-element.103), channel_id=1, source_target_pairs={{6,0},{7,1},{14,8},{15,9},{22,16},{23,17},{30,24},{31,25},{38,32},... | collective-permute-start | bytes 786440 | tf_op jit(solution)/shard_map/ppermute | solution.py:583
  104.5 26.1 %collective-permute-start.10 = (bf16[128,2048]{1,0:T(8,128)(2,1)S(1)}, bf16[128,2048]{1,0:T(8,128)(2,1)S(1)}, u32[]{:S(2)}, u32[]{:S(2)}) collective-permute-start(bf16[128,2048]{1,0:T(8,128)(2,1)S(1)} %copy-done.18), channel_id=1, source_target_pairs={{0,1},{1,0},{2,3},{3,2},{4,5},{5,4},{6,7},{7,6},{8,9},{9,8},{10,11... | collective-permute-start | bytes 1572872 | tf_op jit(solution)/shard_map/ppermute | solution.py:574
  104.9 25.7 %collective-permute-start.11 = (bf16[128,2048]{1,0:T(8,128)(2,1)S(1)}, bf16[128,2048]{1,0:T(8,128)(2,1)S(1)}, u32[]{:S(2)}, u32[]{:S(2)}) collective-permute-start(bf16[128,2048]{1,0:T(8,128)(2,1)S(1)} %copy-done.14), channel_id=1, source_target_pairs={{0,1},{1,0},{2,3},{3,2},{4,5},{5,4},{6,7},{7,6},{8,9},{9,8},{10,11... | collective-permute-start | bytes 1572872 | tf_op jit(solution)/shard_map/ppermute | solution.py:574
  119.7 11.0 %collective-permute-start.12 = (bf16[128,2048]{1,0:T(8,128)(2,1)S(1)}, bf16[128,2048]{1,0:T(8,128)(2,1)}, u32[]{:S(2)}, u32[]{:S(2)}) collective-permute-start(bf16[128,2048]{1,0:T(8,128)(2,1)S(1)} %copy-done.16), channel_id=1, source_target_pairs={{0,1},{1,0},{2,3},{3,2},{4,5},{5,4},{6,7},{7,6},{8,9},{9,8},{10,11... | collective-permute-start | bytes 1572872 | tf_op jit(solution)/shard_map/ppermute | solution.py:574
  121.4 9.3 %collective-permute-start.9 = (bf16[128,2048]{1,0:T(8,128)(2,1)S(1)}, bf16[128,2048]{1,0:T(8,128)(2,1)}, u32[]{:S(2)}, u32[]{:S(2)}) collective-permute-start(bf16[128,2048]{1,0:T(8,128)(2,1)S(1)} %copy-done.12), channel_id=1, source_target_pairs={{0,1},{1,0},{2,3},{3,2},{4,5},{5,4},{6,7},{7,6},{8,9},{9,8},{10,11... | collective-permute-start | bytes 1572872 | tf_op jit(solution)/shard_map/ppermute | solution.py:574
  130.1 6.3 %collective-permute-start.16 = (bf16[2,128,512]{2,1,0:T(8,128)(2,1)}, bf16[2,128,512]{2,1,0:T(8,128)(2,1)S(1)}, u32[]{:S(2)}, u32[]{:S(2)}) collective-permute-start(bf16[2,128,512]{2,1,0:T(8,128)(2,1)} %get-tuple-element.100), channel_id=1, source_target_pairs={{0,1},{1,0},{2,3},{3,2},{4,5},{5,4},{6,7},{7,6},{8,9},{9,8},{10,11... | collective-permute-start | bytes 786440 | tf_op jit(solution)/shard_map/ppermute | solution.py:574
  (22 other events, 101.4 us)

commit v5 on v4

--- a/solution.py
+++ b/solution.py
@@ -259,7 +259,7 @@
         ),
         out_shape=out_shape,
         input_output_aliases=aliases,
-        compiler_params=pltpu.CompilerParams(dimension_semantics=("arbitrary",), vmem_limit_bytes=48 * 2**20),
+        compiler_params=pltpu.CompilerParams(dimension_semantics=("arbitrary",), vmem_limit_bytes=60 * 2**20),
         cost_estimate=LIGHT,
         name=name,
     )
@@ -360,10 +360,12 @@
     )(place, *x_own, *x_other, dv)
 
 
-def halves_kernel(rows, out, done):
-    width = out.shape[2]
+def halves_kernel(k, v, k_out, v_out, done):
+    width = k_out.shape[2]
     copies = [
-        pltpu.make_async_copy(rows.at[:, pl.ds(i % 2 * width, width)], out.at[i], done.at[i]) for i in range(SLOTS)
+        pltpu.make_async_copy(rows.at[:, pl.ds(i % 2 * width, width)], out.at[i], done.at[j, i])
+        for j, (rows, out) in enumerate(((k, k_out), (v, v_out)))
+        for i in range(SLOTS)
     ]
     for copy in copies:
         copy.start()
@@ -371,16 +373,16 @@
         copy.wait()
 
 
-def halves(rows):
-    width = rows.shape[1] // 2
+def halves(k, v):
+    width = k.shape[1] // 2
     return pl.pallas_call(
         halves_kernel,
-        out_shape=jax.ShapeDtypeStruct((SLOTS, BLK, width), LOW),
-        out_specs=pl.BlockSpec(memory_space=pl.ANY),
-        scratch_shapes=[pltpu.SemaphoreType.DMA((SLOTS,))],
+        out_shape=[jax.ShapeDtypeStruct((SLOTS, BLK, width), LOW)] * 2,
+        out_specs=[pl.BlockSpec(memory_space=pl.ANY)] * 2,
+        scratch_shapes=[pltpu.SemaphoreType.DMA((2, SLOTS))],
         cost_estimate=LIGHT,
         name="halves",
-    )(rows)
+    )(k, v)
 
 
 def partner_kernel(place, q, g, q_out, g_out):
@@ -389,12 +391,13 @@
 
 
 def partner_halves(place, q, g):
-    src = pl.BlockSpec((BLK, QW), lambda i, place: (0, (1 - place[1]) * HALF + i))
-    dst = pl.BlockSpec((BLK, QW), lambda i, place: (0, i))
+    steps = 2
+    src = pl.BlockSpec((BLK, HALF * QW // steps), lambda i, place: (0, (1 - place[1]) * steps + i))
+    dst = pl.BlockSpec((BLK, HALF * QW // steps), lambda i, place: (0, i))
     return pl.pallas_call(
         partner_kernel,
         grid_spec=pltpu.PrefetchScalarGridSpec(
-            num_scalar_prefetch=1, grid=(HALF,), in_specs=[src] * 2, out_specs=[dst] * 2
+            num_scalar_prefetch=1, grid=(steps,), in_specs=[src] * 2, out_specs=[dst] * 2
         ),
         out_shape=[jax.ShapeDtypeStruct((BLK, HALF * QW), LOW)] * 2,
         cost_estimate=LIGHT,
@@ -582,10 +585,10 @@
     def earlier(a, d):
         return lax.ppermute(a, "ctx", [(i + 2 * d, i) for i in range(SLOTS - 2 * d)])
 
-    keys = lax.all_to_all(halves(k), "ctx", 0, 0)
+    k_sends, v_sends = halves(k, v)
+    keys = lax.all_to_all(k_sends, "ctx", 0, 0)
     q_par, g_par = [swap(a) for a in partner_halves(place, q, g)]
     x_own = x_sends(place, x)
-    v_sends = halves(v)
     x_own = [x_own[0]] + [further(x_own[d], d) for d in range(1, NZ)]
     keys, v_sends, x_own[1], x_own[3] = lax.optimization_barrier((keys, v_sends, x_own[1], x_own[3]))
     vals = lax.all_to_all(v_sends, "ctx", 0, 0)
@@ -606,11 +609,11 @@
     dk = dk.reshape(NY, 2, BLK, HALF * HD)
     received = [earlier(pick(dk, jnp.maximum(y - d, 0)), d) for d in range(1, NY)]
     partial = weight_partial(place, x_own, x_other, dv_all).reshape(2 * NX * NY, -1, HALF * HD)
-    after, o_pars, dq_pars = lax.optimization_barrier((partial, o_pars, dq_pars))
+    _, o_pars, dq_pars = lax.optimization_barrier((partial, o_pars, dq_pars))
     o_pars, dq_pars = [swap(a) for a in o_pars], [swap(a) for a in dq_pars]
     weight_grad = finish_weight(lax.all_to_all(partial, ("dp", "ctx"), 0, 0, axis_index_groups=across))
     out, query_grad = fill_partner(place, o_own, dq_own, o_pars, dq_pars)
-    mine, other = split_grads(place, dk, received, dv_sends, after)
+    mine, other = split_grads(place, dk, received, dv_sends, query_grad)
     key_grad, value_grad = join_grads(place, mine, swap(other))
     return out[None], query_grad[None], key_grad[None], value_grad[None], weight_grad
 

time: 144 us -> 136 us (0.944); the launches traced: 142 us -> 136 us
  local copies, waits for them, and re-layouts: 11 us -> 4.26 us
  waiting for transfers between devices: 28.1 us -> 31.4 us
  starting transfers between devices: 46.8 us -> 44.7 us
    unnamed x48 -> x28, local copies, waits for them, and re-layouts: 10.9 us -> 3.41 us
    ppermute x3, waiting for transfers between devices: 20.5 us -> 16.9 us  [earlier(): lax.ppermute(a, 'ctx', [(i + 2 * d, i) for i in range(SLOTS - 2 * d)])]
    ppermute x3, waiting for transfers between devices: 0.01 us -> 3.11 us  [further(): lax.ppermute(a, 'dp', [(i, i // NZ * NZ + (i + d) % NZ) for i in range(NX...]
    pallas_call x2, Pallas kernels: 15.4 us -> 17.8 us  [output_and_gradients(): attention_call(output_onward_kernel if before else output_kernel, 'tree_o...]
    all_to_all x1, starting transfers between devices: 9.32 us -> 7.44 us  [per_device(): lax.all_to_all(partial, ('dp', 'ctx'), 0, 0, axis_index_groups=across)]
    pallas_call x1, Pallas kernels: 5.19 us -> 3.46 us  [weight_partial(): pl.pallas_call(weight_kernel, grid_spec=pltpu.PrefetchScalarGridSpec(num_...]
    pallas_call x2 -> x1, Pallas kernels: 4.05 us -> 2.54 us  [halves(): pl.pallas_call(halves_kernel, out_shape=[jax.ShapeDtypeStruct((SLOTS, BLK...]
    pallas_call x1, Pallas kernels: 7.66 us -> 9.11 us  [value_gradient(): attention_call(values_kernel, 'tree_values', HALF // NG, [own, partner, o...]
  transfers between devices with their start and end apart: 22 -> 22, of which waited for: 6 -> 9; matrix products, arithmetic and copies ran while one was open for 1% -> 1% of each run, Pallas kernels for 30% -> 32%
where the time goes in v5:
time: 136 us
  Pallas kernels  53.7 us (39%)
  starting transfers between devices  44.7 us (33%)
  waiting for transfers between devices  31.4 us (23%)
  local copies, waits for them, and re-layouts  4.26 us (3%)
    pallas_call x2, Pallas kernels, output_and_gradients(): attention_call(output_onward_kernel if before else output_kernel, 'tree_o...  17.8 us
    ppermute x3, waiting for transfers between devices, earlier(): lax.ppermute(a, 'ctx', [(i + 2 * d, i) for i in range(SLOTS - 2 * d)])  16.9 us
    pallas_call x1, Pallas kernels, value_gradient(): attention_call(values_kernel, 'tree_values', HALF // NG, [own, partner, o...  9.11 us
    all_to_all x1, starting transfers between devices, per_device(): lax.all_to_all(partial, ('dp', 'ctx'), 0, 0, axis_index_groups=across)  7.44 us
    ppermute x3, starting transfers between devices, further(): lax.ppermute(a, 'dp', [(i, i // NZ * NZ + (i + d) % NZ) for i in range(NX...  7.36 us
    ppermute x11, starting transfers between devices, swap(): return lax.ppermute(a, 'ctx', [(i, i ^ 1) for i in range(SLOTS)])  7.13 us
    all_to_all x1, starting transfers between devices, per_device(): keys = lax.all_to_all(k_sends, 'ctx', 0, 0)  5.98 us
    all_to_all x1, waiting for transfers between devices, per_device(): lax.all_to_all(dv.reshape(NY, 2, BLK, HALF * HD), 'ctx', 0, 0, axis_index...  5.35 us
  transfers between devices with their start and end apart: 22, of which 9 were waited for; matrix products, arithmetic and copies ran while one was open for 1% of the time, Pallas kernels for 32%

profile of v5, /device:TPU:1, one launch (start us, length us, event | category | flops | bytes accessed | tf_op | source)
XLA Modules:
  0.0 135.6 jit_solution(1953230780294832241)
XLA Ops:
  0.6 2.5 %halves.1 = (bf16[8,128,512]{2,1,0:T(8,128)(2,1)}, bf16[8,128,512]{2,1,0:T(8,128)(2,1)}) custom-call(bf16[128,1024]{1,0:T(8,128)(2,1)} %bitcast.35, bf16[128,1024]{1,0:T(8,128)(2,1)} %bitcast.36), custom_call_target="tpu_custom_call" | custom-call | flops 1 | bytes 1 | tf_op jit(solution)/shard_map/halves/pallas_call | solution.py:378
  3.2 6.0 %all-to-all-start = ((bf16[8,128,512]{2,1,0:T(8,128)(2,1)}), bf16[8,128,512]{2,1,0:T(8,128)(2,1)S(1)}, u32[]{:S(2)}, u32[]{:S(2)}) async-start(bf16[8,128,512]{2,1,0:T(8,128)(2,1)} %get-tuple-element.57), calls=%async_computation | async-start | bytes 2097152 | tf_op jit(solution)/shard_map/all_to_all | solution.py:589
  9.7 3.0 %x_sends.1 = (bf16[1024,128]{1,0:T(8,128)(2,1)}, bf16[1024,128]{1,0:T(8,128)(2,1)}, bf16[1024,128]{1,0:T(8,128)(2,1)}, bf16[1024,128]{1,0:T(8,128)(2,1)}) custom-call(s32[3]{0:T(128)} %pad_add_fusion.place.refs_0_, bf16[128,4096]{1,0:T(8,128)(2,1)} %bitcast.33), custom_call_target="tpu_custom_call" | custom-call | flops 1 | bytes 1 | tf_op jit(solution)/shard_map/x_sends/pallas_call | solution.py:504
  16.5 3.3 %partner_halves.1 = (bf16[128,4096]{1,0:T(8,128)(2,1)}, bf16[128,4096]{1,0:T(8,128)(2,1)}) custom-call(s32[3]{0:T(128)} %pad_add_fusion.place.refs_0_, bf16[128,8192]{1,0:T(8,128)(2,1)} %bitcast.21, bf16[128,8192]{1,0:T(8,128)(2,1)} %bitcast.25), custom_call_target="tpu_custom_call" | custom-call | flops 1 | bytes 1 | tf_op jit(solution)/shard_map/partner_halves/pallas_call | solution.py:397
  20.3 3.1 %collective-permute-done.2.refs_1_ = bf16[1024,128]{1,0:T(8,128)(2,1)S(1)} collective-permute-done((bf16[1024,128]{1,0:T(8,128)(2,1)}, bf16[1024,128]{1,0:T(8,128)(2,1)S(1)}, u32[]{:S(2)}, u32[]{:S(2)}) %collective-permute-start.2) | collective-permute-done | bytes 262176 | tf_op jit(solution)/shard_map/ppermute | solution.py:583
  24.3 4.3 %all-to-all-start.1 = ((bf16[8,128,512]{2,1,0:T(8,128)(2,1)}), bf16[8,128,512]{2,1,0:T(8,128)(2,1)S(1)}, u32[]{:S(2)}, u32[]{:S(2)}) async-start(bf16[8,128,512]{2,1,0:T(8,128)(2,1)} %get-tuple-element.63), calls=%async_computation.1 | async-start | bytes 2097152 | tf_op jit(solution)/shard_map/all_to_all | solution.py:594
  28.6 3.6 %collective-permute-start.4 = (bf16[1024,128]{1,0:T(8,128)(2,1)S(1)}, bf16[1024,128]{1,0:T(8,128)(2,1)S(1)}, u32[]{:S(2)}, u32[]{:S(2)}) collective-permute-start(bf16[1024,128]{1,0:T(8,128)(2,1)S(1)} %copy-done.13), channel_id=1, source_target_pairs={{0,16},{8,24},{16,0},{24,8},{32,48},{40,56},{48,32},{56,40},{64,80... | collective-permute-start | bytes 786440 | tf_op jit(solution)/shard_map/ppermute | solution.py:583
  32.2 9.1 %tree_values.1 = (bf16[8,128,512]{2,1,0:T(8,128)(2,1)}, f32[4,2,8,1024]{3,2,1,0:T(8,128)}) custom-call(s32[3]{0:T(128)} %pad_add_fusion.place.refs_0_, s32[1,8]{1,0:T(1,128)} %refs_1_.1, s32[1,8]{1,0:T(1,128)} %refs_2_.1, bf16[128,8192]{1,0:T(8,128)(2,1)} %bitcast.22, bf16[128,4096]{1,0:T(8,128)(2,1)} %collective-permute-done.q_par.refs_4_, ...), custom_call_target="tpu_custom_call" | custom-call | flops 1 | bytes 1 | tf_op jit(solution)/shard_map/tree_values/pallas_call | solution.py:286
  41.3 2.4 %all-to-all-done.1.vals.refs_8_ = bf16[8,128,512]{2,1,0:T(8,128)(2,1)S(1)} async-done(((bf16[8,128,512]{2,1,0:T(8,128)(2,1)}), bf16[8,128,512]{2,1,0:T(8,128)(2,1)S(1)}, u32[]{:S(2)}, u32[]{:S(2)}) %all-to-all-start.1) | async-done | bytes 1048608 | tf_op jit(solution)/shard_map/all_to_all | solution.py:594
  43.7 4.2 %all-to-all-start.2 = ((bf16[4,2,128,512]{3,2,1,0:T(8,128)(2,1)}), bf16[4,2,128,512]{3,2,1,0:T(8,128)(2,1)S(1)}, u32[]{:S(2)}, u32[]{:S(2)}) async-start(bf16[4,2,128,512]{3,2,1,0:T(8,128)(2,1)} %bitcast.34), calls=%async_computation.2 | async-start | bytes 2097152 | tf_op jit(solution)/shard_map/all_to_all | solution.py:597
  47.9 8.8 %tree_outputs.2 = (bf16[128,8192]{1,0:T(8,128)(2,1)}, bf16[128,2048]{1,0:T(8,128)(2,1)}, bf16[128,8192]{1,0:T(8,128)(2,1)}, bf16[128,2048]{1,0:T(8,128)(2,1)}, bf16[8,128,512]{2,1,0:T(8,128)(2,1)}) custom-call(s32[3]{0:T(128)} %pad_add_fusion.place.refs_0_, s32[1,8]{1,0:T(1,128)} %refs_1_.1, s32[1,8]{1,0:T(1,128)} %refs_2_.1, bf16[128,8192]{1,0:T(8,128)(2,1)} %bitcast.23, ...), custom_call_target="tpu_custom_call" | custom-call | flops 1 | bytes 1 | tf_op jit(solution)/shard_map/tree_outputs/pallas_call | solution.py:309
  56.7 5.3 %all-to-all-done.2.terms = bf16[4,2,128,512]{3,2,1,0:T(8,128)(2,1)S(1)} async-done(((bf16[4,2,128,512]{3,2,1,0:T(8,128)(2,1)}), bf16[4,2,128,512]{3,2,1,0:T(8,128)(2,1)S(1)}, u32[]{:S(2)}, u32[]{:S(2)}) %all-to-all-start.2) | async-done | bytes 1048608 | tf_op jit(solution)/shard_map/all_to_all | solution.py:597
  63.1 2.4 %sum_blocks.1.dv = bf16[4,2,128,512]{3,2,1,0:T(8,128)(2,1)} custom-call(bf16[4,2,128,512]{3,2,1,0:T(8,128)(2,1)} %copy-done.6), custom_call_target="tpu_custom_call" | custom-call | flops 1 | bytes 1 | tf_op jit(solution)/shard_map/sum_blocks/pallas_call | solution.py:532
  65.5 4.4 %all-to-all-start.3 = ((bf16[4,2,128,512]{3,2,1,0:T(8,128)(2,1)}), bf16[4,2,128,512]{3,2,1,0:T(8,128)(2,1)S(1)}, u32[]{:S(2)}, u32[]{:S(2)}) async-start(bf16[4,2,128,512]{3,2,1,0:T(8,128)(2,1)} %sum_blocks.1.dv), calls=%async_computation.3 | async-start | bytes 2097152 | tf_op jit(solution)/shard_map/all_to_all | solution.py:605
  72.6 9.0 %tree_outputs.3 = (bf16[128,8192]{1,0:T(8,128)(2,1)}, bf16[128,2048]{1,0:T(8,128)(2,1)}, bf16[128,8192]{1,0:T(8,128)(2,1)}, bf16[128,2048]{1,0:T(8,128)(2,1)}, bf16[8,128,512]{2,1,0:T(8,128)(2,1)}) custom-call(s32[3]{0:T(128)} %pad_add_fusion.place.refs_0_, s32[1,8]{1,0:T(1,128)} %refs_1_.1, ...), custom_call_target="tpu_custom_call", output_to_operand_aliasing={{0}: (10, {}), {2}: (11, {}), {4}: (12, {})} | custom-call | flops 1 | bytes 1 | tf_op jit(solution)/shard_map/tree_outputs/pallas_call | solution.py:309
  83.0 3.5 %weight_partial.1 = bf16[1024,512]{1,0:T(8,128)(2,1)} custom-call(s32[3]{0:T(128)S(1)} %copy-done.1, bf16[1024,128]{1,0:T(8,128)(2,1)S(1)} %copy-done, bf16[1024,128]{1,0:T(8,128)(2,1)S(1)} %collective-permute-done.2.refs_1_, bf16[1024,128]{1,0:T(8,128)(2,1)S(1)} %collective-permute-done.4.refs_2_, bf16[1024,128]{1,0:T(8,128)(2,1)S(1)} %collective-permute-done.3.refs_3_, ...), custom_call_target="tpu_custom_call" | custom-call | flops 1 | bytes 1 | tf_op jit(solution)/shard_map/weight_partial/pallas_call | solution.py:347
  86.5 3.0 %collective-permute-start.10 = (bf16[128,2048]{1,0:T(8,128)(2,1)}, bf16[128,2048]{1,0:T(8,128)(2,1)S(1)}, u32[]{:S(2)}, u32[]{:S(2)}) collective-permute-start(bf16[128,2048]{1,0:T(8,128)(2,1)} %get-tuple-element.95), channel_id=1, source_target_pairs={{0,1},{1,0},{2,3},{3,2},{4,5},{5,4},{6,7},{7,6},{8,9},{9,8},{10,11... | collective-permute-start | bytes 1572872 | tf_op jit(solution)/shard_map/ppermute | solution.py:577
  89.5 7.4 %all-to-all-start.4 = ((bf16[32,32,512]{2,1,0:T(8,128)(2,1)}), bf16[32,32,512]{2,1,0:T(8,128)(2,1)S(1)}, u32[]{:S(2)}, u32[]{:S(2)}) async-start(bf16[32,32,512]{2,1,0:T(8,128)(2,1)} %bitcast.9), calls=%async_computation.4 | async-start | bytes 2097152 | tf_op jit(solution)/shard_map/all_to_all | solution.py:614
  102.3 4.8 %fill_partner.1 = (bf16[128,8192]{1,0:T(8,128)(2,1)}, bf16[128,8192]{1,0:T(8,128)(2,1)}) custom-call(s32[3]{0:T(128)} %pad_add_fusion.place.refs_0_, bf16[128,8192]{1,0:T(8,128)(2,1)} %get-tuple-element.81.o_before, bf16[128,8192]{1,0:T(8,128)(2,1)} %get-tuple-element.82.dq_before, ...), custom_call_target="tpu_custom_call", output_to_operand_aliasing={{0}: (1, {}), {1}: (2, {})} | custom-call | flops 1 | bytes 1 | tf_op jit(solution)/shard_map/fill_partner/pallas_call | solution.py:427
  107.1 8.9 %collective-permute-done.13.r1 = bf16[2,128,512]{2,1,0:T(8,128)(2,1)S(1)} collective-permute-done((bf16[2,128,512]{2,1,0:T(8,128)(2,1)}, bf16[2,128,512]{2,1,0:T(8,128)(2,1)S(1)}, u32[]{:S(2)}, u32[]{:S(2)}) %collective-permute-start.13) | collective-permute-done | bytes 262176 | tf_op jit(solution)/shard_map/ppermute | solution.py:586
  116.0 2.2 %collective-permute-done.14.r2 = bf16[2,128,512]{2,1,0:T(8,128)(2,1)S(1)} collective-permute-done((bf16[2,128,512]{2,1,0:T(8,128)(2,1)}, bf16[2,128,512]{2,1,0:T(8,128)(2,1)S(1)}, u32[]{:S(2)}, u32[]{:S(2)}) %collective-permute-start.14) | collective-permute-done | bytes 262176 | tf_op jit(solution)/shard_map/ppermute | solution.py:586
  118.2 5.8 %collective-permute-done.15.r3 = bf16[2,128,512]{2,1,0:T(8,128)(2,1)S(1)} collective-permute-done((bf16[2,128,512]{2,1,0:T(8,128)(2,1)S(1)}, bf16[2,128,512]{2,1,0:T(8,128)(2,1)S(1)}, u32[]{:S(2)}, u32[]{:S(2)}) %collective-permute-start.15) | collective-permute-done | bytes 262176 | tf_op jit(solution)/shard_map/ppermute | solution.py:586
  124.7 2.8 %split_grads.1 = (bf16[2,128,512]{2,1,0:T(8,128)(2,1)}, bf16[2,128,512]{2,1,0:T(8,128)(2,1)}) custom-call(s32[3]{0:T(128)} %pad_add_fusion.place.refs_0_, bf16[4,2,128,512]{3,2,1,0:T(8,128)(2,1)} %bitcast.31, bf16[2,128,512]{2,1,0:T(8,128)(2,1)} %copy-done.9, bf16[2,128,512]{2,1,0:T(8,128)(2,1)} %copy-done.10, bf16[2,128,512]{2,1,0:T(8,128)(2,1)} %copy-done.11, ...), custom_call_target="tpu_custom_call" | custom-call | flops 1 | bytes 1 | tf_op jit(solution)/shard_map/split_grads/pallas_call | solution.py:455
  130.0 2.5 %join_grads.1 = (bf16[128,1024]{1,0:T(8,128)(2,1)}, bf16[128,1024]{1,0:T(8,128)(2,1)}) custom-call(s32[3]{0:T(128)} %pad_add_fusion.place.refs_0_, bf16[2,128,512]{2,1,0:T(8,128)(2,1)} %get-tuple-element.101.mine, bf16[2,128,512]{2,1,0:T(8,128)(2,1)} %copy-done.12), custom_call_target="tpu_custom_call" | custom-call | flops 1 | bytes 1 | tf_op jit(solution)/shard_map/join_grads/pallas_call | solution.py:482
  (62 shorter events, 22.3 us)
Async XLA Ops:
  3.2 21.1 %all-to-all-start = ((bf16[8,128,512]{2,1,0:T(8,128)(2,1)}), bf16[8,128,512]{2,1,0:T(8,128)(2,1)S(1)}, u32[]{:S(2)}, u32[]{:S(2)}) async-start(bf16[8,128,512]{2,1,0:T(8,128)(2,1)} %get-tuple-element.57), calls=%async_computation | async-start | bytes 2097152 | tf_op jit(solution)/shard_map/all_to_all | solution.py:589
  12.8 10.6 %collective-permute-start.2 = (bf16[1024,128]{1,0:T(8,128)(2,1)}, bf16[1024,128]{1,0:T(8,128)(2,1)S(1)}, u32[]{:S(2)}, u32[]{:S(2)}) collective-permute-start(bf16[1024,128]{1,0:T(8,128)(2,1)} %get-tuple-element.59), channel_id=1, source_target_pairs={{0,8},{8,16},{16,24},{24,0},{32,40},{40,48},{48,56},{56,32},{64,72... | collective-permute-start | bytes 786440 | tf_op jit(solution)/shard_map/ppermute | solution.py:583
  14.4 9.0 %collective-permute-start.3 = (bf16[1024,128]{1,0:T(8,128)(2,1)}, bf16[1024,128]{1,0:T(8,128)(2,1)S(1)}, u32[]{:S(2)}, u32[]{:S(2)}) collective-permute-start(bf16[1024,128]{1,0:T(8,128)(2,1)} %get-tuple-element.60), channel_id=1, source_target_pairs={{0,24},{8,0},{16,8},{24,16},{32,56},{40,32},{48,40},{56,48},{64,88... | collective-permute-start | bytes 786440 | tf_op jit(solution)/shard_map/ppermute | solution.py:583
  19.8 12.4 %collective-permute-start = (bf16[128,4096]{1,0:T(8,128)(2,1)}, bf16[128,4096]{1,0:T(8,128)(2,1)}, u32[]{:S(2)}, u32[]{:S(2)}) collective-permute-start(bf16[128,4096]{1,0:T(8,128)(2,1)} %get-tuple-element.55), channel_id=1, source_target_pairs={{0,1},{1,0},{2,3},{3,2},{4,5},{5,4},{6,7},{7,6},{8,9},{9,8},{10,11... | collective-permute-start | bytes 3145736 | tf_op jit(solution)/shard_map/ppermute | solution.py:577
  20.1 12.1 %collective-permute-start.1 = (bf16[128,4096]{1,0:T(8,128)(2,1)}, bf16[128,4096]{1,0:T(8,128)(2,1)}, u32[]{:S(2)}, u32[]{:S(2)}) collective-permute-start(bf16[128,4096]{1,0:T(8,128)(2,1)} %get-tuple-element.56), channel_id=1, source_target_pairs={{0,1},{1,0},{2,3},{3,2},{4,5},{5,4},{6,7},{7,6},{8,9},{9,8},{10,11... | collective-permute-start | bytes 3145736 | tf_op jit(solution)/shard_map/ppermute | solution.py:577
  24.3 19.4 %all-to-all-start.1 = ((bf16[8,128,512]{2,1,0:T(8,128)(2,1)}), bf16[8,128,512]{2,1,0:T(8,128)(2,1)S(1)}, u32[]{:S(2)}, u32[]{:S(2)}) async-start(bf16[8,128,512]{2,1,0:T(8,128)(2,1)} %get-tuple-element.63), calls=%async_computation.1 | async-start | bytes 2097152 | tf_op jit(solution)/shard_map/all_to_all | solution.py:594
  28.6 12.7 %collective-permute-start.4 = (bf16[1024,128]{1,0:T(8,128)(2,1)S(1)}, bf16[1024,128]{1,0:T(8,128)(2,1)S(1)}, u32[]{:S(2)}, u32[]{:S(2)}) collective-permute-start(bf16[1024,128]{1,0:T(8,128)(2,1)S(1)} %copy-done.13), channel_id=1, source_target_pairs={{0,16},{8,24},{16,0},{24,8},{32,48},{40,56},{48,32},{56,40},{64,80... | collective-permute-start | bytes 786440 | tf_op jit(solution)/shard_map/ppermute | solution.py:583
  43.7 18.4 %all-to-all-start.2 = ((bf16[4,2,128,512]{3,2,1,0:T(8,128)(2,1)}), bf16[4,2,128,512]{3,2,1,0:T(8,128)(2,1)S(1)}, u32[]{:S(2)}, u32[]{:S(2)}) async-start(bf16[4,2,128,512]{3,2,1,0:T(8,128)(2,1)} %bitcast.34), calls=%async_computation.2 | async-start | bytes 2097152 | tf_op jit(solution)/shard_map/all_to_all | solution.py:597
  65.5 17.5 %all-to-all-start.3 = ((bf16[4,2,128,512]{3,2,1,0:T(8,128)(2,1)}), bf16[4,2,128,512]{3,2,1,0:T(8,128)(2,1)S(1)}, u32[]{:S(2)}, u32[]{:S(2)}) async-start(bf16[4,2,128,512]{3,2,1,0:T(8,128)(2,1)} %sum_blocks.1.dv), calls=%async_computation.3 | async-start | bytes 2097152 | tf_op jit(solution)/shard_map/all_to_all | solution.py:605
  69.9 13.1 %collective-permute-start.5 = (bf16[1024,128]{1,0:T(8,128)(2,1)S(1)}, bf16[1024,128]{1,0:T(8,128)(2,1)S(1)}, u32[]{:S(2)}, u32[]{:S(2)}) collective-permute-start(bf16[1024,128]{1,0:T(8,128)(2,1)S(1)} %copy-done), channel_id=1, source_target_pairs={{0,1},{1,0},{2,3},{3,2},{4,5},{5,4},{6,7},{7,6},{8,9},{9,8},{10,11... | collective-permute-start | bytes 786440 | tf_op jit(solution)/shard_map/ppermute | solution.py:577
  72.0 11.0 %collective-permute-start.6 = (bf16[1024,128]{1,0:T(8,128)(2,1)S(1)}, bf16[1024,128]{1,0:T(8,128)(2,1)S(1)}, u32[]{:S(2)}, u32[]{:S(2)}) collective-permute-start(bf16[1024,128]{1,0:T(8,128)(2,1)S(1)} %collective-permute-done.2.refs_1_), channel_id=1, source_target_pairs={{0,1},{1,0},{2,3},{3,2},{4,5},{5,4},{6,7},{7,6},{8,9},{9,8},{10,11... | collective-permute-start | bytes 786440 | tf_op jit(solution)/shard_map/ppermute | solution.py:577
  72.1 10.9 %collective-permute-start.7 = (bf16[1024,128]{1,0:T(8,128)(2,1)S(1)}, bf16[1024,128]{1,0:T(8,128)(2,1)S(1)}, u32[]{:S(2)}, u32[]{:S(2)}) collective-permute-start(bf16[1024,128]{1,0:T(8,128)(2,1)S(1)} %collective-permute-done.4.refs_2_), channel_id=1, source_target_pairs={{0,1},{1,0},{2,3},{3,2},{4,5},{5,4},{6,7},{7,6},{8,9},{9,8},{10,11... | collective-permute-start | bytes 786440 | tf_op jit(solution)/shard_map/ppermute | solution.py:577
  72.5 10.5 %collective-permute-start.8 = (bf16[1024,128]{1,0:T(8,128)(2,1)S(1)}, bf16[1024,128]{1,0:T(8,128)(2,1)S(1)}, u32[]{:S(2)}, u32[]{:S(2)}) collective-permute-start(bf16[1024,128]{1,0:T(8,128)(2,1)S(1)} %collective-permute-done.3.refs_3_), channel_id=1, source_target_pairs={{0,1},{1,0},{2,3},{3,2},{4,5},{5,4},{6,7},{7,6},{8,9},{9,8},{10,11... | collective-permute-start | bytes 786440 | tf_op jit(solution)/shard_map/ppermute | solution.py:577
  72.6 10.5 %copy-start.1 = (s32[3]{0:T(128)S(1)}, s32[3]{0:T(128)}, u32[]{:S(2)}) copy-start(s32[3]{0:T(128)} %pad_add_fusion.place.refs_0_) | copy-start | bytes 40
  86.5 11.0 %copy-start.4 = (bf16[8,128,512]{2,1,0:T(8,128)(2,1)S(1)}, bf16[8,128,512]{2,1,0:T(8,128)(2,1)}, u32[]{:S(2)}) copy-start(bf16[8,128,512]{2,1,0:T(8,128)(2,1)} %get-tuple-element.100) | copy-start | bytes 3145732
  86.5 13.2 %collective-permute-start.10 = (bf16[128,2048]{1,0:T(8,128)(2,1)}, bf16[128,2048]{1,0:T(8,128)(2,1)S(1)}, u32[]{:S(2)}, u32[]{:S(2)}) collective-permute-start(bf16[128,2048]{1,0:T(8,128)(2,1)} %get-tuple-element.95), channel_id=1, source_target_pairs={{0,1},{1,0},{2,3},{3,2},{4,5},{5,4},{6,7},{7,6},{8,9},{9,8},{10,11... | collective-permute-start | bytes 1572872 | tf_op jit(solution)/shard_map/ppermute | solution.py:577
  89.5 11.5 %collective-permute-start.11 = (bf16[128,2048]{1,0:T(8,128)(2,1)}, bf16[128,2048]{1,0:T(8,128)(2,1)S(1)}, u32[]{:S(2)}, u32[]{:S(2)}) collective-permute-start(bf16[128,2048]{1,0:T(8,128)(2,1)} %get-tuple-element.96), channel_id=1, source_target_pairs={{0,1},{1,0},{2,3},{3,2},{4,5},{5,4},{6,7},{7,6},{8,9},{9,8},{10,11... | collective-permute-start | bytes 1572872 | tf_op jit(solution)/shard_map/ppermute | solution.py:577
  89.5 43.1 %all-to-all-start.4 = ((bf16[32,32,512]{2,1,0:T(8,128)(2,1)}), bf16[32,32,512]{2,1,0:T(8,128)(2,1)S(1)}, u32[]{:S(2)}, u32[]{:S(2)}) async-start(bf16[32,32,512]{2,1,0:T(8,128)(2,1)} %bitcast.9), calls=%async_computation.4 | async-start | bytes 2097152 | tf_op jit(solution)/shard_map/all_to_all | solution.py:614
  96.9 5.4 %collective-permute-start.12 = (bf16[128,2048]{1,0:T(8,128)(2,1)}, bf16[128,2048]{1,0:T(8,128)(2,1)}, u32[]{:S(2)}, u32[]{:S(2)}) collective-permute-start(bf16[128,2048]{1,0:T(8,128)(2,1)} %get-tuple-element.97), channel_id=1, source_target_pairs={{0,1},{1,0},{2,3},{3,2},{4,5},{5,4},{6,7},{7,6},{8,9},{9,8},{10,11... | collective-permute-start | bytes 1572872 | tf_op jit(solution)/shard_map/ppermute | solution.py:577
  97.2 5.1 %collective-permute-start.9 = (bf16[128,2048]{1,0:T(8,128)(2,1)}, bf16[128,2048]{1,0:T(8,128)(2,1)}, u32[]{:S(2)}, u32[]{:S(2)}) collective-permute-start(bf16[128,2048]{1,0:T(8,128)(2,1)} %get-tuple-element.94), channel_id=1, source_target_pairs={{0,1},{1,0},{2,3},{3,2},{4,5},{5,4},{6,7},{7,6},{8,9},{9,8},{10,11... | collective-permute-start | bytes 1572872 | tf_op jit(solution)/shard_map/ppermute | solution.py:577
  98.4 17.6 %collective-permute-start.13 = (bf16[2,128,512]{2,1,0:T(8,128)(2,1)}, bf16[2,128,512]{2,1,0:T(8,128)(2,1)S(1)}, u32[]{:S(2)}, u32[]{:S(2)}) collective-permute-start(bf16[2,128,512]{2,1,0:T(8,128)(2,1)} %get-tuple-element.107), channel_id=1, source_target_pairs={{2,0},{3,1},{4,2},{5,3},{6,4},{7,5},{10,8},{11,9},{12,10},{13,11},... | collective-permute-start | bytes 786440 | tf_op jit(solution)/shard_map/ppermute | solution.py:586
  99.7 18.6 %collective-permute-start.14 = (bf16[2,128,512]{2,1,0:T(8,128)(2,1)}, bf16[2,128,512]{2,1,0:T(8,128)(2,1)S(1)}, u32[]{:S(2)}, u32[]{:S(2)}) collective-permute-start(bf16[2,128,512]{2,1,0:T(8,128)(2,1)} %get-tuple-element.106), channel_id=1, source_target_pairs={{4,0},{5,1},{6,2},{7,3},{12,8},{13,9},{14,10},{15,11},{20,16},{21,... | collective-permute-start | bytes 786440 | tf_op jit(solution)/shard_map/ppermute | solution.py:586
  101.0 23.0 %collective-permute-start.15 = (bf16[2,128,512]{2,1,0:T(8,128)(2,1)S(1)}, bf16[2,128,512]{2,1,0:T(8,128)(2,1)S(1)}, u32[]{:S(2)}, u32[]{:S(2)}) collective-permute-start(bf16[2,128,512]{2,1,0:T(8,128)(2,1)S(1)} %get-tuple-element.105), channel_id=1, source_target_pairs={{6,0},{7,1},{14,8},{15,9},{22,16},{23,17},{30,24},{31,25},{38,32},... | collective-permute-start | bytes 786440 | tf_op jit(solution)/shard_map/ppermute | solution.py:586
  127.5 1.8 %collective-permute-start.16 = (bf16[2,128,512]{2,1,0:T(8,128)(2,1)}, bf16[2,128,512]{2,1,0:T(8,128)(2,1)S(1)}, u32[]{:S(2)}, u32[]{:S(2)}) collective-permute-start(bf16[2,128,512]{2,1,0:T(8,128)(2,1)} %get-tuple-element.102), channel_id=1, source_target_pairs={{0,1},{1,0},{2,3},{3,2},{4,5},{5,4},{6,7},{7,6},{8,9},{9,8},{10,11... | collective-permute-start | bytes 786440 | tf_op jit(solution)/shard_map/ppermute | solution.py:577
  (12 other events, 49.0 us)

commit v6 on v5

--- a/solution.py
+++ b/solution.py
@@ -437,57 +437,6 @@
         cost_estimate=LIGHT,
         name="fill_partner",
     )(place, o_all, dq_all, *o_parts, *dq_parts)
-
-
-def split_kernel(place, dk, r1, r2, r3, dv, after, mine, other):
-    c = place[1]
-    for out, e in ((mine, c), (other, 1 - c)):
-        acc = dk[0, e].astype(F32)
-        for r in (r1, r2, r3):
-            acc = acc + r[e].astype(F32)
-        out[0] = acc.astype(LOW)
-        out[1] = dv[0, e]
-
-
-def split_grads(place, dk, received, dv, after):
-    width = dk.shape[3]
-    pair = pl.BlockSpec((2, BLK, width), lambda i, place: (0, 0, 0))
-    return pl.pallas_call(
-        split_kernel,
-        grid_spec=pltpu.PrefetchScalarGridSpec(
-            num_scalar_prefetch=1,
-            grid=(1,),
-            in_specs=[pl.BlockSpec((1, 2, BLK, width), lambda i, place: (place[0], 0, 0, 0))]
-            + [pair] * 3
-            + [pl.BlockSpec((1, 2, BLK, width), lambda i, place: (0, 0, 0, 0)), pl.BlockSpec(memory_space=pl.ANY)],
-            out_specs=[pair, pair],
-        ),
-        out_shape=[jax.ShapeDtypeStruct((2, BLK, width), LOW)] * 2,
-        cost_estimate=LIGHT,
-        name="split_grads",
-    )(place, dk, *received, dv, after)
-
-
-def join_kernel(place, mine, other, key_grad, value_grad):
-    width = mine.shape[2]
-    for i, out in enumerate((key_grad, value_grad)):
-        out[:, pl.ds(pl.multiple_of(place[1] * width, width), width)] = mine[i]
-        out[:, pl.ds(pl.multiple_of((1 - place[1]) * width, width), width)] = other[i]
-
-
-def join_grads(place, mine, other):
-    width = mine.shape[2]
-    pair = pl.BlockSpec((2, BLK, width), lambda i, place: (0, 0, 0))
-    rows = pl.BlockSpec((BLK, 2 * width), lambda i, place: (0, 0))
-    return pl.pallas_call(
-        join_kernel,
-        grid_spec=pltpu.PrefetchScalarGridSpec(
-            num_scalar_prefetch=1, grid=(1,), in_specs=[pair, pair], out_specs=[rows, rows]
-        ),
-        out_shape=[jax.ShapeDtypeStruct((BLK, 2 * width), LOW)] * 2,
-        cost_estimate=LIGHT,
-        name="join_grads",
-    )(place, mine, other)
 
 
 def x_kernel(place, x, *outs):
@@ -613,8 +562,13 @@
     o_pars, dq_pars = [swap(a) for a in o_pars], [swap(a) for a in dq_pars]
     weight_grad = finish_weight(lax.all_to_all(partial, ("dp", "ctx"), 0, 0, axis_index_groups=across))
     out, query_grad = fill_partner(place, o_own, dq_own, o_pars, dq_pars)
-    mine, other = split_grads(place, dk, received, dv_sends, query_grad)
-    key_grad, value_grad = join_grads(place, mine, swap(other))
+    dk, query_grad = lax.optimization_barrier((dk, query_grad))
+    dk_sum = pick(dk, y).astype(F32)
+    for term in received:
+        dk_sum = dk_sum + term.astype(F32)
+    both = jnp.stack([dk_sum.astype(LOW), dv_sends[0]], axis=1)
+    mine, other = pick(both, c), swap(pick(both, 1 - c))
+    key_grad, value_grad = jnp.concatenate([jnp.where(c == 0, mine, other), jnp.where(c == 0, other, mine)], axis=-1)
     return out[None], query_grad[None], key_grad[None], value_grad[None], weight_grad
 
 

time: 136 us -> 129 us (0.949)
  waiting for transfers between devices: 31.4 us -> 20.8 us
  Pallas kernels: 53.7 us -> 48.4 us
  starting transfers between devices: 44.7 us -> 49.9 us
  other arithmetic: 0.59 us -> 2.87 us
  local copies, waits for them, and re-layouts: 4.26 us -> 5.96 us
    ppermute x3, waiting for transfers between devices: 16.9 us -> 0.01 us  [earlier(): lax.ppermute(a, 'ctx', [(i + 2 * d, i) for i in range(SLOTS - 2 * d)])]
    all_to_all x1, waiting for transfers between devices: 0.01 us -> 6.31 us  [per_device(): lax.all_to_all(partial, ('dp', 'ctx'), 0, 0, axis_index_groups=across)]
    all_to_all x1, starting transfers between devices: 7.44 us -> 12.9 us  [per_device(): lax.all_to_all(partial, ('dp', 'ctx'), 0, 0, axis_index_groups=across)]
    pallas_call x2 -> x0, Pallas kernels: 5.32 us -> none  [the longest x1 2.81 us: split_grads(): pl.pallas_call(split_kernel, grid_spec=pltpu.PrefetchScalarGridSpec(num_s...]
    unnamed x28 -> x22, local copies, waits for them, and re-layouts: 3.41 us -> 2.92 us
  transfers between devices with their start and end apart: 22 -> 22, of which waited for: 9 -> 7; matrix products, arithmetic and copies ran while one was open for 1% -> 5% of each run, Pallas kernels for 32% -> 29%
where the time goes in v6:
time: 129 us
  starting transfers between devices  49.9 us (39%)
  Pallas kernels  48.4 us (38%)
  waiting for transfers between devices  20.8 us (16%)
  local copies, waits for them, and re-layouts  5.96 us (5%)
  other arithmetic  2.87 us (2%)
    pallas_call x2, Pallas kernels, output_and_gradients(): attention_call(output_onward_kernel if before else output_kernel, 'tree_o...  17.8 us
    all_to_all x1, starting transfers between devices, per_device(): lax.all_to_all(partial, ('dp', 'ctx'), 0, 0, axis_index_groups=across)  12.9 us
    pallas_call x1, Pallas kernels, value_gradient(): attention_call(values_kernel, 'tree_values', HALF // NG, [own, partner, o...  9.09 us
    ppermute x3, starting transfers between devices, further(): lax.ppermute(a, 'dp', [(i, i // NZ * NZ + (i + d) % NZ) for i in range(NX...  7.36 us
    ppermute x11, starting transfers between devices, swap(): return lax.ppermute(a, 'ctx', [(i, i ^ 1) for i in range(SLOTS)])  6.96 us
    all_to_all x1, waiting for transfers between devices, per_device(): lax.all_to_all(partial, ('dp', 'ctx'), 0, 0, axis_index_groups=across)  6.31 us
    all_to_all x1, starting transfers between devices, per_device(): keys = lax.all_to_all(k_sends, 'ctx', 0, 0)  5.98 us
    all_to_all x1, waiting for transfers between devices, per_device(): lax.all_to_all(dv.reshape(NY, 2, BLK, HALF * HD), 'ctx', 0, 0, axis_index...  5.39 us
  transfers between devices with their start and end apart: 22, of which 7 were waited for; matrix products, arithmetic and copies ran while one was open for 5% of the time, Pallas kernels for 29%

profile of v6, /device:TPU:1, one launch (start us, length us, event | category | flops | bytes accessed | tf_op | source)
XLA Modules:
  0.0 128.8 jit_solution(17093331163606122564)
XLA Ops:
  0.6 2.5 %halves.1 = (bf16[8,128,512]{2,1,0:T(8,128)(2,1)}, bf16[8,128,512]{2,1,0:T(8,128)(2,1)}) custom-call(bf16[128,1024]{1,0:T(8,128)(2,1)} %bitcast.48, bf16[128,1024]{1,0:T(8,128)(2,1)} %bitcast.49), custom_call_target="tpu_custom_call" | custom-call | flops 1 | bytes 1 | tf_op jit(solution)/shard_map/halves/pallas_call | solution.py:378
  3.1 6.0 %all-to-all-start = ((bf16[8,128,512]{2,1,0:T(8,128)(2,1)}), bf16[8,128,512]{2,1,0:T(8,128)(2,1)S(1)}, u32[]{:S(2)}, u32[]{:S(2)}) async-start(bf16[8,128,512]{2,1,0:T(8,128)(2,1)} %get-tuple-element.55), calls=%async_computation | async-start | bytes 2097152 | tf_op jit(solution)/shard_map/all_to_all | solution.py:538
  9.7 3.0 %x_sends.1 = (bf16[1024,128]{1,0:T(8,128)(2,1)}, bf16[1024,128]{1,0:T(8,128)(2,1)}, bf16[1024,128]{1,0:T(8,128)(2,1)}, bf16[1024,128]{1,0:T(8,128)(2,1)}) custom-call(s32[3]{0:T(128)} %pad_add_fusion.place.refs_0_, bf16[128,4096]{1,0:T(8,128)(2,1)} %bitcast.46), custom_call_target="tpu_custom_call" | custom-call | flops 1 | bytes 1 | tf_op jit(solution)/shard_map/x_sends/pallas_call | solution.py:453
  14.4 2.1 %collective-permute-start.3 = (bf16[1024,128]{1,0:T(8,128)(2,1)}, bf16[1024,128]{1,0:T(8,128)(2,1)S(1)}, u32[]{:S(2)}, u32[]{:S(2)}) collective-permute-start(bf16[1024,128]{1,0:T(8,128)(2,1)} %get-tuple-element.58), channel_id=1, source_target_pairs={{0,24},{8,0},{16,8},{24,16},{32,56},{40,32},{48,40},{56,48},{64,88... | collective-permute-start | bytes 786440 | tf_op jit(solution)/shard_map/ppermute | solution.py:532
  16.5 3.3 %partner_halves.1 = (bf16[128,4096]{1,0:T(8,128)(2,1)}, bf16[128,4096]{1,0:T(8,128)(2,1)}) custom-call(s32[3]{0:T(128)} %pad_add_fusion.place.refs_0_, bf16[128,8192]{1,0:T(8,128)(2,1)} %bitcast.34, bf16[128,8192]{1,0:T(8,128)(2,1)} %bitcast.38), custom_call_target="tpu_custom_call" | custom-call | flops 1 | bytes 1 | tf_op jit(solution)/shard_map/partner_halves/pallas_call | solution.py:397
  20.3 3.1 %collective-permute-done.2.refs_1_ = bf16[1024,128]{1,0:T(8,128)(2,1)S(1)} collective-permute-done((bf16[1024,128]{1,0:T(8,128)(2,1)}, bf16[1024,128]{1,0:T(8,128)(2,1)S(1)}, u32[]{:S(2)}, u32[]{:S(2)}) %collective-permute-start.2) | collective-permute-done | bytes 262176 | tf_op jit(solution)/shard_map/ppermute | solution.py:532
  24.2 4.3 %all-to-all-start.1 = ((bf16[8,128,512]{2,1,0:T(8,128)(2,1)}), bf16[8,128,512]{2,1,0:T(8,128)(2,1)S(1)}, u32[]{:S(2)}, u32[]{:S(2)}) async-start(bf16[8,128,512]{2,1,0:T(8,128)(2,1)} %get-tuple-element.61), calls=%async_computation.1 | async-start | bytes 2097152 | tf_op jit(solution)/shard_map/all_to_all | solution.py:543
  28.6 3.6 %collective-permute-start.4 = (bf16[1024,128]{1,0:T(8,128)(2,1)S(1)}, bf16[1024,128]{1,0:T(8,128)(2,1)S(1)}, u32[]{:S(2)}, u32[]{:S(2)}) collective-permute-start(bf16[1024,128]{1,0:T(8,128)(2,1)S(1)} %copy-done.10), channel_id=1, source_target_pairs={{0,16},{8,24},{16,0},{24,8},{32,48},{40,56},{48,32},{56,40},{64,80... | collective-permute-start | bytes 786440 | tf_op jit(solution)/shard_map/ppermute | solution.py:532
  32.2 9.1 %tree_values.1 = (bf16[8,128,512]{2,1,0:T(8,128)(2,1)}, f32[4,2,8,1024]{3,2,1,0:T(8,128)}) custom-call(s32[3]{0:T(128)} %pad_add_fusion.place.refs_0_, s32[1,8]{1,0:T(1,128)} %refs_1_.1, s32[1,8]{1,0:T(1,128)} %refs_2_.1, bf16[128,8192]{1,0:T(8,128)(2,1)} %bitcast.35, bf16[128,4096]{1,0:T(8,128)(2,1)} %collective-permute-done.q_par.refs_4_, ...), custom_call_target="tpu_custom_call" | custom-call | flops 1 | bytes 1 | tf_op jit(solution)/shard_map/tree_values/pallas_call | solution.py:286
  41.3 2.4 %all-to-all-done.1.vals.refs_8_ = bf16[8,128,512]{2,1,0:T(8,128)(2,1)S(1)} async-done(((bf16[8,128,512]{2,1,0:T(8,128)(2,1)}), bf16[8,128,512]{2,1,0:T(8,128)(2,1)S(1)}, u32[]{:S(2)}, u32[]{:S(2)}) %all-to-all-start.1) | async-done | bytes 1048608 | tf_op jit(solution)/shard_map/all_to_all | solution.py:543
  43.7 3.5 %all-to-all-start.2 = ((bf16[4,2,128,512]{3,2,1,0:T(8,128)(2,1)}), bf16[4,2,128,512]{3,2,1,0:T(8,128)(2,1)S(1)}, u32[]{:S(2)}, u32[]{:S(2)}) async-start(bf16[4,2,128,512]{3,2,1,0:T(8,128)(2,1)} %bitcast.47), calls=%async_computation.2 | async-start | bytes 2097152 | tf_op jit(solution)/shard_map/all_to_all | solution.py:546
  47.2 8.8 %tree_outputs.2 = (bf16[128,8192]{1,0:T(8,128)(2,1)}, bf16[128,2048]{1,0:T(8,128)(2,1)}, bf16[128,8192]{1,0:T(8,128)(2,1)}, bf16[128,2048]{1,0:T(8,128)(2,1)}, bf16[8,128,512]{2,1,0:T(8,128)(2,1)}) custom-call(s32[3]{0:T(128)} %pad_add_fusion.place.refs_0_, s32[1,8]{1,0:T(1,128)} %refs_1_.1, s32[1,8]{1,0:T(1,128)} %refs_2_.1, bf16[128,8192]{1,0:T(8,128)(2,1)} %bitcast.36, ...), custom_call_target="tpu_custom_call" | custom-call | flops 1 | bytes 1 | tf_op jit(solution)/shard_map/tree_outputs/pallas_call | solution.py:309
  56.0 5.4 %all-to-all-done.2.terms = bf16[4,2,128,512]{3,2,1,0:T(8,128)(2,1)S(1)} async-done(((bf16[4,2,128,512]{3,2,1,0:T(8,128)(2,1)}), bf16[4,2,128,512]{3,2,1,0:T(8,128)(2,1)S(1)}, u32[]{:S(2)}, u32[]{:S(2)}) %all-to-all-start.2) | async-done | bytes 1048608 | tf_op jit(solution)/shard_map/all_to_all | solution.py:546
  62.4 2.4 %sum_blocks.1 = bf16[4,2,128,512]{3,2,1,0:T(8,128)(2,1)} custom-call(bf16[4,2,128,512]{3,2,1,0:T(8,128)(2,1)} %copy-done.5), custom_call_target="tpu_custom_call" | custom-call | flops 1 | bytes 1 | tf_op jit(solution)/shard_map/sum_blocks/pallas_call | solution.py:481
  64.8 5.0 %all-to-all-start.3 = ((bf16[4,2,128,512]{3,2,1,0:T(8,128)(2,1)}), bf16[4,2,128,512]{3,2,1,0:T(8,128)(2,1)S(1)}, u32[]{:S(2)}, u32[]{:S(2)}) async-start(bf16[4,2,128,512]{3,2,1,0:T(8,128)(2,1)} %sum_blocks.1), calls=%async_computation.3 | async-start | bytes 2097152 | tf_op jit(solution)/shard_map/all_to_all | solution.py:554
  69.9 2.1 %collective-permute-start.5 = (bf16[1024,128]{1,0:T(8,128)(2,1)S(1)}, bf16[1024,128]{1,0:T(8,128)(2,1)S(1)}, u32[]{:S(2)}, u32[]{:S(2)}) collective-permute-start(bf16[1024,128]{1,0:T(8,128)(2,1)S(1)} %copy-done), channel_id=1, source_target_pairs={{0,1},{1,0},{2,3},{3,2},{4,5},{5,4},{6,7},{7,6},{8,9},{9,8},{10,11... | collective-permute-start | bytes 786440 | tf_op jit(solution)/shard_map/ppermute | solution.py:526
  72.5 9.0 %tree_outputs.3 = (bf16[128,8192]{1,0:T(8,128)(2,1)}, bf16[128,2048]{1,0:T(8,128)(2,1)}, bf16[128,8192]{1,0:T(8,128)(2,1)}, bf16[128,2048]{1,0:T(8,128)(2,1)}, bf16[8,128,512]{2,1,0:T(8,128)(2,1)}) custom-call(s32[3]{0:T(128)} %pad_add_fusion.place.refs_0_, s32[1,8]{1,0:T(1,128)} %refs_1_.1, ...), custom_call_target="tpu_custom_call", output_to_operand_aliasing={{0}: (10, {}), {2}: (11, {}), {4}: (12, {})} | custom-call | flops 1 | bytes 1 | tf_op jit(solution)/shard_map/tree_outputs/pallas_call | solution.py:309
  83.0 3.5 %weight_partial.1 = bf16[1024,512]{1,0:T(8,128)(2,1)} custom-call(s32[3]{0:T(128)S(1)} %copy-done.1, bf16[1024,128]{1,0:T(8,128)(2,1)S(1)} %copy-done, bf16[1024,128]{1,0:T(8,128)(2,1)S(1)} %collective-permute-done.2.refs_1_, bf16[1024,128]{1,0:T(8,128)(2,1)S(1)} %collective-permute-done.4.refs_2_, bf16[1024,128]{1,0:T(8,128)(2,1)S(1)} %collective-permute-done.3.refs_3_, ...), custom_call_target="tpu_custom_call" | custom-call | flops 1 | bytes 1 | tf_op jit(solution)/shard_map/weight_partial/pallas_call | solution.py:347
  86.4 3.0 %collective-permute-start.10 = (bf16[128,2048]{1,0:T(8,128)(2,1)}, bf16[128,2048]{1,0:T(8,128)(2,1)S(1)}, u32[]{:S(2)}, u32[]{:S(2)}) collective-permute-start(bf16[128,2048]{1,0:T(8,128)(2,1)} %get-tuple-element.93), channel_id=1, source_target_pairs={{0,1},{1,0},{2,3},{3,2},{4,5},{5,4},{6,7},{7,6},{8,9},{9,8},{10,11... | collective-permute-start | bytes 1572872 | tf_op jit(solution)/shard_map/ppermute | solution.py:526
  89.9 2.1 %dynamic-slice_bitcast_fusion.2 = (bf16[2,128,512]{2,1,0:T(8,128)(2,1)}, bf16[2,128,512]{2,1,0:T(8,128)(2,1)}, bf16[2,128,512]{2,1,0:T(8,128)(2,1)}) fusion(bf16[4,2,128,512]{3,2,1,0:T(8,128)(2,1)} %bitcast.44, s32[]{:T(128)S(6)} %max.9, s32[]{:T(128)S(6)} %max.11, s32[]{:T(128)S(6)} %max.10), kind=kLoop, calls=%fused_computation.20 | loop fusion | bytes 1572876 | tf_op jit(solution)/shard_map/jit(dynamic_index_in_dim)/squeeze | solution.py:529
  95.9 12.9 %all-to-all-start.4 = ((bf16[32,32,512]{2,1,0:T(8,128)(2,1)}), bf16[32,32,512]{2,1,0:T(8,128)(2,1)S(1)}, u32[]{:S(2)}, u32[]{:S(2)}) async-start(bf16[32,32,512]{2,1,0:T(8,128)(2,1)} %bitcast.9), calls=%async_computation.4 | async-start | bytes 2097152 | tf_op jit(solution)/shard_map/all_to_all | solution.py:563
  110.8 4.7 %fill_partner.1 = (bf16[128,8192]{1,0:T(8,128)(2,1)}, bf16[128,8192]{1,0:T(8,128)(2,1)}) custom-call(s32[3]{0:T(128)} %pad_add_fusion.place.refs_0_, bf16[128,8192]{1,0:T(8,128)(2,1)} %get-tuple-element.79.o_before, bf16[128,8192]{1,0:T(8,128)(2,1)} %get-tuple-element.80.dq_before, ...), custom_call_target="tpu_custom_call", output_to_operand_aliasing={{0}: (1, {}), {1}: (2, {})} | custom-call | flops 1 | bytes 1 | tf_op jit(solution)/shard_map/fill_partner/pallas_call | solution.py:427
  119.5 6.3 %all-to-all-done.4.parts = bf16[32,32,512]{2,1,0:T(8,128)(2,1)S(1)} async-done(((bf16[32,32,512]{2,1,0:T(8,128)(2,1)}), bf16[32,32,512]{2,1,0:T(8,128)(2,1)S(1)}, u32[]{:S(2)}, u32[]{:S(2)}) %all-to-all-start.4) | async-done | bytes 1048608 | tf_op jit(solution)/shard_map/all_to_all | solution.py:563
  126.8 2.0 %finish_weight.1 = f32[32,1024]{1,0:T(8,128)} custom-call(bf16[32,32,512]{2,1,0:T(8,128)(2,1)} %copy-done.4), custom_call_target="tpu_custom_call" | custom-call | flops 1 | bytes 1 | tf_op jit(solution)/shard_map/finish_weight/pallas_call | solution.py:503
  (59 shorter events, 17.8 us)
Async XLA Ops:
  3.1 21.1 %all-to-all-start = ((bf16[8,128,512]{2,1,0:T(8,128)(2,1)}), bf16[8,128,512]{2,1,0:T(8,128)(2,1)S(1)}, u32[]{:S(2)}, u32[]{:S(2)}) async-start(bf16[8,128,512]{2,1,0:T(8,128)(2,1)} %get-tuple-element.55), calls=%async_computation | async-start | bytes 2097152 | tf_op jit(solution)/shard_map/all_to_all | solution.py:538
  12.8 10.6 %collective-permute-start.2 = (bf16[1024,128]{1,0:T(8,128)(2,1)}, bf16[1024,128]{1,0:T(8,128)(2,1)S(1)}, u32[]{:S(2)}, u32[]{:S(2)}) collective-permute-start(bf16[1024,128]{1,0:T(8,128)(2,1)} %get-tuple-element.57), channel_id=1, source_target_pairs={{0,8},{8,16},{16,24},{24,0},{32,40},{40,48},{48,56},{56,32},{64,72... | collective-permute-start | bytes 786440 | tf_op jit(solution)/shard_map/ppermute | solution.py:532
  14.4 9.0 %collective-permute-start.3 = (bf16[1024,128]{1,0:T(8,128)(2,1)}, bf16[1024,128]{1,0:T(8,128)(2,1)S(1)}, u32[]{:S(2)}, u32[]{:S(2)}) collective-permute-start(bf16[1024,128]{1,0:T(8,128)(2,1)} %get-tuple-element.58), channel_id=1, source_target_pairs={{0,24},{8,0},{16,8},{24,16},{32,56},{40,32},{48,40},{56,48},{64,88... | collective-permute-start | bytes 786440 | tf_op jit(solution)/shard_map/ppermute | solution.py:532
  19.8 12.4 %collective-permute-start = (bf16[128,4096]{1,0:T(8,128)(2,1)}, bf16[128,4096]{1,0:T(8,128)(2,1)}, u32[]{:S(2)}, u32[]{:S(2)}) collective-permute-start(bf16[128,4096]{1,0:T(8,128)(2,1)} %get-tuple-element.53), channel_id=1, source_target_pairs={{0,1},{1,0},{2,3},{3,2},{4,5},{5,4},{6,7},{7,6},{8,9},{9,8},{10,11... | collective-permute-start | bytes 3145736 | tf_op jit(solution)/shard_map/ppermute | solution.py:526
  20.1 12.1 %collective-permute-start.1 = (bf16[128,4096]{1,0:T(8,128)(2,1)}, bf16[128,4096]{1,0:T(8,128)(2,1)}, u32[]{:S(2)}, u32[]{:S(2)}) collective-permute-start(bf16[128,4096]{1,0:T(8,128)(2,1)} %get-tuple-element.54), channel_id=1, source_target_pairs={{0,1},{1,0},{2,3},{3,2},{4,5},{5,4},{6,7},{7,6},{8,9},{9,8},{10,11... | collective-permute-start | bytes 3145736 | tf_op jit(solution)/shard_map/ppermute | solution.py:526
  24.2 19.4 %all-to-all-start.1 = ((bf16[8,128,512]{2,1,0:T(8,128)(2,1)}), bf16[8,128,512]{2,1,0:T(8,128)(2,1)S(1)}, u32[]{:S(2)}, u32[]{:S(2)}) async-start(bf16[8,128,512]{2,1,0:T(8,128)(2,1)} %get-tuple-element.61), calls=%async_computation.1 | async-start | bytes 2097152 | tf_op jit(solution)/shard_map/all_to_all | solution.py:543
  28.6 12.7 %collective-permute-start.4 = (bf16[1024,128]{1,0:T(8,128)(2,1)S(1)}, bf16[1024,128]{1,0:T(8,128)(2,1)S(1)}, u32[]{:S(2)}, u32[]{:S(2)}) collective-permute-start(bf16[1024,128]{1,0:T(8,128)(2,1)S(1)} %copy-done.10), channel_id=1, source_target_pairs={{0,16},{8,24},{16,0},{24,8},{32,48},{40,56},{48,32},{56,40},{64,80... | collective-permute-start | bytes 786440 | tf_op jit(solution)/shard_map/ppermute | solution.py:532
  43.7 17.8 %all-to-all-start.2 = ((bf16[4,2,128,512]{3,2,1,0:T(8,128)(2,1)}), bf16[4,2,128,512]{3,2,1,0:T(8,128)(2,1)S(1)}, u32[]{:S(2)}, u32[]{:S(2)}) async-start(bf16[4,2,128,512]{3,2,1,0:T(8,128)(2,1)} %bitcast.47), calls=%async_computation.2 | async-start | bytes 2097152 | tf_op jit(solution)/shard_map/all_to_all | solution.py:546
  64.8 18.1 %all-to-all-start.3 = ((bf16[4,2,128,512]{3,2,1,0:T(8,128)(2,1)}), bf16[4,2,128,512]{3,2,1,0:T(8,128)(2,1)S(1)}, u32[]{:S(2)}, u32[]{:S(2)}) async-start(bf16[4,2,128,512]{3,2,1,0:T(8,128)(2,1)} %sum_blocks.1), calls=%async_computation.3 | async-start | bytes 2097152 | tf_op jit(solution)/shard_map/all_to_all | solution.py:554
  69.9 13.1 %collective-permute-start.5 = (bf16[1024,128]{1,0:T(8,128)(2,1)S(1)}, bf16[1024,128]{1,0:T(8,128)(2,1)S(1)}, u32[]{:S(2)}, u32[]{:S(2)}) collective-permute-start(bf16[1024,128]{1,0:T(8,128)(2,1)S(1)} %copy-done), channel_id=1, source_target_pairs={{0,1},{1,0},{2,3},{3,2},{4,5},{5,4},{6,7},{7,6},{8,9},{9,8},{10,11... | collective-permute-start | bytes 786440 | tf_op jit(solution)/shard_map/ppermute | solution.py:526
  71.9 11.0 %collective-permute-start.6 = (bf16[1024,128]{1,0:T(8,128)(2,1)S(1)}, bf16[1024,128]{1,0:T(8,128)(2,1)S(1)}, u32[]{:S(2)}, u32[]{:S(2)}) collective-permute-start(bf16[1024,128]{1,0:T(8,128)(2,1)S(1)} %collective-permute-done.2.refs_1_), channel_id=1, source_target_pairs={{0,1},{1,0},{2,3},{3,2},{4,5},{5,4},{6,7},{7,6},{8,9},{9,8},{10,11... | collective-permute-start | bytes 786440 | tf_op jit(solution)/shard_map/ppermute | solution.py:526
  72.0 10.9 %collective-permute-start.7 = (bf16[1024,128]{1,0:T(8,128)(2,1)S(1)}, bf16[1024,128]{1,0:T(8,128)(2,1)S(1)}, u32[]{:S(2)}, u32[]{:S(2)}) collective-permute-start(bf16[1024,128]{1,0:T(8,128)(2,1)S(1)} %collective-permute-done.4.refs_2_), channel_id=1, source_target_pairs={{0,1},{1,0},{2,3},{3,2},{4,5},{5,4},{6,7},{7,6},{8,9},{9,8},{10,11... | collective-permute-start | bytes 786440 | tf_op jit(solution)/shard_map/ppermute | solution.py:526
  72.4 10.5 %collective-permute-start.8 = (bf16[1024,128]{1,0:T(8,128)(2,1)S(1)}, bf16[1024,128]{1,0:T(8,128)(2,1)S(1)}, u32[]{:S(2)}, u32[]{:S(2)}) collective-permute-start(bf16[1024,128]{1,0:T(8,128)(2,1)S(1)} %collective-permute-done.3.refs_3_), channel_id=1, source_target_pairs={{0,1},{1,0},{2,3},{3,2},{4,5},{5,4},{6,7},{7,6},{8,9},{9,8},{10,11... | collective-permute-start | bytes 786440 | tf_op jit(solution)/shard_map/ppermute | solution.py:526
  86.4 6.8 %collective-permute-start.10 = (bf16[128,2048]{1,0:T(8,128)(2,1)}, bf16[128,2048]{1,0:T(8,128)(2,1)S(1)}, u32[]{:S(2)}, u32[]{:S(2)}) collective-permute-start(bf16[128,2048]{1,0:T(8,128)(2,1)} %get-tuple-element.93), channel_id=1, source_target_pairs={{0,1},{1,0},{2,3},{3,2},{4,5},{5,4},{6,7},{7,6},{8,9},{9,8},{10,11... | collective-permute-start | bytes 1572872 | tf_op jit(solution)/shard_map/ppermute | solution.py:526
  89.4 5.2 %collective-permute-start.11 = (bf16[128,2048]{1,0:T(8,128)(2,1)}, bf16[128,2048]{1,0:T(8,128)(2,1)S(1)}, u32[]{:S(2)}, u32[]{:S(2)}) collective-permute-start(bf16[128,2048]{1,0:T(8,128)(2,1)} %get-tuple-element.94), channel_id=1, source_target_pairs={{0,1},{1,0},{2,3},{3,2},{4,5},{5,4},{6,7},{7,6},{8,9},{9,8},{10,11... | collective-permute-start | bytes 1572872 | tf_op jit(solution)/shard_map/ppermute | solution.py:526
  89.4 20.4 %collective-permute-start.12 = (bf16[128,2048]{1,0:T(8,128)(2,1)}, bf16[128,2048]{1,0:T(8,128)(2,1)S(1)}, u32[]{:S(2)}, u32[]{:S(2)}) collective-permute-start(bf16[128,2048]{1,0:T(8,128)(2,1)} %get-tuple-element.95), channel_id=1, source_target_pairs={{0,1},{1,0},{2,3},{3,2},{4,5},{5,4},{6,7},{7,6},{8,9},{9,8},{10,11... | collective-permute-start | bytes 1572872 | tf_op jit(solution)/shard_map/ppermute | solution.py:526
  89.9 19.9 %collective-permute-start.9 = (bf16[128,2048]{1,0:T(8,128)(2,1)}, bf16[128,2048]{1,0:T(8,128)(2,1)S(1)}, u32[]{:S(2)}, u32[]{:S(2)}) collective-permute-start(bf16[128,2048]{1,0:T(8,128)(2,1)} %get-tuple-element.92), channel_id=1, source_target_pairs={{0,1},{1,0},{2,3},{3,2},{4,5},{5,4},{6,7},{7,6},{8,9},{9,8},{10,11... | collective-permute-start | bytes 1572872 | tf_op jit(solution)/shard_map/ppermute | solution.py:526
  92.0 23.6 %collective-permute-start.13 = (bf16[2,128,512]{2,1,0:T(8,128)(2,1)}, bf16[2,128,512]{2,1,0:T(8,128)(2,1)}, u32[]{:S(2)}, u32[]{:S(2)}) collective-permute-start(bf16[2,128,512]{2,1,0:T(8,128)(2,1)} %get-tuple-element.101), channel_id=1, source_target_pairs={{2,0},{3,1},{4,2},{5,3},{6,4},{7,5},{10,8},{11,9},{12,10},{13,11},... | collective-permute-start | bytes 786440 | tf_op jit(solution)/shard_map/ppermute | solution.py:535
  93.3 16.6 %copy-start.6 = (bf16[128,2048]{1,0:T(8,128)(2,1)}, bf16[128,2048]{1,0:T(8,128)(2,1)S(1)}, u32[]{:S(2)}) copy-start(bf16[128,2048]{1,0:T(8,128)(2,1)S(1)} %collective-permute-done.10.o_b) | copy-start | bytes 1572868
  93.3 22.3 %collective-permute-start.14 = (bf16[2,128,512]{2,1,0:T(8,128)(2,1)}, bf16[2,128,512]{2,1,0:T(8,128)(2,1)}, u32[]{:S(2)}, u32[]{:S(2)}) collective-permute-start(bf16[2,128,512]{2,1,0:T(8,128)(2,1)} %get-tuple-element.103), channel_id=1, source_target_pairs={{4,0},{5,1},{6,2},{7,3},{12,8},{13,9},{14,10},{15,11},{20,16},{21,... | collective-permute-start | bytes 786440 | tf_op jit(solution)/shard_map/ppermute | solution.py:535
  94.6 15.3 %copy-start.7 = (bf16[128,2048]{1,0:T(8,128)(2,1)}, bf16[128,2048]{1,0:T(8,128)(2,1)S(1)}, u32[]{:S(2)}) copy-start(bf16[128,2048]{1,0:T(8,128)(2,1)S(1)} %collective-permute-done.11.dq_a) | copy-start | bytes 1572868
  94.6 20.9 %collective-permute-start.15 = (bf16[2,128,512]{2,1,0:T(8,128)(2,1)}, bf16[2,128,512]{2,1,0:T(8,128)(2,1)}, u32[]{:S(2)}, u32[]{:S(2)}) collective-permute-start(bf16[2,128,512]{2,1,0:T(8,128)(2,1)} %get-tuple-element.102), channel_id=1, source_target_pairs={{6,0},{7,1},{14,8},{15,9},{22,16},{23,17},{30,24},{31,25},{38,32},... | collective-permute-start | bytes 786440 | tf_op jit(solution)/shard_map/ppermute | solution.py:535
  95.9 29.8 %all-to-all-start.4 = ((bf16[32,32,512]{2,1,0:T(8,128)(2,1)}), bf16[32,32,512]{2,1,0:T(8,128)(2,1)S(1)}, u32[]{:S(2)}, u32[]{:S(2)}) async-start(bf16[32,32,512]{2,1,0:T(8,128)(2,1)} %bitcast.9), calls=%async_computation.4 | async-start | bytes 2097152 | tf_op jit(solution)/shard_map/all_to_all | solution.py:563
  117.0 1.6 %collective-permute-start.16 = (bf16[2,128,512]{2,1,0:T(8,128)(2,1)S(1)}, bf16[2,128,512]{2,1,0:T(8,128)(2,1)S(1)}, u32[]{:S(2)}, u32[]{:S(2)}) collective-permute-start(bf16[2,128,512]{2,1,0:T(8,128)(2,1)S(1)} %fusion.6), channel_id=1, source_target_pairs={{0,1},{1,0},{2,3},{3,2},{4,5},{5,4},{6,7},{7,6},{8,9},{9,8},{10,11... | collective-permute-start | bytes 786440 | tf_op jit(solution)/shard_map/ppermute | solution.py:526
  (9 other events, 41.9 us)

commit v7 on v6

--- a/solution.py
+++ b/solution.py
@@ -156,7 +156,7 @@
 def output_kernel(
     place, parents, labels,
     q_own, q_par, g_own, g_par, keys, vals, stats,
-    o_own, o_par, dq_own, dq_par, dk_out,
+    o_own, o_par, dq_own, dq_par, dk0, dk1, dk2, dk3,
     chain, k_pair, v_pair, kt_pair, vt_pair, q_st, g_st, gt_st, w_st, ds_st, in_st, ot_st, dqt_st, dk_acc,
 ):
     y = place[0]
@@ -235,13 +235,15 @@
 
     one_block(0, 2 * y + c, q_own, g_own, o_own, dq_own)
     one_block(1, 2 * y + 1 - c, q_par, g_par, o_par, dq_par)
-    for s in range(SLOTS):
-        for n in heads:
-            dk_out[s, :, n * HD : (n + 1) * HD] = (dk_acc[n, s] * SCALE).astype(LOW)
+    for d, out in enumerate((dk0, dk1, dk2, dk3)):
+        for e in range(2):
+            s = 2 * jnp.maximum(y - d, 0) + e
+            for n in heads:
+                out[e, :, n * HD : (n + 1) * HD] = (dk_acc[n, s] * SCALE).astype(LOW)
 
 
 def output_onward_kernel(*refs):
-    output_kernel(*refs[:10], *refs[13:])
+    output_kernel(*refs[:10], *refs[16:])
 
 
 ROWS = GRP * BLK
@@ -306,12 +308,14 @@
     own, partner, partner_out = own_spec(start), partner_spec(start), partner_spec(0)
     own_shape = jax.ShapeDtypeStruct((BLK, 2 * HALF * QW), LOW)
     partner_shape = jax.ShapeDtypeStruct((BLK, NG * QW), LOW)
+    grads = pl.BlockSpec((2, BLK, NG * HD), lambda i, place, par, lab: (0, 0, start + i))
+    grads_shape = jax.ShapeDtypeStruct((2, BLK, HALF * HD), LOW)
     return attention_call(
         output_onward_kernel if before else output_kernel, "tree_outputs", 1,
         [own, partner, own, partner, blocks_spec(start), blocks_spec(start), stats_spec(start)]
         + [pl.BlockSpec(memory_space=pl.ANY)] * len(before),
-        [own, partner_out, own, partner_out, blocks_spec(start)],
-        [own_shape, partner_shape, own_shape, partner_shape, jax.ShapeDtypeStruct((SLOTS, BLK, HALF * HD), LOW)],
+        [own, partner_out, own, partner_out] + [grads] * NY,
+        [own_shape, partner_shape, own_shape, partner_shape] + [grads_shape] * NY,
         [
             ((NG, PAIRS, 2 * BLK, HD), LOW),
             ((NG, PAIRS, 2 * BLK, HD), LOW),
@@ -327,7 +331,7 @@
             ((NG, HD, ROWS), F32),
             ((NG, SLOTS, BLK, HD), F32),
         ],
-        {10: 0, 11: 2, 12: 4} if before else {},
+        {10: 0, 11: 2, 12: 4, 13: 5, 14: 6, 15: 7} if before else {},
     )(*args, *before)
 
 
@@ -464,51 +468,6 @@
     )(place, x)
 
 
-def sum_kernel(terms, out, total, done):
-    for e in range(2):
-        acc = terms[0, e].astype(F32)
-        for i in range(1, NY):
-            acc = acc + terms[i, e].astype(F32)
-        total[e] = acc.astype(LOW)
-    copies = [pltpu.make_async_copy(total, out.at[i], done.at[i]) for i in range(NZ)]
-    for copy in copies:
-        copy.start()
-    for copy in copies:
-        copy.wait()
-
-
-def sum_blocks(terms):
-    return pl.pallas_call(
-        sum_kernel,
-        out_shape=jax.ShapeDtypeStruct((NZ,) + terms.shape[1:], LOW),
-        out_specs=pl.BlockSpec(memory_space=pl.ANY),
-        scratch_shapes=[pltpu.VMEM(terms.shape[1:], LOW), pltpu.SemaphoreType.DMA((NZ,))],
-        compiler_params=pltpu.CompilerParams(vmem_limit_bytes=60 * 2**20),
-        cost_estimate=LIGHT,
-        name="sum_blocks",
-    )(terms)
-
-
-def finish_kernel(parts, out):
-    width = parts.shape[2]
-    for half in range(2):
-        acc = parts[half].astype(F32)
-        for i in range(1, NX * NY):
-            acc = acc + parts[2 * i + half].astype(F32)
-        out[:, half * width : (half + 1) * width] = acc * (16 * SLOTS * BLK) ** -0.5
-
-
-def finish_weight(parts):
-    rows, width = parts.shape[1:]
-    return pl.pallas_call(
-        finish_kernel,
-        out_shape=jax.ShapeDtypeStruct((rows, 2 * width), F32),
-        compiler_params=pltpu.CompilerParams(vmem_limit_bytes=60 * 2**20),
-        cost_estimate=LIGHT,
-        name="finish_weight",
-    )(parts)
-
-
 def device(x, z, y, c):
     return (x * NZ + z) * SLOTS + y * 2 + c
 
@@ -545,25 +504,27 @@
     dv, vals, x_own = lax.optimization_barrier((dv, vals, x_own))
     dv = lax.all_to_all(dv.reshape(NY, 2, BLK, HALF * HD), "ctx", 0, 0, axis_index_groups=along_y)
     args = (place, parents, labels, q, q_par, g, g_par, keys, vals, stats)
-    o_own, o_par, dq_own, dq_par, dk = output_and_gradients(0, (), *args)
+    o_own, o_par, dq_own, dq_par, *dk = output_and_gradients(0, (), *args)
     o_pars, dq_pars = [o_par], [dq_par]
     dv, dk, x_own = lax.optimization_barrier((dv, dk, x_own))
     x_other = [swap(a) for a in x_own]
-    dv_sends = sum_blocks(dv)
+    dv_sum = sum(dv[i].astype(F32) for i in range(NY)).astype(LOW)
+    dv_sends = jnp.broadcast_to(dv_sum[None], dv.shape)
     dv_sends, dk = lax.optimization_barrier((dv_sends, dk))
     dv_all = lax.all_to_all(dv_sends, "dp", 0, 0, axis_index_groups=along_z)
-    o_own, o_par, dq_own, dq_par, dk = output_and_gradients(1, (o_own, dq_own, dk), *args)
+    o_own, o_par, dq_own, dq_par, *dk = output_and_gradients(1, (o_own, dq_own, *dk), *args)
     o_pars, dq_pars = o_pars + [o_par], dq_pars + [dq_par]
     dv_all, dk = lax.optimization_barrier((dv_all, dk))
-    dk = dk.reshape(NY, 2, BLK, HALF * HD)
-    received = [earlier(pick(dk, jnp.maximum(y - d, 0)), d) for d in range(1, NY)]
+    received = [earlier(dk[d], d) for d in range(1, NY)]
     partial = weight_partial(place, x_own, x_other, dv_all).reshape(2 * NX * NY, -1, HALF * HD)
     _, o_pars, dq_pars = lax.optimization_barrier((partial, o_pars, dq_pars))
     o_pars, dq_pars = [swap(a) for a in o_pars], [swap(a) for a in dq_pars]
-    weight_grad = finish_weight(lax.all_to_all(partial, ("dp", "ctx"), 0, 0, axis_index_groups=across))
+    shares = lax.all_to_all(partial, ("dp", "ctx"), 0, 0, axis_index_groups=across)
+    total = jnp.sum(shares.reshape(NX * NY, 2, *shares.shape[1:]).astype(F32), axis=0)
+    weight_grad = jnp.concatenate([total[0], total[1]], axis=1) * (16 * SLOTS * BLK) ** -0.5
     out, query_grad = fill_partner(place, o_own, dq_own, o_pars, dq_pars)
     dk, query_grad = lax.optimization_barrier((dk, query_grad))
-    dk_sum = pick(dk, y).astype(F32)
+    dk_sum = dk[0].astype(F32)
     for term in received:
         dk_sum = dk_sum + term.astype(F32)
     both = jnp.stack([dk_sum.astype(LOW), dv_sends[0]], axis=1)

time: 129 us -> 124 us (0.961)
  Pallas kernels: 48.4 us -> 44 us
  local copies, waits for them, and re-layouts: 5.96 us -> 3.54 us
  starting transfers between devices: 49.9 us -> 52 us
    pallas_call x2 -> x0, Pallas kernels: 4.44 us -> none  [the longest x1 2.42 us: sum_blocks(): pl.pallas_call(sum_kernel, out_shape=jax.ShapeDtypeStruct((NZ,) + terms.s...]
    all_to_all x1, starting transfers between devices: 5.04 us -> 7.39 us  [per_device(): dv_all = lax.all_to_all(dv_sends, 'dp', 0, 0, axis_index_groups=along_z)]
    squeeze x1, local copies, waits for them, and re-layouts: 2.07 us -> 0.01 us  [per_device(): total[0]]
    unnamed x22 -> x24, local copies, waits for them, and re-layouts: 2.92 us -> 1.5 us
  transfers between devices with their start and end apart: 22 -> 22, of which waited for: 7 -> 8; matrix products, arithmetic and copies ran while one was open for 5% -> 3% of each run, Pallas kernels for 29% -> 30%
where the time goes in v7:
time: 124 us; the launch traced here: 125 us
  starting transfers between devices  52 us (42%)
  Pallas kernels  44 us (35%)
  waiting for transfers between devices  20.7 us (17%)
  other arithmetic  3.71 us (3%)
  local copies, waits for them, and re-layouts  3.54 us (3%)
    pallas_call x2, Pallas kernels, output_and_gradients(): attention_call(output_onward_kernel if before else output_kernel, 'tree_o...  17.8 us
    all_to_all x1, starting transfers between devices, per_device(): lax.all_to_all(partial, ('dp', 'ctx'), 0, 0, axis_index_groups=across)  12.4 us
    pallas_call x1, Pallas kernels, value_gradient(): attention_call(values_kernel, 'tree_values', HALF // NG, [own, partner, o...  9.05 us
    all_to_all x1, starting transfers between devices, per_device(): dv_all = lax.all_to_all(dv_sends, 'dp', 0, 0, axis_index_groups=along_z)  7.39 us
    ppermute x3, starting transfers between devices, further(): lax.ppermute(a, 'dp', [(i, i // NZ * NZ + (i + d) % NZ) for i in range(NX...  7.36 us
    ppermute x11, starting transfers between devices, swap(): return lax.ppermute(a, 'ctx', [(i, i ^ 1) for i in range(SLOTS)])  7.2 us
    all_to_all x1, starting transfers between devices, per_device(): keys = lax.all_to_all(k_sends, 'ctx', 0, 0)  5.98 us
    all_to_all x1, waiting for transfers between devices, per_device(): lax.all_to_all(partial, ('dp', 'ctx'), 0, 0, axis_index_groups=across)  5.73 us
  transfers between devices with their start and end apart: 22, of which 8 were waited for; matrix products, arithmetic and copies ran while one was open for 3% of the time, Pallas kernels for 30%

profile of v7, /device:TPU:1, one launch (start us, length us, event | category | flops | bytes accessed | tf_op | source)
XLA Modules:
  0.0 124.9 jit_solution(6986681623329542344)
XLA Ops:
  0.6 2.5 %halves.1 = (bf16[8,128,512]{2,1,0:T(8,128)(2,1)}, bf16[8,128,512]{2,1,0:T(8,128)(2,1)}) custom-call(bf16[128,1024]{1,0:T(8,128)(2,1)} %bitcast.45, bf16[128,1024]{1,0:T(8,128)(2,1)} %bitcast.46), custom_call_target="tpu_custom_call" | custom-call | flops 1 | bytes 1 | tf_op jit(solution)/shard_map/halves/pallas_call | solution.py:382
  3.1 6.0 %all-to-all-start = ((bf16[8,128,512]{2,1,0:T(8,128)(2,1)}), bf16[8,128,512]{2,1,0:T(8,128)(2,1)S(1)}, u32[]{:S(2)}, u32[]{:S(2)}) async-start(bf16[8,128,512]{2,1,0:T(8,128)(2,1)} %get-tuple-element.70), calls=%async_computation | async-start | bytes 2097152 | tf_op jit(solution)/shard_map/all_to_all | solution.py:497
  9.7 3.1 %x_sends.1 = (bf16[1024,128]{1,0:T(8,128)(2,1)}, bf16[1024,128]{1,0:T(8,128)(2,1)}, bf16[1024,128]{1,0:T(8,128)(2,1)}, bf16[1024,128]{1,0:T(8,128)(2,1)}) custom-call(s32[3]{0:T(128)} %pad_add_fusion.place.refs_0_, bf16[128,4096]{1,0:T(8,128)(2,1)} %bitcast.43), custom_call_target="tpu_custom_call" | custom-call | flops 1 | bytes 1 | tf_op jit(solution)/shard_map/x_sends/pallas_call | solution.py:457
  12.8 1.6 %collective-permute-start.2 = (bf16[1024,128]{1,0:T(8,128)(2,1)}, bf16[1024,128]{1,0:T(8,128)(2,1)S(1)}, u32[]{:S(2)}, u32[]{:S(2)}) collective-permute-start(bf16[1024,128]{1,0:T(8,128)(2,1)} %get-tuple-element.72), channel_id=1, source_target_pairs={{0,8},{8,16},{16,24},{24,0},{32,40},{40,48},{48,56},{56,32},{64,72... | collective-permute-start | bytes 786440 | tf_op jit(solution)/shard_map/ppermute | solution.py:491
  14.4 2.1 %collective-permute-start.3 = (bf16[1024,128]{1,0:T(8,128)(2,1)}, bf16[1024,128]{1,0:T(8,128)(2,1)S(1)}, u32[]{:S(2)}, u32[]{:S(2)}) collective-permute-start(bf16[1024,128]{1,0:T(8,128)(2,1)} %get-tuple-element.73), channel_id=1, source_target_pairs={{0,24},{8,0},{16,8},{24,16},{32,56},{40,32},{48,40},{56,48},{64,88... | collective-permute-start | bytes 786440 | tf_op jit(solution)/shard_map/ppermute | solution.py:491
  16.5 3.3 %partner_halves.1 = (bf16[128,4096]{1,0:T(8,128)(2,1)}, bf16[128,4096]{1,0:T(8,128)(2,1)}) custom-call(s32[3]{0:T(128)} %pad_add_fusion.place.refs_0_, bf16[128,8192]{1,0:T(8,128)(2,1)} %bitcast.32, bf16[128,8192]{1,0:T(8,128)(2,1)} %bitcast.36), custom_call_target="tpu_custom_call" | custom-call | flops 1 | bytes 1 | tf_op jit(solution)/shard_map/partner_halves/pallas_call | solution.py:401
  20.3 3.1 %collective-permute-done.2.refs_1_ = bf16[1024,128]{1,0:T(8,128)(2,1)S(1)} collective-permute-done((bf16[1024,128]{1,0:T(8,128)(2,1)}, bf16[1024,128]{1,0:T(8,128)(2,1)S(1)}, u32[]{:S(2)}, u32[]{:S(2)}) %collective-permute-start.2) | collective-permute-done | bytes 262176 | tf_op jit(solution)/shard_map/ppermute | solution.py:491
  24.2 4.3 %all-to-all-start.1 = ((bf16[8,128,512]{2,1,0:T(8,128)(2,1)}), bf16[8,128,512]{2,1,0:T(8,128)(2,1)S(1)}, u32[]{:S(2)}, u32[]{:S(2)}) async-start(bf16[8,128,512]{2,1,0:T(8,128)(2,1)} %get-tuple-element.76), calls=%async_computation.1 | async-start | bytes 2097152 | tf_op jit(solution)/shard_map/all_to_all | solution.py:502
  28.6 3.6 %collective-permute-start.4 = (bf16[1024,128]{1,0:T(8,128)(2,1)S(1)}, bf16[1024,128]{1,0:T(8,128)(2,1)S(1)}, u32[]{:S(2)}, u32[]{:S(2)}) collective-permute-start(bf16[1024,128]{1,0:T(8,128)(2,1)S(1)} %copy-done.11), channel_id=1, source_target_pairs={{0,16},{8,24},{16,0},{24,8},{32,48},{40,56},{48,32},{56,40},{64,80... | collective-permute-start | bytes 786440 | tf_op jit(solution)/shard_map/ppermute | solution.py:491
  32.2 9.0 %tree_values.1 = (bf16[8,128,512]{2,1,0:T(8,128)(2,1)}, f32[4,2,8,1024]{3,2,1,0:T(8,128)}) custom-call(s32[3]{0:T(128)} %pad_add_fusion.place.refs_0_, s32[1,8]{1,0:T(1,128)} %refs_1_.1, s32[1,8]{1,0:T(1,128)} %refs_2_.1, bf16[128,8192]{1,0:T(8,128)(2,1)} %bitcast.33, bf16[128,4096]{1,0:T(8,128)(2,1)} %collective-permute-done.q_par.refs_4_, ...), custom_call_target="tpu_custom_call" | custom-call | flops 1 | bytes 1 | tf_op jit(solution)/shard_map/tree_values/pallas_call | solution.py:288
  41.2 2.5 %all-to-all-done.1.vals.refs_8_ = bf16[8,128,512]{2,1,0:T(8,128)(2,1)S(1)} async-done(((bf16[8,128,512]{2,1,0:T(8,128)(2,1)}), bf16[8,128,512]{2,1,0:T(8,128)(2,1)S(1)}, u32[]{:S(2)}, u32[]{:S(2)}) %all-to-all-start.1) | async-done | bytes 1048608 | tf_op jit(solution)/shard_map/all_to_all | solution.py:502
  43.7 3.5 %all-to-all-start.2 = ((bf16[4,2,128,512]{3,2,1,0:T(8,128)(2,1)}), bf16[4,2,128,512]{3,2,1,0:T(8,128)(2,1)S(1)}, u32[]{:S(2)}, u32[]{:S(2)}) async-start(bf16[4,2,128,512]{3,2,1,0:T(8,128)(2,1)} %bitcast.44), calls=%async_computation.2 | async-start | bytes 2097152 | tf_op jit(solution)/shard_map/all_to_all | solution.py:505
  47.2 8.8 %tree_outputs.2 = (bf16[128,8192]{1,0:T(8,128)(2,1)}, bf16[128,2048]{1,0:T(8,128)(2,1)}, bf16[128,8192]{1,0:T(8,128)(2,1)}, bf16[128,2048]{1,0:T(8,128)(2,1)}, b...) custom-call(s32[3]{0:T(128)} %pad_add_fusion.place.refs_0_, ...), custom_call_target="tpu_custom_call" | custom-call | flops 1 | bytes 1 | tf_op jit(solution)/shard_map/tree_outputs/pallas_call | solution.py:313
  56.0 5.4 %all-to-all-done.2 = bf16[4,2,128,512]{3,2,1,0:T(8,128)(2,1)S(1)} async-done(((bf16[4,2,128,512]{3,2,1,0:T(8,128)(2,1)}), bf16[4,2,128,512]{3,2,1,0:T(8,128)(2,1)S(1)}, u32[]{:S(2)}, u32[]{:S(2)}) %all-to-all-start.2) | async-done | bytes 1048608 | tf_op jit(solution)/shard_map/all_to_all | solution.py:505
  62.6 7.4 %all-to-all-start.3 = ((bf16[4,2,128,512]{3,2,1,0:T(8,128)(2,1)}), bf16[4,2,128,512]{3,2,1,0:T(8,128)(2,1)S(1)}, u32[]{:S(2)}, u32[]{:S(2)}) async-start(bf16[4,2,128,512]{3,2,1,0:T(8,128)(2,1)} %broadcast_in_dim.15), calls=%async_computation.3 | async-start | bytes 2097152 | tf_op jit(solution)/shard_map/all_to_all | solution.py:514
  70.0 2.1 %collective-permute-start.5 = (bf16[1024,128]{1,0:T(8,128)(2,1)S(1)}, bf16[1024,128]{1,0:T(8,128)(2,1)S(1)}, u32[]{:S(2)}, u32[]{:S(2)}) collective-permute-start(bf16[1024,128]{1,0:T(8,128)(2,1)S(1)} %copy-done), channel_id=1, source_target_pairs={{0,1},{1,0},{2,3},{3,2},{4,5},{5,4},{6,7},{7,6},{8,9},{9,8},{10,11... | collective-permute-start | bytes 786440 | tf_op jit(solution)/shard_map/ppermute | solution.py:485
  72.8 9.0 %tree_outputs.3 = (bf16[128,8192]{1,0:T(8,128)(2,1)}, bf16[128,2048]{1,0:T(8,128)(2,1)}, bf16[128,8192]{1,0:T(8,128)(2,1)}, bf16[128,2048]{1,0:T(8,128)(2,1)}, b...) custom-call(s32[3]{0:T(128)} %pad_add_fusion.place.refs_0_, ...), custom_call_target="tpu_custom_call", output_to_operand_aliasing={{0}: (10, {}), {2}: (11, {}), {4}: (12, {}), {5}: (13, {}),... | custom-call | flops 1 | bytes 1 | tf_op jit(solution)/shard_map/tree_outputs/pallas_call | solution.py:313
  81.7 1.3 %all-to-all-done.3.refs_8_ = bf16[4,2,128,512]{3,2,1,0:T(8,128)(2,1)S(1)} async-done(((bf16[4,2,128,512]{3,2,1,0:T(8,128)(2,1)}), bf16[4,2,128,512]{3,2,1,0:T(8,128)(2,1)S(1)}, u32[]{:S(2)}, u32[]{:S(2)}) %all-to-all-start.3) | async-done | bytes 1048608 | tf_op jit(solution)/shard_map/all_to_all | solution.py:514
  83.1 3.5 %weight_partial.1 = bf16[1024,512]{1,0:T(8,128)(2,1)} custom-call(s32[3]{0:T(128)S(1)} %copy-done.1, bf16[1024,128]{1,0:T(8,128)(2,1)S(1)} %copy-done, bf16[1024,128]{1,0:T(8,128)(2,1)S(1)} %collective-permute-done.2.refs_1_, bf16[1024,128]{1,0:T(8,128)(2,1)S(1)} %collective-permute-done.4.refs_2_, bf16[1024,128]{1,0:T(8,128)(2,1)S(1)} %collective-permute-done.3.refs_3_, ...), custom_call_target="tpu_custom_call" | custom-call | flops 1 | bytes 1 | tf_op jit(solution)/shard_map/weight_partial/pallas_call | solution.py:351
  86.5 3.1 %collective-permute-start.10 = (bf16[128,2048]{1,0:T(8,128)(2,1)S(1)}, bf16[128,2048]{1,0:T(8,128)(2,1)S(1)}, u32[]{:S(2)}, u32[]{:S(2)}) collective-permute-start(bf16[128,2048]{1,0:T(8,128)(2,1)S(1)} %copy-done.10), channel_id=1, source_target_pairs={{0,1},{1,0},{2,3},{3,2},{4,5},{5,4},{6,7},{7,6},{8,9},{9,8},{10,11... | collective-permute-start | bytes 1572872 | tf_op jit(solution)/shard_map/ppermute | solution.py:485
  94.7 12.4 %all-to-all-start.4 = ((bf16[32,32,512]{2,1,0:T(8,128)(2,1)}), bf16[32,32,512]{2,1,0:T(8,128)(2,1)S(1)}, u32[]{:S(2)}, u32[]{:S(2)}) async-start(bf16[32,32,512]{2,1,0:T(8,128)(2,1)} %bitcast.10), calls=%async_computation.4 | async-start | bytes 2097152 | tf_op jit(solution)/shard_map/all_to_all | solution.py:522
  108.9 4.9 %fill_partner.1 = (bf16[128,8192]{1,0:T(8,128)(2,1)}, bf16[128,8192]{1,0:T(8,128)(2,1)}) custom-call(s32[3]{0:T(128)} %pad_add_fusion.place.refs_0_, bf16[128,8192]{1,0:T(8,128)(2,1)} %get-tuple-element.103.o_before, bf16[128,8192]{1,0:T(8,128)(2,1)} %get-tuple-element.104.dq_before, ...), custom_call_target="tpu_custom_call", output_to_operand_aliasing={{0}: (1, {}), {1}: (2, {})} | custom-call | flops 1 | bytes 1 | tf_op jit(solution)/shard_map/fill_partner/pallas_call | solution.py:431
  116.1 1.3 %collective-permute-done.16 = bf16[2,128,512]{2,1,0:T(8,128)(2,1)S(1)} collective-permute-done((bf16[2,128,512]{2,1,0:T(8,128)(2,1)S(1)}, bf16[2,128,512]{2,1,0:T(8,128)(2,1)S(1)}, u32[]{:S(2)}, u32[]{:S(2)}) %collective-permute-start.16) | collective-permute-done | bytes 262176 | tf_op jit(solution)/shard_map/ppermute | solution.py:485
  118.3 5.7 %all-to-all-done.4 = bf16[32,32,512]{2,1,0:T(8,128)(2,1)S(1)} async-done(((bf16[32,32,512]{2,1,0:T(8,128)(2,1)}), bf16[32,32,512]{2,1,0:T(8,128)(2,1)S(1)}, u32[]{:S(2)}, u32[]{:S(2)}) %all-to-all-start.4) | async-done | bytes 1048608 | tf_op jit(solution)/shard_map/all_to_all | solution.py:522
  (63 shorter events, 14.5 us)
Async XLA Ops:
  3.1 21.1 %all-to-all-start = ((bf16[8,128,512]{2,1,0:T(8,128)(2,1)}), bf16[8,128,512]{2,1,0:T(8,128)(2,1)S(1)}, u32[]{:S(2)}, u32[]{:S(2)}) async-start(bf16[8,128,512]{2,1,0:T(8,128)(2,1)} %get-tuple-element.70), calls=%async_computation | async-start | bytes 2097152 | tf_op jit(solution)/shard_map/all_to_all | solution.py:497
  12.8 10.6 %collective-permute-start.2 = (bf16[1024,128]{1,0:T(8,128)(2,1)}, bf16[1024,128]{1,0:T(8,128)(2,1)S(1)}, u32[]{:S(2)}, u32[]{:S(2)}) collective-permute-start(bf16[1024,128]{1,0:T(8,128)(2,1)} %get-tuple-element.72), channel_id=1, source_target_pairs={{0,8},{8,16},{16,24},{24,0},{32,40},{40,48},{48,56},{56,32},{64,72... | collective-permute-start | bytes 786440 | tf_op jit(solution)/shard_map/ppermute | solution.py:491
  14.4 9.0 %collective-permute-start.3 = (bf16[1024,128]{1,0:T(8,128)(2,1)}, bf16[1024,128]{1,0:T(8,128)(2,1)S(1)}, u32[]{:S(2)}, u32[]{:S(2)}) collective-permute-start(bf16[1024,128]{1,0:T(8,128)(2,1)} %get-tuple-element.73), channel_id=1, source_target_pairs={{0,24},{8,0},{16,8},{24,16},{32,56},{40,32},{48,40},{56,48},{64,88... | collective-permute-start | bytes 786440 | tf_op jit(solution)/shard_map/ppermute | solution.py:491
  19.8 12.4 %collective-permute-start = (bf16[128,4096]{1,0:T(8,128)(2,1)}, bf16[128,4096]{1,0:T(8,128)(2,1)}, u32[]{:S(2)}, u32[]{:S(2)}) collective-permute-start(bf16[128,4096]{1,0:T(8,128)(2,1)} %get-tuple-element.68), channel_id=1, source_target_pairs={{0,1},{1,0},{2,3},{3,2},{4,5},{5,4},{6,7},{7,6},{8,9},{9,8},{10,11... | collective-permute-start | bytes 3145736 | tf_op jit(solution)/shard_map/ppermute | solution.py:485
  20.1 12.1 %collective-permute-start.1 = (bf16[128,4096]{1,0:T(8,128)(2,1)}, bf16[128,4096]{1,0:T(8,128)(2,1)}, u32[]{:S(2)}, u32[]{:S(2)}) collective-permute-start(bf16[128,4096]{1,0:T(8,128)(2,1)} %get-tuple-element.69), channel_id=1, source_target_pairs={{0,1},{1,0},{2,3},{3,2},{4,5},{5,4},{6,7},{7,6},{8,9},{9,8},{10,11... | collective-permute-start | bytes 3145736 | tf_op jit(solution)/shard_map/ppermute | solution.py:485
  24.2 19.4 %all-to-all-start.1 = ((bf16[8,128,512]{2,1,0:T(8,128)(2,1)}), bf16[8,128,512]{2,1,0:T(8,128)(2,1)S(1)}, u32[]{:S(2)}, u32[]{:S(2)}) async-start(bf16[8,128,512]{2,1,0:T(8,128)(2,1)} %get-tuple-element.76), calls=%async_computation.1 | async-start | bytes 2097152 | tf_op jit(solution)/shard_map/all_to_all | solution.py:502
  28.6 12.7 %collective-permute-start.4 = (bf16[1024,128]{1,0:T(8,128)(2,1)S(1)}, bf16[1024,128]{1,0:T(8,128)(2,1)S(1)}, u32[]{:S(2)}, u32[]{:S(2)}) collective-permute-start(bf16[1024,128]{1,0:T(8,128)(2,1)S(1)} %copy-done.11), channel_id=1, source_target_pairs={{0,16},{8,24},{16,0},{24,8},{32,48},{40,56},{48,32},{56,40},{64,80... | collective-permute-start | bytes 786440 | tf_op jit(solution)/shard_map/ppermute | solution.py:491
  43.7 17.8 %all-to-all-start.2 = ((bf16[4,2,128,512]{3,2,1,0:T(8,128)(2,1)}), bf16[4,2,128,512]{3,2,1,0:T(8,128)(2,1)S(1)}, u32[]{:S(2)}, u32[]{:S(2)}) async-start(bf16[4,2,128,512]{3,2,1,0:T(8,128)(2,1)} %bitcast.44), calls=%async_computation.2 | async-start | bytes 2097152 | tf_op jit(solution)/shard_map/all_to_all | solution.py:505
  62.6 20.4 %all-to-all-start.3 = ((bf16[4,2,128,512]{3,2,1,0:T(8,128)(2,1)}), bf16[4,2,128,512]{3,2,1,0:T(8,128)(2,1)S(1)}, u32[]{:S(2)}, u32[]{:S(2)}) async-start(bf16[4,2,128,512]{3,2,1,0:T(8,128)(2,1)} %broadcast_in_dim.15), calls=%async_computation.3 | async-start | bytes 2097152 | tf_op jit(solution)/shard_map/all_to_all | solution.py:514
  70.0 13.0 %collective-permute-start.5 = (bf16[1024,128]{1,0:T(8,128)(2,1)S(1)}, bf16[1024,128]{1,0:T(8,128)(2,1)S(1)}, u32[]{:S(2)}, u32[]{:S(2)}) collective-permute-start(bf16[1024,128]{1,0:T(8,128)(2,1)S(1)} %copy-done), channel_id=1, source_target_pairs={{0,1},{1,0},{2,3},{3,2},{4,5},{5,4},{6,7},{7,6},{8,9},{9,8},{10,11... | collective-permute-start | bytes 786440 | tf_op jit(solution)/shard_map/ppermute | solution.py:485
  72.2 10.9 %collective-permute-start.6 = (bf16[1024,128]{1,0:T(8,128)(2,1)S(1)}, bf16[1024,128]{1,0:T(8,128)(2,1)S(1)}, u32[]{:S(2)}, u32[]{:S(2)}) collective-permute-start(bf16[1024,128]{1,0:T(8,128)(2,1)S(1)} %collective-permute-done.2.refs_1_), channel_id=1, source_target_pairs={{0,1},{1,0},{2,3},{3,2},{4,5},{5,4},{6,7},{7,6},{8,9},{9,8},{10,11... | collective-permute-start | bytes 786440 | tf_op jit(solution)/shard_map/ppermute | solution.py:485
  72.3 10.8 %collective-permute-start.7 = (bf16[1024,128]{1,0:T(8,128)(2,1)S(1)}, bf16[1024,128]{1,0:T(8,128)(2,1)S(1)}, u32[]{:S(2)}, u32[]{:S(2)}) collective-permute-start(bf16[1024,128]{1,0:T(8,128)(2,1)S(1)} %collective-permute-done.4.refs_2_), channel_id=1, source_target_pairs={{0,1},{1,0},{2,3},{3,2},{4,5},{5,4},{6,7},{7,6},{8,9},{9,8},{10,11... | collective-permute-start | bytes 786440 | tf_op jit(solution)/shard_map/ppermute | solution.py:485
  72.7 10.4 %collective-permute-start.8 = (bf16[1024,128]{1,0:T(8,128)(2,1)S(1)}, bf16[1024,128]{1,0:T(8,128)(2,1)S(1)}, u32[]{:S(2)}, u32[]{:S(2)}) collective-permute-start(bf16[1024,128]{1,0:T(8,128)(2,1)S(1)} %collective-permute-done.3.refs_3_), channel_id=1, source_target_pairs={{0,1},{1,0},{2,3},{3,2},{4,5},{5,4},{6,7},{7,6},{8,9},{9,8},{10,11... | collective-permute-start | bytes 786440 | tf_op jit(solution)/shard_map/ppermute | solution.py:485
  86.5 4.9 %collective-permute-start.10 = (bf16[128,2048]{1,0:T(8,128)(2,1)S(1)}, bf16[128,2048]{1,0:T(8,128)(2,1)S(1)}, u32[]{:S(2)}, u32[]{:S(2)}) collective-permute-start(bf16[128,2048]{1,0:T(8,128)(2,1)S(1)} %copy-done.10), channel_id=1, source_target_pairs={{0,1},{1,0},{2,3},{3,2},{4,5},{5,4},{6,7},{7,6},{8,9},{9,8},{10,11... | collective-permute-start | bytes 1572872 | tf_op jit(solution)/shard_map/ppermute | solution.py:485
  89.6 3.8 %collective-permute-start.11 = (bf16[128,2048]{1,0:T(8,128)(2,1)S(1)}, bf16[128,2048]{1,0:T(8,128)(2,1)S(1)}, u32[]{:S(2)}, u32[]{:S(2)}) collective-permute-start(bf16[128,2048]{1,0:T(8,128)(2,1)S(1)} %copy-done.9), channel_id=1, source_target_pairs={{0,1},{1,0},{2,3},{3,2},{4,5},{5,4},{6,7},{7,6},{8,9},{9,8},{10,11... | collective-permute-start | bytes 1572872 | tf_op jit(solution)/shard_map/ppermute | solution.py:485
  89.7 18.4 %collective-permute-start.12 = (bf16[128,2048]{1,0:T(8,128)(2,1)}, bf16[128,2048]{1,0:T(8,128)(2,1)S(1)}, u32[]{:S(2)}, u32[]{:S(2)}) collective-permute-start(bf16[128,2048]{1,0:T(8,128)(2,1)} %get-tuple-element.122), channel_id=1, source_target_pairs={{0,1},{1,0},{2,3},{3,2},{4,5},{5,4},{6,7},{7,6},{8,9},{9,8},{10,11... | collective-permute-start | bytes 1572872 | tf_op jit(solution)/shard_map/ppermute | solution.py:485
  90.1 18.0 %collective-permute-start.9 = (bf16[128,2048]{1,0:T(8,128)(2,1)}, bf16[128,2048]{1,0:T(8,128)(2,1)}, u32[]{:S(2)}, u32[]{:S(2)}) collective-permute-start(bf16[128,2048]{1,0:T(8,128)(2,1)} %get-tuple-element.119), channel_id=1, source_target_pairs={{0,1},{1,0},{2,3},{3,2},{4,5},{5,4},{6,7},{7,6},{8,9},{9,8},{10,11... | collective-permute-start | bytes 1572872 | tf_op jit(solution)/shard_map/ppermute | solution.py:485
  90.2 23.6 %collective-permute-start.13 = (bf16[2,128,512]{2,1,0:T(8,128)(2,1)}, bf16[2,128,512]{2,1,0:T(8,128)(2,1)}, u32[]{:S(2)}, u32[]{:S(2)}) collective-permute-start(bf16[2,128,512]{2,1,0:T(8,128)(2,1)} %get-tuple-element.125), channel_id=1, source_target_pairs={{2,0},{3,1},{4,2},{5,3},{6,4},{7,5},{10,8},{11,9},{12,10},{13,11},... | collective-permute-start | bytes 786440 | tf_op jit(solution)/shard_map/ppermute | solution.py:494
  91.5 16.6 %copy-start.5 = (bf16[128,2048]{1,0:T(8,128)(2,1)}, bf16[128,2048]{1,0:T(8,128)(2,1)S(1)}, u32[]{:S(2)}) copy-start(bf16[128,2048]{1,0:T(8,128)(2,1)S(1)} %collective-permute-done.10.o_b) | copy-start | bytes 1572868
  91.5 22.3 %collective-permute-start.14 = (bf16[2,128,512]{2,1,0:T(8,128)(2,1)}, bf16[2,128,512]{2,1,0:T(8,128)(2,1)S(1)}, u32[]{:S(2)}, u32[]{:S(2)}) collective-permute-start(bf16[2,128,512]{2,1,0:T(8,128)(2,1)} %get-tuple-element.126), channel_id=1, source_target_pairs={{4,0},{5,1},{6,2},{7,3},{12,8},{13,9},{14,10},{15,11},{20,16},{21,... | collective-permute-start | bytes 786440 | tf_op jit(solution)/shard_map/ppermute | solution.py:494
  93.4 14.7 %copy-start.6 = (bf16[128,2048]{1,0:T(8,128)(2,1)}, bf16[128,2048]{1,0:T(8,128)(2,1)S(1)}, u32[]{:S(2)}) copy-start(bf16[128,2048]{1,0:T(8,128)(2,1)S(1)} %collective-permute-done.11.dq_a) | copy-start | bytes 1572868
  93.4 21.1 %collective-permute-start.15 = (bf16[2,128,512]{2,1,0:T(8,128)(2,1)}, bf16[2,128,512]{2,1,0:T(8,128)(2,1)}, u32[]{:S(2)}, u32[]{:S(2)}) collective-permute-start(bf16[2,128,512]{2,1,0:T(8,128)(2,1)} %get-tuple-element.127), channel_id=1, source_target_pairs={{6,0},{7,1},{14,8},{15,9},{22,16},{23,17},{30,24},{31,25},{38,32},... | collective-permute-start | bytes 786440 | tf_op jit(solution)/shard_map/ppermute | solution.py:494
  94.7 29.3 %all-to-all-start.4 = ((bf16[32,32,512]{2,1,0:T(8,128)(2,1)}), bf16[32,32,512]{2,1,0:T(8,128)(2,1)S(1)}, u32[]{:S(2)}, u32[]{:S(2)}) async-start(bf16[32,32,512]{2,1,0:T(8,128)(2,1)} %bitcast.10), calls=%async_computation.4 | async-start | bytes 2097152 | tf_op jit(solution)/shard_map/all_to_all | solution.py:522
  115.8 1.6 %collective-permute-start.16 = (bf16[2,128,512]{2,1,0:T(8,128)(2,1)S(1)}, bf16[2,128,512]{2,1,0:T(8,128)(2,1)S(1)}, u32[]{:S(2)}, u32[]{:S(2)}) collective-permute-start(bf16[2,128,512]{2,1,0:T(8,128)(2,1)S(1)} %fusion.4), channel_id=1, source_target_pairs={{0,1},{1,0},{2,3},{3,2},{4,5},{5,4},{6,7},{7,6},{8,9},{9,8},{10,11... | collective-permute-start | bytes 786440 | tf_op jit(solution)/shard_map/ppermute | solution.py:485
  (10 other events, 56.3 us)
